TPU v7x, 32 devices: a whole 2x2x4 slice. The times are simulated.
32 devices in a mesh: dp: 8 (over z, y), seq: 4 (over x, core).
Axes of the slice: x: 2, y: 2, z: 4, core: 2. Of those that a mesh axis runs over, the one named last changes fastest.
Arguments:
- layer_input: bfloat16 [8, 1536, 1024], P('dp', 'seq'), may hold values from -6 to 6
- skip_input: bfloat16 [8, 1536, 1024], P('dp', 'seq'), may hold values from -6 to 6
- time_embed: bfloat16 [8, 1536, 1024], P('dp', 'seq'), may hold values from -6 to 6
- segment_ids: int32 [8, 1536], P('dp', 'seq'), may hold values from 0 to 2, as said below
- positions: int32 [8, 1536], P('dp', 'seq'), may hold values from 0 to 1535, as said below
- valid_mask: int32 [8, 1536], P('dp', 'seq'), may hold values from 0 to 1, as said below
- skip_weight: bfloat16 [2048, 1024], P(('dp', 'seq')), may hold values from -0.125 to 0.125
- time_weight: bfloat16 [1024, 5120], P(('dp', 'seq')), may hold values from -0.1875 to 0.1875
- query_weight: bfloat16 [1024, 1024], P(('dp', 'seq')), may hold values from -0.1875 to 0.1875
- key_weight: bfloat16 [1024, 1024], P(('dp', 'seq')), may hold values from -0.1875 to 0.1875
- value_weight: bfloat16 [1024, 1024], P(('dp', 'seq')), may hold values from -0.1875 to 0.1875
- out_weight: bfloat16 [1024, 1024], P(('dp', 'seq')), may hold values from -4 to 4
- up_weight: bfloat16 [1024, 4096], P(('dp', 'seq')), may hold values from -0.1875 to 0.1875
- down_weight: bfloat16 [4096, 1024], P(('dp', 'seq')), may hold values from -0.09375 to 0.09375
- cotangent: bfloat16 [8, 1536, 1024], P('dp', 'seq'), may hold values from -6 to 6
Outputs:
- output: bfloat16 [8, 1536, 1024], P('dp', 'seq')
- input_grad: float32 [8, 1536, 1024], P('dp', 'seq')
- skip_grad: float32 [8, 1536, 1024], P('dp', 'seq')
- time_grad: float32 [8, 1536, 1024], P('dp', 'seq')
- skip_weight_grad: float32 [2048, 1024], P(('dp', 'seq'))
- time_weight_grad: float32 [1024, 5120], P(('dp', 'seq'))
- query_weight_grad: float32 [1024, 1024], P(('dp', 'seq'))
- key_weight_grad: float32 [1024, 1024], P(('dp', 'seq'))
- value_weight_grad: float32 [1024, 1024], P(('dp', 'seq'))
- out_weight_grad: float32 [1024, 1024], P(('dp', 'seq'))
- up_weight_grad: float32 [1024, 4096], P(('dp', 'seq'))
- down_weight_grad: float32 [4096, 1024], P(('dp', 'seq'))
Inputs may be any that keep to these rules, and one draw needn't show every extreme that they name: In each row, segment_ids is 0 before a cut among frames 1 to 191, 2 from a second cut onward and 1 between; the second cut lies after 3 * 384 frames, so utterance 1 spans all four shards of its row; padding frames carry 2. positions of real frames count frames from the first frame of their utterance; padding frames carry their index in the row, so the last frame of every row has 1535. valid_mask is 1 except on a tail of 1 to 191 frames of each row, which lies inside utterance 2 and leaves it at least one real frame.
All inputs are finite; a program needn't handle non-finite values.
Results may differ from a plain program's by a relative error of at most 0.02.
Values may be sent and summed in bfloat16 or wider, within the bound.
No kernel may reach another device: no remote copies, remote signals or barrier semaphores. Data moves between devices by JAX's collectives and lax.ppermute only.
A program may use at most 320 MiB of HBM per device.

v0:
```python
import jax
import jax.numpy as jnp
from jax import lax
from jax.sharding import PartitionSpec as P

HD = 64


norm_eps = 1e-06
gelu_coef = 0.7978845608028654


def silu_value(v):
    return v * jax.nn.sigmoid(v)


def silu_slope(v):
    sig = jax.nn.sigmoid(v)
    return sig * (1.0 + v * (1.0 - sig))


def gelu_value(u):
    return 0.5 * u * (1.0 + jnp.tanh(gelu_coef * (u + 0.044715 * u * u * u)))


def gelu_slope(u):
    inner = jnp.tanh(gelu_coef * (u + 0.044715 * u * u * u))
    return 0.5 * (1.0 + inner) + 0.5 * u * (1.0 - inner * inner) * gelu_coef * (
        1.0 + 3.0 * 0.044715 * u * u
    )


def norm_rows(v):
    mean = jnp.mean(v, axis=-1, keepdims=True)
    centred = v - mean
    inverse = lax.rsqrt(jnp.mean(centred * centred, axis=-1, keepdims=True) + norm_eps)
    return (centred * inverse, inverse)


def norm_back(grad, normed, inverse):
    return inverse * (
        grad
        - jnp.mean(grad, axis=-1, keepdims=True)
        - normed * jnp.mean(grad * normed, axis=-1, keepdims=True)
    )


def angle_tables(where, half):
    freq = 10000.0 ** (-jnp.arange(half, dtype=jnp.float32) / half)
    angle = where.astype(jnp.float32)[..., None] * freq
    return (jnp.cos(angle)[..., None, :], jnp.sin(angle)[..., None, :])


def rotate(v, cosine, sine):
    half = v.shape[-1] // 2
    first = v[..., :half]
    second = v[..., half:]
    return jnp.concatenate(
        [first * cosine - second * sine, second * cosine + first * sine], axis=-1
    )


def unrotate(grad, cosine, sine):
    half = grad.shape[-1] // 2
    first = grad[..., :half]
    second = grad[..., half:]
    return jnp.concatenate(
        [first * cosine + second * sine, second * cosine - first * sine], axis=-1
    )


def masked_scores(query_block, seg_block, keys, seg_keys, valid_keys, scale):
    scores = (
        jnp.einsum("qhd,khd->hqk", query_block, keys, preferred_element_type=jnp.float32) * scale
    )
    allowed = (seg_block[:, None] == seg_keys[None, :]) & (valid_keys[None, :] > 0)
    return jnp.where(allowed[None], scores, -1e30)


def attend_row(query, keys, values, seg_keys, valid_keys, block, scale):
    length, heads, size = query.shape
    count = length // block

    def one_block(args):
        query_block, seg_block = args
        scores = masked_scores(query_block, seg_block, keys, seg_keys, valid_keys, scale)
        top = jnp.max(scores, axis=-1, keepdims=True)
        expo = jnp.exp(scores - top)
        total = jnp.sum(expo, axis=-1, keepdims=True)
        probs = (expo / total).astype(jnp.bfloat16)
        result = jnp.einsum("hqk,khd->qhd", probs, values, preferred_element_type=jnp.float32)
        return (result.astype(jnp.bfloat16), (top + jnp.log(total))[..., 0])

    results, logsum = lax.map(
        one_block, (query.reshape(count, block, heads, size), seg_keys.reshape(count, block))
    )
    return (results.reshape(length, heads, size), logsum)


def attend_back(query, keys, values, seg_keys, valid_keys, logsum, grad_out, block, scale):
    length, heads, size = query.shape
    count = length // block

    def one_block(carry, args):
        key_grad, value_grad = carry
        query_block, seg_block, logsum_block, grad_block = args
        scores = masked_scores(query_block, seg_block, keys, seg_keys, valid_keys, scale)
        probs = jnp.exp(scores - logsum_block[..., None])
        probs_grad = jnp.einsum(
            "qhd,khd->hqk", grad_block, values, preferred_element_type=jnp.float32
        )
        delta = jnp.sum(probs * probs_grad, axis=-1, keepdims=True)
        score_grad = (probs * (probs_grad - delta)).astype(jnp.bfloat16)
        query_grad = (
            jnp.einsum("hqk,khd->qhd", score_grad, keys, preferred_element_type=jnp.float32) * scale
        )
        key_grad = (
            key_grad
            + jnp.einsum(
                "hqk,qhd->khd", score_grad, query_block, preferred_element_type=jnp.float32
            )
            * scale
        )
        value_grad = value_grad + jnp.einsum(
            "hqk,qhd->khd",
            probs.astype(jnp.bfloat16),
            grad_block,
            preferred_element_type=jnp.float32,
        )
        return ((key_grad, value_grad), query_grad)

    empty = jnp.zeros((length, heads, size), jnp.float32)
    (key_grad, value_grad), query_grad = lax.scan(
        one_block,
        (empty, empty),
        (
            query.reshape(count, block, heads, size),
            seg_keys.reshape(count, block),
            logsum,
            grad_out.reshape(count, block, heads, size),
        ),
    )
    return (query_grad.reshape(length, heads, size), key_grad, value_grad)


def stack_rows(grad, groups, parts):
    return grad.reshape(groups, parts, grad.shape[0] // (groups * parts), grad.shape[1])


def on_device(
    layer_input,
    skip_input,
    time_embed,
    segment_ids,
    positions,
    valid_mask,
    skip_weight,
    time_weight,
    query_weight,
    key_weight,
    value_weight,
    out_weight,
    up_weight,
    down_weight,
    cotangent,
):
    rows, frames, width = layer_input.shape
    tokens = rows * frames
    parts = lax.axis_size("seq")
    skip_full, time_full, query_full, key_full, value_full, out_full, up_full, down_full = (
        lax.all_gather(skip_weight, ("dp", "seq"), axis=0, tiled=True),
        lax.all_gather(time_weight, ("dp", "seq"), axis=0, tiled=True),
        lax.all_gather(query_weight, ("dp", "seq"), axis=0, tiled=True),
        lax.all_gather(key_weight, ("dp", "seq"), axis=0, tiled=True),
        lax.all_gather(value_weight, ("dp", "seq"), axis=0, tiled=True),
        lax.all_gather(out_weight, ("dp", "seq"), axis=0, tiled=True),
        lax.all_gather(up_weight, ("dp", "seq"), axis=0, tiled=True),
        lax.all_gather(down_weight, ("dp", "seq"), axis=0, tiled=True),
    )
    triple_full = jnp.concatenate([query_full, key_full, value_full], axis=1)
    seg_row, pos_row, valid_row = (
        lax.all_gather(segment_ids, "seq", axis=1, tiled=True),
        lax.all_gather(positions, "seq", axis=1, tiled=True),
        lax.all_gather(valid_mask, "seq", axis=1, tiled=True),
    )
    length = seg_row.shape[1]
    local_width = width // parts
    heads = local_width // HD
    block = min(512, length)
    scale = HD ** (-0.5)
    head_shape = (rows, length, heads, HD)
    cosine, sine = angle_tables(pos_row, HD // 2)
    joined = jnp.concatenate([layer_input, skip_input], axis=2).reshape(tokens, 2 * width)
    base = jnp.dot(joined, skip_full, preferred_element_type=jnp.float32)
    time_value = time_embed.reshape(tokens, width).astype(jnp.float32)
    time_act = silu_value(time_value).astype(jnp.bfloat16)
    modul = jnp.dot(time_act, time_full, preferred_element_type=jnp.float32)
    shift_a, scale_a, shift_b, scale_b, gate_b = jnp.split(modul, 5, axis=1)
    normed_a, inverse_a = norm_rows(base)
    hidden_a = (normed_a * (1.0 + scale_a) + shift_a).astype(jnp.bfloat16)
    triple = (
        jnp.dot(hidden_a, triple_full, preferred_element_type=jnp.float32)
        .astype(jnp.bfloat16)
        .reshape(rows, frames, 3 * width)
    )
    query, keys, values = jnp.split(triple, 3, axis=2)
    query_heads, key_heads, value_heads = (
        lax.all_to_all(query, "seq", split_axis=2, concat_axis=1, tiled=True),
        lax.all_to_all(keys, "seq", split_axis=2, concat_axis=1, tiled=True),
        lax.all_to_all(values, "seq", split_axis=2, concat_axis=1, tiled=True),
    )
    query_rot = rotate(query_heads.reshape(head_shape).astype(jnp.float32), cosine, sine).astype(
        jnp.bfloat16
    )
    key_rot = rotate(key_heads.reshape(head_shape).astype(jnp.float32), cosine, sine).astype(
        jnp.bfloat16
    )
    value_rows = value_heads.reshape(head_shape)

    def forward_row(args):
        query_one, key_one, value_one, seg_one, valid_one = args
        return attend_row(query_one, key_one, value_one, seg_one, valid_one, block, scale)

    attended_heads, logsum = lax.map(
        forward_row, (query_rot, key_rot, value_rows, seg_row, valid_row)
    )
    attended = lax.all_to_all(
        attended_heads.reshape(rows, length, local_width),
        "seq",
        split_axis=1,
        concat_axis=2,
        tiled=True,
    )
    attended_flat = attended.reshape(tokens, width)
    middle = base + jnp.dot(attended_flat, out_full, preferred_element_type=jnp.float32)
    normed_b, inverse_b = norm_rows(middle)
    hidden_b = (normed_b * (1.0 + scale_b) + shift_b).astype(jnp.bfloat16)
    upper = jnp.dot(hidden_b, up_full, preferred_element_type=jnp.float32)
    acted = gelu_value(upper).astype(jnp.bfloat16)
    ffn = jnp.dot(acted, down_full, preferred_element_type=jnp.float32)
    output = (middle + gate_b * ffn).astype(jnp.bfloat16).reshape(rows, frames, width)
    upstream = cotangent.reshape(tokens, width).astype(jnp.float32)
    gate_b_grad = upstream * ffn
    ffn_grad = (upstream * gate_b).astype(jnp.bfloat16)
    grad_down = jnp.einsum("tf,td->fd", acted, ffn_grad, preferred_element_type=jnp.float32)
    acted_grad = jnp.einsum("td,fd->tf", ffn_grad, down_full, preferred_element_type=jnp.float32)
    upper_grad = (acted_grad * gelu_slope(upper)).astype(jnp.bfloat16)
    grad_up = jnp.einsum("tc,tf->cf", hidden_b, upper_grad, preferred_element_type=jnp.float32)
    hidden_b_grad = jnp.einsum("tf,cf->tc", upper_grad, up_full, preferred_element_type=jnp.float32)
    scale_b_grad = hidden_b_grad * normed_b
    middle_grad = upstream + norm_back(hidden_b_grad * (1.0 + scale_b), normed_b, inverse_b)
    branch_grad = middle_grad.astype(jnp.bfloat16)
    grad_out = jnp.einsum(
        "tc,td->cd", attended_flat, branch_grad, preferred_element_type=jnp.float32
    )
    attended_grad = jnp.einsum(
        "td,cd->tc", branch_grad, out_full, preferred_element_type=jnp.float32
    ).astype(jnp.bfloat16)
    attended_grad_heads = lax.all_to_all(
        attended_grad.reshape(rows, frames, width), "seq", split_axis=2, concat_axis=1, tiled=True
    )

    def backward_row(args):
        query_one, key_one, value_one, seg_one, valid_one, logsum_one, grad_one = args
        return attend_back(
            query_one, key_one, value_one, seg_one, valid_one, logsum_one, grad_one, block, scale
        )

    query_rot_grad, key_rot_grad, value_grad = lax.map(
        backward_row,
        (
            query_rot,
            key_rot,
            value_rows,
            seg_row,
            valid_row,
            logsum,
            attended_grad_heads.reshape(head_shape),
        ),
    )
    query_grad = (
        unrotate(query_rot_grad, cosine, sine)
        .astype(jnp.bfloat16)
        .reshape(rows, length, local_width)
    )
    key_grad = (
        unrotate(key_rot_grad, cosine, sine).astype(jnp.bfloat16).reshape(rows, length, local_width)
    )
    value_back = value_grad.astype(jnp.bfloat16).reshape(rows, length, local_width)
    query_back, key_back, value_frames = (
        lax.all_to_all(query_grad, "seq", split_axis=1, concat_axis=2, tiled=True),
        lax.all_to_all(key_grad, "seq", split_axis=1, concat_axis=2, tiled=True),
        lax.all_to_all(value_back, "seq", split_axis=1, concat_axis=2, tiled=True),
    )
    triple_grad = jnp.concatenate([query_back, key_back, value_frames], axis=2).reshape(
        tokens, 3 * width
    )
    grad_triple = jnp.einsum("tc,tk->ck", hidden_a, triple_grad, preferred_element_type=jnp.float32)
    grad_query, grad_key, grad_value = jnp.split(grad_triple, 3, axis=1)
    hidden_a_grad = jnp.einsum(
        "tk,ck->tc", triple_grad, triple_full, preferred_element_type=jnp.float32
    )
    scale_a_grad = hidden_a_grad * normed_a
    base_grad = (
        middle_grad + norm_back(hidden_a_grad * (1.0 + scale_a), normed_a, inverse_a)
    ).astype(jnp.bfloat16)
    grad_skip = jnp.einsum("tj,td->jd", joined, base_grad, preferred_element_type=jnp.float32)
    joined_grad = jnp.einsum("td,jd->tj", base_grad, skip_full, preferred_element_type=jnp.float32)
    input_grad = joined_grad[:, :width].reshape(rows, frames, width)
    skip_grad = joined_grad[:, width:].reshape(rows, frames, width)
    modul_grad = jnp.concatenate(
        [hidden_a_grad, scale_a_grad, hidden_b_grad, scale_b_grad, gate_b_grad], axis=1
    ).astype(jnp.bfloat16)
    grad_time = jnp.einsum("tc,tm->cm", time_act, modul_grad, preferred_element_type=jnp.float32)
    time_act_grad = jnp.einsum(
        "tm,cm->tc", modul_grad, time_full, preferred_element_type=jnp.float32
    )
    time_grad = (time_act_grad * silu_slope(time_value)).reshape(rows, frames, width)
    groups = lax.axis_size("dp")
    first = (
        lax.psum_scatter(
            stack_rows(grad_skip, groups, parts).astype(jnp.bfloat16),
            "dp",
            scatter_dimension=0,
            tiled=True,
        ).astype(jnp.float32),
        lax.psum_scatter(
            stack_rows(grad_time, groups, parts).astype(jnp.bfloat16),
            "dp",
            scatter_dimension=0,
            tiled=True,
        ).astype(jnp.float32),
        lax.psum_scatter(
            stack_rows(grad_query, groups, parts).astype(jnp.bfloat16),
            "dp",
            scatter_dimension=0,
            tiled=True,
        ).astype(jnp.float32),
        lax.psum_scatter(
            stack_rows(grad_key, groups, parts).astype(jnp.bfloat16),
            "dp",
            scatter_dimension=0,
            tiled=True,
        ).astype(jnp.float32),
        lax.psum_scatter(
            stack_rows(grad_value, groups, parts).astype(jnp.bfloat16),
            "dp",
            scatter_dimension=0,
            tiled=True,
        ).astype(jnp.float32),
        lax.psum_scatter(
            stack_rows(grad_out, groups, parts).astype(jnp.bfloat16),
            "dp",
            scatter_dimension=0,
            tiled=True,
        ).astype(jnp.float32),
        lax.psum_scatter(
            stack_rows(grad_up, groups, parts).astype(jnp.bfloat16),
            "dp",
            scatter_dimension=0,
            tiled=True,
        ).astype(jnp.float32),
        lax.psum_scatter(
            stack_rows(grad_down, groups, parts).astype(jnp.bfloat16),
            "dp",
            scatter_dimension=0,
            tiled=True,
        ).astype(jnp.float32),
    )
    second = (
        lax.psum_scatter(
            first[0].astype(jnp.bfloat16), "seq", scatter_dimension=1, tiled=True
        ).astype(jnp.float32),
        lax.psum_scatter(
            first[1].astype(jnp.bfloat16), "seq", scatter_dimension=1, tiled=True
        ).astype(jnp.float32),
        lax.psum_scatter(
            first[2].astype(jnp.bfloat16), "seq", scatter_dimension=1, tiled=True
        ).astype(jnp.float32),
        lax.psum_scatter(
            first[3].astype(jnp.bfloat16), "seq", scatter_dimension=1, tiled=True
        ).astype(jnp.float32),
        lax.psum_scatter(
            first[4].astype(jnp.bfloat16), "seq", scatter_dimension=1, tiled=True
        ).astype(jnp.float32),
        lax.psum_scatter(
            first[5].astype(jnp.bfloat16), "seq", scatter_dimension=1, tiled=True
        ).astype(jnp.float32),
        lax.psum_scatter(
            first[6].astype(jnp.bfloat16), "seq", scatter_dimension=1, tiled=True
        ).astype(jnp.float32),
        lax.psum_scatter(
            first[7].astype(jnp.bfloat16), "seq", scatter_dimension=1, tiled=True
        ).astype(jnp.float32),
    )
    summed = tuple((piece.reshape(piece.shape[2], piece.shape[3]) for piece in second))
    return (
        output,
        input_grad,
        skip_grad,
        time_grad,
        summed[0],
        summed[1],
        summed[2],
        summed[3],
        summed[4],
        summed[5],
        summed[6],
        summed[7],
    )


def solution(mesh):
    in_specs = (
        P("dp", "seq", None),
        P("dp", "seq", None),
        P("dp", "seq", None),
        P("dp", "seq"),
        P("dp", "seq"),
        P("dp", "seq"),
        P(("dp", "seq"), None),
        P(("dp", "seq"), None),
        P(("dp", "seq"), None),
        P(("dp", "seq"), None),
        P(("dp", "seq"), None),
        P(("dp", "seq"), None),
        P(("dp", "seq"), None),
        P(("dp", "seq"), None),
        P("dp", "seq", None),
    )
    out_specs = (
        P("dp", "seq", None),
        P("dp", "seq", None),
        P("dp", "seq", None),
        P("dp", "seq", None),
        P(("dp", "seq"), None),
        P(("dp", "seq"), None),
        P(("dp", "seq"), None),
        P(("dp", "seq"), None),
        P(("dp", "seq"), None),
        P(("dp", "seq"), None),
        P(("dp", "seq"), None),
        P(("dp", "seq"), None),
    )
    return jax.shard_map(
        on_device, mesh=mesh, in_specs=in_specs, out_specs=out_specs, check_vma=False
    )
```

profile of v0, /device:TPU:0, one launch (start us, length us, event | category | flops | bytes accessed | tf_op | source)
XLA Modules:
  0.0 1795.7 jit_solution(6513423913120023633)
XLA Ops:
  13.2 56.8 %all-gather.13.cloned.1.call-done = bf16[1024,1024]{1,0:T(8,128)(2,1)} async-done(((bf16[32,1024]{1,0:T(8,128)(2,1)}), bf16[1024,1024]{1,0:T(8,128)(2,1)}) %all-gather.13.cloned.1.call-update) | async-done | bytes 2097168 | tf_op jit(solution)/shard_map/all_gather | solution.py:173
  73.1 55.0 %all-gather.15.cloned.1.call-done = bf16[1024,1024]{1,0:T(8,128)(2,1)} async-done(((bf16[32,1024]{1,0:T(8,128)(2,1)}), bf16[1024,1024]{1,0:T(8,128)(2,1)}) %all-gather.15.cloned.1.call-update) | async-done | bytes 2097168 | tf_op jit(solution)/shard_map/all_gather | solution.py:174
  131.3 54.9 %all-gather.17.cloned.1.call-done = bf16[1024,1024]{1,0:T(8,128)(2,1)} async-done(((bf16[32,1024]{1,0:T(8,128)(2,1)}), bf16[1024,1024]{1,0:T(8,128)(2,1)}) %all-gather.17.cloned.1.call-update) | async-done | bytes 2097168 | tf_op jit(solution)/shard_map/all_gather | solution.py:175
  189.3 60.5 %all-gather.9.cloned.1.call-done = bf16[2048,1024]{1,0:T(8,128)(2,1)} async-done(((bf16[64,1024]{1,0:T(8,128)(2,1)}), bf16[2048,1024]{1,0:T(8,128)(2,1)}) %all-gather.9.cloned.1.call-update) | async-done | bytes 4194320 | tf_op jit(solution)/shard_map/all_gather | solution.py:171
  254.3 83.6 %all-gather.11.cloned.1.call-done = bf16[1024,5120]{1,0:T(8,128)(2,1)} async-done(((bf16[32,5120]{1,0:T(8,128)(2,1)}), bf16[1024,5120]{1,0:T(8,128)(2,1)}) %all-gather.11.cloned.1.call-update) | async-done | bytes 10485776 | tf_op jit(solution)/shard_map/all_gather | solution.py:172
  337.9 7.2 fusion.78
  345.5 8.2 fusion.44
  357.7 5.4 reduce.7
  364.1 4.8 all-to-all-start.2
  371.1 5.4 reduce.5
  380.6 4.2 all-to-all-start.1
  387.8 5.4 reduce.6
  400.1 14.4 all_gather.34
  414.5 5.2 all_gather.35
  420.3 5.3 all_gather.40
  448.5 37.0 %while.47 = (s32[]{:T(128)}, bf16[3,512,4,64]{1,3,2,0:T(8,128)(2,1)S(1)}, f32[3,4,512]{2,1,0:T(4,128)S(1)}, s32[3,512]{1,0:T(4,128)S(1)}, s32[1536]{0:T(1024)S(1...) while((s32[]{:T(128)}, ...), condition=%wide.region_5.6_spmd, body=%wide.region_2.5_spmd.sunk | while | flops 844758528 | bytes 43078780 | solution.py:94
  456.3 4.6 fusion.142
  468.6 4.6 fusion.142
  480.8 4.6 fusion.142
  487.6 6.6 reshape.557
  494.2 9.1 reduce.8
  504.3 17.4 all_to_all.117
  535.4 9.7 fusion.87
  545.1 12.3 all-gather.23.cloned.1.call-done
  557.5 12.0 fusion.42
  569.5 6.3 fusion.80
  575.9 7.9 fusion.82
  591.1 5.0 copy.139
  596.1 7.3 reduce.9
  613.7 7.6 all-to-all-done.4
  631.9 102.2 %while.48 = (s32[]{:T(128)}, f32[1536,4,64]{0,2,1:T(8,128)}, f32[1536,4,64]{0,2,1:T(8,128)}, f32[3,512,4,64]{1,0,3,2:T(4,128)}, bf16[3,512,4,64]{1,3,2,0:T(8,128...) while((s32[]{:T(128)}, f32[1536,4,64]{0,2,1:T(8,128)}, ...), condition=%wide.region_12.13_spmd.clone, body=%wide.region_10.12_spmd.clone.sunk | while | flops 2045246976 | bytes 139785472 | solution.py:133
  635.6 5.5 multiply_reduce_fusion.6
  654.1 11.1 dynamic_update_slice.33
  668.9 5.5 multiply_reduce_fusion.6
  688.6 11.1 dynamic_update_slice.33
  703.4 5.5 multiply_reduce_fusion.6
  723.0 11.1 dynamic_update_slice.33
  741.0 8.5 reduce.12
  755.3 8.1 reduce.11
  771.1 8.1 reduce.10
  791.0 5.6 all-to-all-done.7
  798.5 5.1 convolution_convert_fusion.3
  809.6 7.2 fusion.81
  819.7 4.4 convolution_convert_fusion.5
  824.4 12.0 convolution_convert_fusion.1
  836.5 10.1 convolution_convert_fusion.2
  858.5 8.1 convolution_convert_fusion
  867.3 5.9 reduce-scatter.25.cloned.1.call-done
  873.2 70.0 %reduce-scatter.33.cloned.1.call-done = bf16[1,4,32,1024]{3,2,1,0:T(8,128)(2,1)} async-done(((bf16[8,4,32,1024]{3,2,1,0:T(8,128)(2,1)}), bf16[1,4,32,1024]{3,2,1,0:T(8,128)(2,1)}) %reduce-scatter.33.cloned.1.call-update) | async-done | bytes 262160 | tf_op jit(solution)/shard_map/reduce_scatter | solution.py:345
  943.2 70.1 %reduce-scatter.29.cloned.1.call-done = bf16[1,4,32,1024]{3,2,1,0:T(8,128)(2,1)} async-done(((bf16[8,4,32,1024]{3,2,1,0:T(8,128)(2,1)}), bf16[1,4,32,1024]{3,2,1,0:T(8,128)(2,1)}) %reduce-scatter.29.cloned.1.call-update) | async-done | bytes 262160 | tf_op jit(solution)/shard_map/reduce_scatter | solution.py:339
  1013.4 90.6 %reduce-scatter.17.cloned.1.call-done = bf16[1,4,64,1024]{3,2,1,0:T(8,128)(2,1)} async-done(((bf16[8,4,64,1024]{3,2,1,0:T(8,128)(2,1)}), bf16[1,4,64,1024]{3,2,1,0:T(8,128)(2,1)}) %reduce-scatter.17.cloned.1.call-update) | async-done | bytes 524304 | tf_op jit(solution)/shard_map/reduce_scatter | solution.py:321
  1104.1 152.6 %reduce-scatter.45.cloned.1.call-done = bf16[1,4,128,1024]{3,2,1,0:T(8,128)(2,1)} async-done(((bf16[8,4,128,1024]{3,2,1,0:T(8,128)(2,1)}), bf16[1,4,128,1024]{3,2,1,0:T(8,128)(2,1)}) %reduce-scatter.45.cloned.1.call-update) | async-done | bytes 1048592 | tf_op jit(solution)/shard_map/reduce_scatter | solution.py:363
  1256.8 151.4 %reduce-scatter.41.cloned.1.call-done = bf16[1,4,32,4096]{3,2,1,0:T(8,128)(2,1)} async-done(((bf16[8,4,32,4096]{3,2,1,0:T(8,128)(2,1)}), bf16[1,4,32,4096]{3,2,1,0:T(8,128)(2,1)}) %reduce-scatter.41.cloned.1.call-update) | async-done | bytes 1048592 | tf_op jit(solution)/shard_map/reduce_scatter | solution.py:357
  1408.3 4.4 fusion.88
  1412.7 9.9 fusion.52
  1422.6 166.5 %reduce-scatter.21.cloned.1.call-done = bf16[1,4,32,5120]{3,2,1,0:T(8,128)(2,1)} async-done(((bf16[8,4,32,5120]{3,2,1,0:T(8,128)(2,1)}), bf16[1,4,32,5120]{3,2,1,0:T(8,128)(2,1)}) %reduce-scatter.21.cloned.1.call-update) | async-done | bytes 1310736 | tf_op jit(solution)/shard_map/reduce_scatter | solution.py:327
  1591.1 19.7 %reduce-scatter.39.cloned.1.call-done = bf16[1,1,32,1024]{3,2,1,0:T(8,128)(2,1)} async-done(((bf16[1,4,32,1024]{3,2,1,0:T(8,128)(2,1)}), bf16[1,1,32,1024]{3,2,1,0:T(8,128)(2,1)}) %reduce-scatter.39.cloned.1.call-update) | async-done | bytes 65552 | tf_op jit(solution)/shard_map/reduce_scatter | solution.py:386
  1612.3 20.9 %reduce-scatter.27.cloned.1.call-done = bf16[1,1,32,1024]{3,2,1,0:T(8,128)(2,1)} async-done(((bf16[1,4,32,1024]{3,2,1,0:T(8,128)(2,1)}), bf16[1,1,32,1024]{3,2,1,0:T(8,128)(2,1)}) %reduce-scatter.27.cloned.1.call-update) | async-done | bytes 65552 | tf_op jit(solution)/shard_map/reduce_scatter | solution.py:377
  1634.6 21.2 %reduce-scatter.35.cloned.1.call-done = bf16[1,1,32,1024]{3,2,1,0:T(8,128)(2,1)} async-done(((bf16[1,4,32,1024]{3,2,1,0:T(8,128)(2,1)}), bf16[1,1,32,1024]{3,2,1,0:T(8,128)(2,1)}) %reduce-scatter.35.cloned.1.call-update) | async-done | bytes 65552 | tf_op jit(solution)/shard_map/reduce_scatter | solution.py:383
  1657.3 20.8 %reduce-scatter.31.cloned.1.call-done = bf16[1,1,32,1024]{3,2,1,0:T(8,128)(2,1)} async-done(((bf16[1,4,32,1024]{3,2,1,0:T(8,128)(2,1)}), bf16[1,1,32,1024]{3,2,1,0:T(8,128)(2,1)}) %reduce-scatter.31.cloned.1.call-update) | async-done | bytes 65552 | tf_op jit(solution)/shard_map/reduce_scatter | solution.py:380
  1679.7 22.9 %reduce-scatter.19.cloned.1.call-done = bf16[1,1,64,1024]{3,2,1,0:T(8,128)(2,1)} async-done(((bf16[1,4,64,1024]{3,2,1,0:T(8,128)(2,1)}), bf16[1,1,64,1024]{3,2,1,0:T(8,128)(2,1)}) %reduce-scatter.19.cloned.1.call-update) | async-done | bytes 131088 | tf_op jit(solution)/shard_map/reduce_scatter | solution.py:371
  1704.1 25.8 %reduce-scatter.47.cloned.1.call-done = bf16[1,1,128,1024]{3,2,1,0:T(8,128)(2,1)} async-done(((bf16[1,4,128,1024]{3,2,1,0:T(8,128)(2,1)}), bf16[1,1,128,1024]{3,2,1,0:T(8,128)(2,1)}) %reduce-scatter.47.cloned.1.call-update) | async-done | bytes 262160 | tf_op jit(solution)/shard_map/reduce_scatter | solution.py:392
  1731.8 25.8 %reduce-scatter.43.cloned.1.call-done = bf16[1,1,32,4096]{3,2,1,0:T(8,128)(2,1)} async-done(((bf16[1,4,32,4096]{3,2,1,0:T(8,128)(2,1)}), bf16[1,1,32,4096]{3,2,1,0:T(8,128)(2,1)}) %reduce-scatter.43.cloned.1.call-update) | async-done | bytes 262160 | tf_op jit(solution)/shard_map/reduce_scatter | solution.py:389
  1759.3 27.2 %reduce-scatter.23.cloned.1.call-done = bf16[1,1,32,5120]{3,2,1,0:T(8,128)(2,1)} async-done(((bf16[1,4,32,5120]{3,2,1,0:T(8,128)(2,1)}), bf16[1,1,32,5120]{3,2,1,0:T(8,128)(2,1)}) %reduce-scatter.23.cloned.1.call-update) | async-done | bytes 327696 | tf_op jit(solution)/shard_map/reduce_scatter | solution.py:374
  (339 shorter events, 255.1 us)
Async XLA Ops:
  7.2 5.9 copy-start.33
  7.2 62.8 %all-gather.13.cloned.1.call-start = ((), (), s32[]{:S(2)}) async-start(), calls=%async_computation.26 | async-start | bytes 2162688 | tf_op jit(solution)/shard_map/all_gather | solution.py:173
  7.9 120.2 %all-gather.15.cloned.1.call-start = ((), (), s32[]{:S(2)}) async-start(), calls=%async_computation.27 | async-start | bytes 2162688 | tf_op jit(solution)/shard_map/all_gather | solution.py:174
  8.7 177.6 %all-gather.17.cloned.1.call-start = ((), (), s32[]{:S(2)}) async-start(), calls=%async_computation.28 | async-start | bytes 2162688 | tf_op jit(solution)/shard_map/all_gather | solution.py:175
  9.4 240.5 %all-gather.9.cloned.1.call-start = ((), (), s32[]{:S(2)}) async-start(), calls=%async_computation.24 | async-start | bytes 4325376 | tf_op jit(solution)/shard_map/all_gather | solution.py:171
  10.0 327.9 %all-gather.11.cloned.1.call-start = ((), (), s32[]{:S(2)}) async-start(), calls=%async_computation.25 | async-start | bytes 10813440 | tf_op jit(solution)/shard_map/all_gather | solution.py:172
  10.6 517.1 %all-gather.19.cloned.1.call-start = ((), (), s32[]{:S(2)}) async-start(), calls=%async_computation.29 | async-start | bytes 2162688 | tf_op jit(solution)/shard_map/all_gather | solution.py:176
  11.1 524.3 %all-gather.21.cloned.1.call-start = ((), (), s32[]{:S(2)}) async-start(), calls=%async_computation.30 | async-start | bytes 8650752 | tf_op jit(solution)/shard_map/all_gather | solution.py:177
  13.2 236.7 %copy-start.17 = (bf16[1,384,2048]{2,1,0:T(8,128)(2,1)}, bf16[1,384,2048]{2,1,0:T(8,128)(2,1)S(1)}, u32[]{:S(2)}) copy-start(bf16[1,384,2048]{2,1,0:T(8,128)(2,1)S(1)} %constant_dynamic-update-slice_fusion) | copy-start | bytes 4718596
  253.9 91.2 %copy-start.7 = (f32[384,1024]{1,0:T(8,128)}, f32[384,1024]{1,0:T(8,128)S(1)}, u32[]{:S(2)}) copy-start(f32[384,1024]{1,0:T(8,128)S(1)} %get-tuple-element.426) | copy-start | bytes 4718596
  253.9 91.1 %copy-start.45 = (f32[384]{0:T(512)}, f32[384]{0:T(512)S(1)}, u32[]{:S(2)}) copy-start(f32[384]{0:T(512)S(1)} %broadcast_multiply_fusion.5) | copy-start | bytes 4612
  254.3 90.8 %copy-start.49 = (f32[384]{0:T(512)}, f32[384]{0:T(512)S(1)}, u32[]{:S(2)}) copy-start(f32[384]{0:T(512)S(1)} %add_rsqrt_fusion.1) | copy-start | bytes 4612
  345.1 8.7 copy-start.9
  345.5 8.3 copy-start.31
  364.1 4.8 copy-start.21
  364.1 16.5 all-to-all-start.2
  380.6 15.9 all-to-all-start.1
  384.8 172.6 %all-gather.23.cloned.1.call-start = ((), (), s32[]{:S(2)}) async-start(), calls=%async_computation.31 | async-start | bytes 8650752 | tf_op jit(solution)/shard_map/all_gather | solution.py:178
  393.2 6.9 copy-start.51
  393.2 21.3 %copy-start.52 = (s32[1,384]{1,0:T(1,128)S(1)}, s32[1,384]{1,0:T(1,128)}, u32[]{:S(2)}) copy-start(s32[1,384]{1,0:T(1,128)} %param.24) | copy-start | bytes 4612
  393.2 27.1 %copy-start.53 = (s32[1,384]{1,0:T(1,128)S(1)}, s32[1,384]{1,0:T(1,128)}, u32[]{:S(2)}) copy-start(s32[1,384]{1,0:T(1,128)} %param.23) | copy-start | bytes 4612
  396.5 40.9 %all-to-all-start = ((bf16[4,2,49152]{2,1,0:T(2,128)(2,1)}), bf16[4,2,49152]{2,1,0:T(2,128)(2,1)S(1)}, u32[]{:S(2)}, u32[]{:S(2)}) async-start(bf16[4,2,49152]{2,1,0:T(2,128)(2,1)} %reshape.562), calls=%async_computation | async-start | bytes 1572864 | tf_op jit(solution)/shard_map/all_to_all | solution.py:208
  426.4 16.9 copy-start.23
  426.4 16.9 copy-start.25
  531.1 52.7 %copy-start.43 = (f32[384]{0:T(512)}, f32[384]{0:T(512)S(1)}, u32[]{:S(2)}) copy-start(f32[384]{0:T(512)S(1)} %broadcast_multiply_fusion.4) | copy-start | bytes 4612
  532.2 51.6 %copy-start.47 = (f32[384]{0:T(512)}, f32[384]{0:T(512)S(1)}, u32[]{:S(2)}) copy-start(f32[384]{0:T(512)S(1)} %add_rsqrt_fusion) | copy-start | bytes 4612
  557.4 12.1 copy-start.5
  557.5 12.1 copy-start.54
  569.5 6.3 copy-start.55
  575.8 8.0 copy-start.10
  575.8 8.0 copy-start.19
  583.8 4.2 copy-start.14
  583.8 5.3 copy-start.22
  605.4 15.9 all-to-all-start.4
  609.5 257.2 %reduce-scatter.37.cloned.1.call-start = ((), (), s32[]{:S(2)}) async-start(), calls=%async_computation.42 | async-start | bytes 2359296 | tf_op jit(solution)/shard_map/reduce_scatter | solution.py:351
  653.6 11.7 copy-start.2
  678.0 4.0 copy-start
  688.0 11.6 copy-start.2
  712.4 4.0 copy-start
  722.4 11.6 copy-start.2
  749.5 4.5 copy-start.28
  750.5 15.1 all-to-all-start.5
  763.4 6.4 copy-start.3
  765.6 15.9 all-to-all-start.6
  781.5 15.1 all-to-all-start.7
  785.0 88.1 %reduce-scatter.25.cloned.1.call-start = ((), (), s32[]{:S(2)}) async-start(), calls=%async_computation.36 | async-start | bytes 2359296 | tf_op jit(solution)/shard_map/reduce_scatter | solution.py:333
  797.9 5.8 copy-start.35
  806.5 136.6 %reduce-scatter.33.cloned.1.call-start = ((), (), s32[]{:S(2)}) async-start(), calls=%async_computation.40 | async-start | bytes 2359296 | tf_op jit(solution)/shard_map/reduce_scatter | solution.py:345
  807.2 206.1 %reduce-scatter.29.cloned.1.call-start = ((), (), s32[]{:S(2)}) async-start(), calls=%async_computation.38 | async-start | bytes 2359296 | tf_op jit(solution)/shard_map/reduce_scatter | solution.py:339
  807.9 296.2 %reduce-scatter.17.cloned.1.call-start = ((), (), s32[]{:S(2)}) async-start(), calls=%async_computation.32 | async-start | bytes 4718592 | tf_op jit(solution)/shard_map/reduce_scatter | solution.py:321
  809.5 7.2 copy-start.13
  824.2 432.5 %reduce-scatter.45.cloned.1.call-start = ((), (), s32[]{:S(2)}) async-start(), calls=%async_computation.46 | async-start | bytes 9437184 | tf_op jit(solution)/shard_map/reduce_scatter | solution.py:363
  836.5 571.8 %reduce-scatter.41.cloned.1.call-start = ((), (), s32[]{:S(2)}) async-start(), calls=%async_computation.44 | async-start | bytes 9437184 | tf_op jit(solution)/shard_map/reduce_scatter | solution.py:357
  846.7 742.5 %reduce-scatter.21.cloned.1.call-start = ((), (), s32[]{:S(2)}) async-start(), calls=%async_computation.34 | async-start | bytes 11796480 | tf_op jit(solution)/shard_map/reduce_scatter | solution.py:327
  866.6 744.2 %reduce-scatter.39.cloned.1.call-start = ((), (), s32[]{:S(2)}) async-start(), calls=%async_computation.43 | async-start | bytes 327680 | tf_op jit(solution)/shard_map/reduce_scatter | solution.py:386
  867.2 765.9 %reduce-scatter.27.cloned.1.call-start = ((), (), s32[]{:S(2)}) async-start(), calls=%async_computation.37 | async-start | bytes 327680 | tf_op jit(solution)/shard_map/reduce_scatter | solution.py:377
  873.1 782.7 %reduce-scatter.35.cloned.1.call-start = ((), (), s32[]{:S(2)}) async-start(), calls=%async_computation.41 | async-start | bytes 327680 | tf_op jit(solution)/shard_map/reduce_scatter | solution.py:383
  943.2 735.0 %reduce-scatter.31.cloned.1.call-start = ((), (), s32[]{:S(2)}) async-start(), calls=%async_computation.39 | async-start | bytes 327680 | tf_op jit(solution)/shard_map/reduce_scatter | solution.py:380
  1013.3 689.2 %reduce-scatter.19.cloned.1.call-start = ((), (), s32[]{:S(2)}) async-start(), calls=%async_computation.33 | async-start | bytes 655360 | tf_op jit(solution)/shard_map/reduce_scatter | solution.py:371
  1104.1 625.9 %reduce-scatter.47.cloned.1.call-start = ((), (), s32[]{:S(2)}) async-start(), calls=%async_computation.47 | async-start | bytes 1310720 | tf_op jit(solution)/shard_map/reduce_scatter | solution.py:392
  1256.7 500.8 %reduce-scatter.43.cloned.1.call-start = ((), (), s32[]{:S(2)}) async-start(), calls=%async_computation.45 | async-start | bytes 1310720 | tf_op jit(solution)/shard_map/reduce_scatter | solution.py:389
  1408.2 378.3 %reduce-scatter.23.cloned.1.call-start = ((), (), s32[]{:S(2)}) async-start(), calls=%async_computation.35 | async-start | bytes 1638400 | tf_op jit(solution)/shard_map/reduce_scatter | solution.py:374
  1408.3 4.4 copy-start.34
  1408.3 4.4 copy-start.40
  (29 other events, 49.0 us)
Sparse Core Ops, SparseCore 0:
  10.9 59.0 all-gather.12
  72.8 55.2 all-gather.14
  131.0 55.2 all-gather.16
  188.9 60.8 all-gather.8
  252.5 85.2 all-gather.10
  340.6 54.8 all-gather.18
  398.4 77.4 all-gather.20
  478.7 78.7 all-gather.22
  613.9 67.5 reduce-scatter.36
  806.6 66.4 reduce-scatter.24
  876.7 66.4 reduce-scatter.32
  946.5 66.7 reduce-scatter.28
  1016.9 87.0 reduce-scatter.16
  1107.9 148.7 reduce-scatter.44
  1260.2 147.9 reduce-scatter.40
  1412.1 177.0 reduce-scatter.20
  1591.6 19.1 reduce-scatter.38
  1613.1 20.0 reduce-scatter.26
  1635.7 20.0 reduce-scatter.34
  1658.1 19.9 reduce-scatter.30
  1680.8 21.6 reduce-scatter.18
  1705.0 24.8 reduce-scatter.46
  1732.7 24.8 reduce-scatter.42
  1760.0 26.5 reduce-scatter.22
where the time goes:
time: 1810 us; the launch traced here: 1800 us
  waiting for transfers between devices  1240 us (69%)
  matrix products  204 us (11%)
  local copies, waits for them, and re-layouts  145 us (8%)
  other arithmetic  116 us (6%)
  blocking collectives  42.2 us (2%)
  starting transfers between devices  29.3 us (2%)
    reduce_scatter x1, waiting for transfers between devices, on_device(): lax.psum_scatter(stack_rows(grad_time, groups, parts).astype(jnp.bfloat16...  167 us
    reduce_scatter x1, waiting for transfers between devices, on_device(): lax.psum_scatter(stack_rows(grad_down, groups, parts).astype(jnp.bfloat16...  153 us
    reduce_scatter x1, waiting for transfers between devices, on_device(): lax.psum_scatter(stack_rows(grad_up, groups, parts).astype(jnp.bfloat16),...  151 us
    reduce_scatter x1, waiting for transfers between devices, on_device(): lax.psum_scatter(stack_rows(grad_skip, groups, parts).astype(jnp.bfloat16...  90.6 us
    all_gather x1, waiting for transfers between devices, on_device(): lax.all_gather(time_weight, ('dp', 'seq'), axis=0, tiled=True)  83.6 us
    reduce_scatter x1, waiting for transfers between devices, on_device(): lax.psum_scatter(stack_rows(grad_key, groups, parts).astype(jnp.bfloat16)...  70.1 us
    reduce_scatter x1, waiting for transfers between devices, on_device(): lax.psum_scatter(stack_rows(grad_value, groups, parts).astype(jnp.bfloat1...  70 us
    all_gather x1, waiting for transfers between devices, on_device(): lax.all_gather(skip_weight, ('dp', 'seq'), axis=0, tiled=True)  60.5 us
  transfers between devices with their start and end apart: 31, of which 27 were waited for; matrix products, arithmetic and copies ran while one was open for 23% of the time, Pallas kernels for 0%

commit v1 on v0

v1 whole, which is shorter than its diff:
```python
import functools

import jax
import jax.numpy as jnp
from jax import lax
from jax.experimental import pallas as pl
from jax.experimental.pallas import tpu as pltpu
from jax.sharding import PartitionSpec as P

HD = 64
NEG = 1e30
norm_eps = 1e-06
gelu_coef = 0.7978845608028654
f32, bf16 = jnp.float32, jnp.bfloat16

RING = (0, 2, 4, 6, 7, 5, 3, 1)
PLACE = tuple(RING.index(d) for d in range(8))


def dot_nt(a, b):
    return lax.dot_general(a, b, (((1,), (1,)), ((), ())), preferred_element_type=f32)


def dot_nn(a, b):
    return lax.dot_general(a, b, (((1,), (0,)), ((), ())), preferred_element_type=f32)


def dot_tn(a, b):
    return lax.dot_general(a, b, (((0,), (0,)), ((), ())), preferred_element_type=f32)


def silu_slope(v):
    sig = jax.nn.sigmoid(v)
    return sig * (1.0 + v * (1.0 - sig))


def gelu_value(u):
    return 0.5 * u * (1.0 + jnp.tanh(gelu_coef * (u + 0.044715 * u * u * u)))


def gelu_slope(u):
    inner = jnp.tanh(gelu_coef * (u + 0.044715 * u * u * u))
    return 0.5 * (1.0 + inner) + 0.5 * u * (1.0 - inner * inner) * gelu_coef * (
        1.0 + 3.0 * 0.044715 * u * u
    )


def norm_rows(v):
    mean = jnp.mean(v, axis=-1, keepdims=True)
    centred = v - mean
    inverse = lax.rsqrt(jnp.mean(centred * centred, axis=-1, keepdims=True) + norm_eps)
    return (centred * inverse, inverse)


def norm_back(grad, normed, inverse):
    return inverse * (
        grad
        - jnp.mean(grad, axis=-1, keepdims=True)
        - normed * jnp.mean(grad * normed, axis=-1, keepdims=True)
    )

def lanes_of(shape):
    return lax.broadcasted_iota(jnp.int32, shape, 1)


def swap_halves(v):
    lane = lanes_of(v.shape)
    return jnp.where(lane % HD < HD // 2, pltpu.roll(v, 128 - HD // 2, 1), pltpu.roll(v, HD // 2, 1))


def three_parts(v):
    hi = v.astype(bf16)
    rest = v - hi.astype(f32)
    mid = rest.astype(bf16)
    low = (rest - mid.astype(f32)).astype(bf16)
    return hi, mid, low


def attend_kernel(pieces, block, scale, *refs):
    qkv = refs[:pieces]
    cos_ref, sin_ref, qext_ref, kext_ref = refs[pieces : pieces + 4]
    att_ref, lse_ref, qrot_ref, krot_ref = refs[pieces + 4 : pieces + 8]
    kx, vx = refs[pieces + 8 :]
    pair, step = pl.program_id(0), pl.program_id(1)
    frames = qkv[0].shape[0]
    per_piece = frames // block

    @pl.when(step == 0)
    def _():
        for j in range(pieces):
            rows = pl.ds(j * frames, frames)
            k = qkv[j][:, pl.ds(pl.multiple_of(256 + pair * 128, 128), 128)].astype(f32)
            k = (k * cos_ref[rows, :] + swap_halves(k) * sin_ref[rows, :]).astype(bf16)
            krot_ref[rows, :] = k
            v = qkv[j][:, pl.ds(pl.multiple_of(512 + pair * 128, 128), 128)]
            ext = kext_ref[rows, :]
            lane = lanes_of(k.shape)
            one = jnp.where(lane % HD == 0, 1.0, 0.0).astype(bf16)
            low_lane = lane < HD
            kx[0, rows, :] = jnp.where(low_lane, k, ext)
            kx[1, rows, :] = jnp.where(low_lane, ext, k)
            vx[0, rows, :] = jnp.where(low_lane, v, one)
            vx[1, rows, :] = jnp.where(low_lane, one, v)

    rows = pl.ds(pl.multiple_of(step * block, block), block)
    for j in range(pieces):

        @pl.when(step // per_piece == j)
        def _(j=j):
            sub = pl.ds(pl.multiple_of((step - j * per_piece) * block, block), block)
            q = qkv[j][sub, pl.ds(pl.multiple_of(pair * 128, 128), 128)].astype(f32)
            q = (q * cos_ref[rows, :] + swap_halves(q) * sin_ref[rows, :]).astype(bf16)
            qrot_ref[...] = (q.astype(f32) * scale).astype(bf16)

    q = qrot_ref[...]
    ext = qext_ref[rows, :]
    low_lane = lanes_of(q.shape) < HD
    outs = []
    for h in range(2):
        qx = jnp.where(low_lane, q, ext) if h == 0 else jnp.where(low_lane, ext, q)
        scores = dot_nt(qx, kx[h])
        top = jnp.max(scores, axis=1, keepdims=True)
        expo = jnp.exp(scores - top)
        mixed = dot_nn(expo.astype(bf16), vx[h])
        total = mixed[:, HD : HD + 1] if h == 0 else mixed[:, 0:1]
        outs.append((mixed / total, top + jnp.log(total)))
    low_out = lanes_of((block, 128)) < HD
    att_ref[...] = jnp.where(low_out, outs[0][0], outs[1][0]).astype(bf16)
    lse_ref[...] = jnp.where(low_out, outs[0][1], outs[1][1])


def attend(qkv, cosine, sine, qext, kext, block=384, scale=HD**-0.5):
    pieces = len(qkv)
    total = pieces * qkv[0].shape[0]
    whole = lambda p, i: (0, 0)
    full = lambda a: pl.BlockSpec(a.shape, whole)
    tile = pl.BlockSpec((block, 128), lambda p, i: (i, p))
    column = pl.BlockSpec((total, 128), lambda p, i: (0, p))
    return pl.pallas_call(
        functools.partial(attend_kernel, pieces, block, scale),
        grid=(2, total // block),
        in_specs=[full(a) for a in (*qkv, cosine, sine, qext, kext)],
        out_specs=[tile, tile, tile, column],
        out_shape=[
            jax.ShapeDtypeStruct((total, 256), bf16),
            jax.ShapeDtypeStruct((total, 256), f32),
            jax.ShapeDtypeStruct((total, 256), bf16),
            jax.ShapeDtypeStruct((total, 256), bf16),
        ],
        scratch_shapes=[pltpu.VMEM((2, total, 128), bf16), pltpu.VMEM((2, total, 128), bf16)],
        compiler_params=pltpu.CompilerParams(vmem_limit_bytes=48 * 2**20),
        cost_estimate=pl.CostEstimate(
            flops=4 * total * total * 512, bytes_accessed=total * 4096, transcendentals=4 * total * total
        ),
        name="attend",
    )(*qkv, cosine, sine, qext, kext)


def attend_back_kernel(pieces, block, scale, *refs):
    grads = refs[:pieces]
    values = refs[pieces : 2 * pieces]
    qrot_ref, krot_ref, att_ref, lse_ref, cos_ref, sin_ref, qext_ref, kext_ref = refs[2 * pieces : 2 * pieces + 8]
    out_ref = refs[2 * pieces + 8]
    qx, gx, qm, gm, dq = refs[2 * pieces + 9 :]
    pair, step = pl.program_id(0), pl.program_id(1)
    last = pl.num_programs(1) - 1
    frames = grads[0].shape[0]
    per_piece = frames // block

    @pl.when(step == 0)
    def _():
        for j in range(pieces):
            rows = pl.ds(j * frames, frames)
            q = qrot_ref[rows, :]
            g = grads[j][:, pl.ds(pl.multiple_of(pair * 128, 128), 128)]
            lane = lanes_of(q.shape)
            low_lane = lane < HD
            spot = lane % HD
            prod = g.astype(f32) * att_ref[rows, :].astype(f32)
            zero = jnp.zeros_like(q)
            lse = lse_ref[rows, :]
            for h in range(2):
                own = low_lane if h == 0 else jnp.logical_not(low_lane)
                lse_h = lse[:, 0:1] if h == 0 else lse[:, HD : HD + 1]
                delta = jnp.sum(jnp.where(own, prod, 0.0), axis=1, keepdims=True)
                a, b, c = (t.astype(f32) for t in three_parts(-lse_h))
                part = jnp.where(spot == 4, a, jnp.where(spot == 5, b, jnp.where(spot == 6, c, qext_ref[rows, :].astype(f32))))
                qx[h, rows, :] = jnp.where(own, q, part.astype(bf16))
                a, b, c = (t.astype(f32) for t in three_parts(-delta))
                part = jnp.where(spot == 0, a, jnp.where(spot == 1, b, jnp.where(spot == 2, c, 0.0)))
                gx[h, rows, :] = jnp.where(own, g, part.astype(bf16))
                qm[h, rows, :] = jnp.where(own, q, zero)
                gm[h, rows, :] = jnp.where(own, g, zero)
        dq[...] = jnp.zeros_like(dq)

    rows = pl.ds(pl.multiple_of(step * block, block), block)
    for j in range(pieces):

        @pl.when(step // per_piece == j)
        def _(j=j):
            sub = pl.ds(pl.multiple_of((step - j * per_piece) * block, block), block)
            k = krot_ref[rows, :]
            v = values[j][sub, pl.ds(pl.multiple_of(512 + pair * 128, 128), 128)]
            ext = kext_ref[rows, :]
            lane = lanes_of(k.shape)
            low_lane = lane < HD
            three = jnp.where(lane % HD < 3, 1.0, 0.0).astype(bf16)
            zero = jnp.zeros_like(k)
            small = k.astype(f32) * scale
            dk = jnp.zeros((block, 128), f32)
            dv = jnp.zeros((block, 128), f32)
            for h in range(2):
                own = low_lane if h == 0 else jnp.logical_not(low_lane)
                kx = jnp.where(own, k, ext)
                vx = jnp.where(own, v, three)
                probs = jnp.exp(dot_nt(kx, qx[h]))
                grad = (probs * dot_nt(vx, gx[h])).astype(bf16)
                dv = dv + dot_nn(probs.astype(bf16), gm[h])
                dk = dk + dot_nn(grad, qm[h])
                turned = jnp.transpose(jnp.where(own, small, 0.0)).astype(bf16)
                dq[...] += dot_nn(turned, grad)
            dk = dk * cos_ref[rows, :] - swap_halves(dk) * sin_ref[rows, :]
            out_ref[rows, pl.ds(pl.multiple_of(256 + pair * 128, 128), 128)] = dk.astype(bf16)
            out_ref[rows, pl.ds(pl.multiple_of(512 + pair * 128, 128), 128)] = dv.astype(bf16)

    @pl.when(step == last)
    def _():
        g = jnp.transpose(dq[...])
        g = g * cos_ref[...] - swap_halves(g) * sin_ref[...]
        out_ref[:, pl.ds(pl.multiple_of(pair * 128, 128), 128)] = g.astype(bf16)


def attend_back(grads, qkv, qrot, krot, att, lse, cosine, sine, qext, kext, block=384, scale=HD**-0.5):
    pieces = len(grads)
    total = pieces * grads[0].shape[0]
    whole = lambda p, i: (0, 0)
    full = lambda a: pl.BlockSpec(a.shape, whole)
    column = pl.BlockSpec((total, 128), lambda p, i: (0, p))
    return pl.pallas_call(
        functools.partial(attend_back_kernel, pieces, block, scale),
        grid=(2, total // block),
        in_specs=[full(a) for a in (*grads, *qkv)] + [column] * 4 + [full(a) for a in (cosine, sine, qext, kext)],
        out_specs=pl.BlockSpec((total, 768), whole),
        out_shape=jax.ShapeDtypeStruct((total, 768), bf16),
        scratch_shapes=[pltpu.VMEM((2, total, 128), bf16)] * 4 + [pltpu.VMEM((128, total), f32)],
        compiler_params=pltpu.CompilerParams(vmem_limit_bytes=56 * 2**20),
        cost_estimate=pl.CostEstimate(
            flops=10 * total * total * 512, bytes_accessed=total * 8192, transcendentals=4 * total * total
        ),
        name="attend_back",
    )(*grads, *qkv, qrot, krot, att, lse, cosine, sine, qext, kext)


def frame_tables(seg, pos, valid):
    half = HD // 2
    freq = 10000.0 ** (-jnp.arange(half, dtype=f32) / half)
    angle = pos.astype(f32)[:, None] * freq
    cosine, sine = jnp.cos(angle), jnp.sin(angle)
    cosine = jnp.concatenate([cosine] * 4, axis=1)
    sine = jnp.concatenate([-sine, sine, -sine, sine], axis=1)
    spot = jnp.arange(128)[None, :] % HD
    seg, valid = seg[:, None], valid[:, None] > 0
    qext = jnp.where((spot < 3) & (spot != seg) | (spot == 3), -NEG, 0.0).astype(bf16)
    kext = ((spot == seg) & (spot < 3) | (spot == 3) & ~valid | (spot >= 4) & (spot < 7)).astype(bf16)
    return cosine, sine, qext, kext


def swap(v, mask):
    return lax.ppermute(v, "seq", [(i, i ^ mask) for i in range(4)])


def spread(v):
    near = swap(v, 1)
    far = swap(v, 2)
    return [v, near, far, swap(far, 1)]


def collect(parts):
    low = [part.astype(bf16) for part in parts]
    far_near = swap(low[3], 1)
    near = swap(low[1], 1)
    far = swap((low[2].astype(f32) + far_near.astype(f32)).astype(bf16), 2)
    return parts[0] + near.astype(f32) + far.astype(f32)


def exchange(parts):
    return [parts[0], swap(parts[1], 1), swap(parts[2], 2), swap(parts[3], 3)]


def by_place(parts, me):
    odd, high = (me & 1) == 1, (me & 2) == 2
    parts = [jnp.where(odd, parts[t ^ 1], parts[t]) for t in range(4)]
    return [jnp.where(high, parts[t ^ 2], parts[t]) for t in range(4)]


def ring_step(v, step):
    return lax.ppermute(v, "dp", [(RING[i], RING[(i + step) % 8]) for i in range(8)])


def ring_gather(v, way):
    found = [None] * 8
    found[0] = one = other = v
    for k in range(1, 5):
        one = ring_step(one, way)
        found[(way * k) % 8] = one
        if k < 4:
            other = ring_step(other, -way)
            found[(-way * k) % 8] = other
    return found


def ring_scatter(v, place, way):
    order = jnp.asarray(RING, jnp.int32)

    def block(k):
        return lax.dynamic_index_in_dim(v, order[(place + way * k) % 8], 0, keepdims=False)

    one, other = block(4), block(-3)
    for k in range(3, -1, -1):
        one = ring_step(one, way)
        if k > 0:
            one = (one.astype(f32) + block(k).astype(f32)).astype(bf16)
    for k in range(2, -1, -1):
        other = ring_step(other, -way)
        if k > 0:
            other = (other.astype(f32) + block(-k).astype(f32)).astype(bf16)
    return block(0).astype(f32) + one.astype(f32) + other.astype(f32)


def after(v, *others):
    return lax.optimization_barrier((v, *others))[0]


def assemble_kernel(copies, n_in, n_out, index_ref, *refs):
    arrays, outs, sems = refs[:n_in], refs[n_in : n_in + n_out], refs[-1]
    moves = []
    me = index_ref[8]
    for number, (a, row, count, out, k, j, per_dp, per_seq, column) in enumerate(copies):
        start = index_ref[k] * per_dp + jnp.bitwise_xor(me, j) * per_seq
        target = outs[out].at[
            pl.ds(pl.multiple_of(start, count), count), pl.ds(column, arrays[a].shape[1])
        ]
        moves.append(
            pltpu.make_async_copy(arrays[a].at[pl.ds(row, count), :], target, sems.at[number])
        )
    for move in moves:
        move.start()
    for move in moves:
        move.wait()


def assemble(index, arrays, copies, shapes):
    anywhere = pl.BlockSpec(memory_space=pl.ANY)
    return pl.pallas_call(
        functools.partial(assemble_kernel, tuple(copies), len(arrays), len(shapes)),
        grid_spec=pltpu.PrefetchScalarGridSpec(
            num_scalar_prefetch=1,
            grid=(1,),
            in_specs=[anywhere] * len(arrays),
            out_specs=[anywhere] * len(shapes),
            scratch_shapes=[pltpu.SemaphoreType.DMA((len(copies),))],
        ),
        out_shape=[jax.ShapeDtypeStruct(shape, bf16) for shape in shapes],
        name="assemble",
    )(index, *arrays)


class Gather:
    def __init__(self, index):
        self.index, self.arrays, self.copies, self.shapes = index, [], [], []

    def out(self, rows, columns):
        self.shapes.append((rows, columns))
        return len(self.shapes) - 1

    def add(self, piece, k, blocks):
        self.arrays.append(piece)
        for row, count, out, j, per_dp, per_seq, column in blocks:
            self.copies.append(
                (len(self.arrays) - 1, row, count, out, k, j, per_dp, per_seq, column)
            )

    def run(self):
        return assemble(self.index, self.arrays, self.copies, self.shapes)


def scatter_full(grad, me, place, groups, way):
    rows, columns = grad.shape
    if groups != 8:
        low = grad.astype(bf16).reshape(groups * 4, rows // (groups * 4), columns)
        return lax.psum_scatter(low, ("dp", "seq"), scatter_dimension=0).astype(f32)
    low = grad.astype(bf16).reshape(groups, 2, 2, rows // (groups * 4), columns)
    odd, high = (me & 1) == 1, (me & 2) == 2
    keep = jnp.where(odd, low[:, :, 1], low[:, :, 0])
    send = jnp.where(odd, low[:, :, 0], low[:, :, 1])
    both = (keep.astype(f32) + swap(send, 1).astype(f32)).astype(bf16)
    mine = ring_scatter(both, place, way)
    keep = jnp.where(high, mine[1], mine[0])
    send = jnp.where(high, mine[0], mine[1]).astype(bf16)
    return keep + swap(send, 2).astype(f32)


def scatter_dp(grad, place, groups, way):
    low = grad.astype(bf16)
    if groups != 8:
        return lax.psum_scatter(low, "dp", scatter_dimension=0).astype(f32)
    return ring_scatter(low, place, way)


def to_rows(block, me):
    rows = block.shape[0] // 4
    low = block.astype(bf16)
    parts = by_place([low[t * rows : (t + 1) * rows] for t in range(4)], me)
    return by_place(exchange(parts), me)


def on_device(
    layer_input,
    skip_input,
    time_embed,
    segment_ids,
    positions,
    valid_mask,
    skip_weight,
    time_weight,
    query_weight,
    key_weight,
    value_weight,
    out_weight,
    up_weight,
    down_weight,
    cotangent,
):
    rows, frames, width = layer_input.shape
    hidden = up_weight.shape[1]
    groups = lax.axis_size("dp")
    me, dp = lax.axis_index("seq"), lax.axis_index("dp")
    local = width // 4
    local_hidden = hidden // 4

    triple = jnp.stack(
        [w.reshape(-1, 4, local) for w in (query_weight, key_weight, value_weight)], axis=2
    )
    triple = triple.reshape(-1, 4, 3 * local)
    upper_w = up_weight.reshape(-1, groups, 4, hidden // (groups * 4)).transpose(0, 2, 1, 3)
    upper_w = upper_w.reshape(-1, 4, local_hidden)
    qkv_parts = exchange(by_place([triple[:, t] for t in range(4)], me))
    up_parts = exchange(by_place([upper_w[:, t] for t in range(4)], me))

    time_a, time_b = time_weight[:, : 2 * width], time_weight[:, 2 * width :]
    if groups == 8:
        place = jnp.asarray(PLACE, jnp.int32)[dp]
        order = jnp.asarray(RING, jnp.int32)[(place - jnp.arange(8)) % 8]
        index = jnp.concatenate([order, me[None].astype(jnp.int32)])
        n_skip, n_time, n_out = skip_weight.shape[0], time_weight.shape[0], out_weight.shape[0]

        def full_piece(gather, piece, k, j, layout):
            near = swap(piece, 1)
            for array, jj in ((piece, j), (near, j ^ 1)):
                gather.add(
                    array,
                    k,
                    [(row, count, out, jj, 4 * count, count, column) for row, count, out, column in layout],
                )

        first = Gather(index)
        o_skip, o_time_a = first.out(32 * n_skip, width), first.out(32 * n_time, 2 * width)
        own = jnp.concatenate([skip_weight, time_a[:, :width], time_a[:, width:]], axis=0)
        layout = [
            (0, n_skip, o_skip, 0),
            (n_skip, n_time, o_time_a, 0),
            (n_skip + n_time, n_time, o_time_a, width),
        ]
        found_own, found_far = ring_gather(own, 1), ring_gather(swap(own, 2), -1)
        for k in range(8):
            full_piece(first, found_own[k], k, 0, layout)
            full_piece(first, found_far[k], k, 2, layout)
        skip_full, time_a_full = first.run()

        second = Gather(index)
        o_triple, o_out = second.out(width, 3 * local), second.out(width, width)
        triple_own = jnp.concatenate(qkv_parts, axis=0)
        out_own = jnp.concatenate([out_weight, swap(out_weight, 2)], axis=0)
        triple_own, out_own = after(
            (triple_own, out_own), found_own[4], found_far[4], found_own[5], found_far[3]
        )
        found_triple, found_out = ring_gather(triple_own, 1), ring_gather(out_own, -1)
        n_triple = query_weight.shape[0]
        for k in range(8):
            second.add(
                found_triple[k],
                k,
                [(j * n_triple, n_triple, o_triple, j, 4 * n_triple, n_triple, 0) for j in range(4)],
            )
            near = swap(found_out[k], 1)
            for array, flip in ((found_out[k], 0), (near, 1)):
                second.add(
                    array,
                    k,
                    [(jj * n_out, n_out, o_out, (2 * jj) ^ flip, 4 * n_out, n_out, 0) for jj in range(2)],
                )
        triple_full, out_full = second.run()

        third = Gather(index)
        o_up, o_down = third.out(width, local_hidden), third.out(local_hidden, width)
        o_time_b = third.out(32 * n_time, 3 * width)
        up_own = jnp.concatenate(up_parts, axis=0)
        down_own, time_own = down_weight, time_b
        up_own, down_own, time_own, time_far = after(
            (up_own, down_own, time_own, swap(time_b, 2)),
            found_triple[4],
            found_out[4],
            found_triple[5],
            found_out[3],
        )
        found_up, found_down = ring_gather(up_own, 1), ring_gather(down_own, -1)
        found_own, found_far = ring_gather(time_own, 1), ring_gather(time_far, -1)
        n_up, n_down = up_weight.shape[0], down_weight.shape[0]
        for k in range(8):
            third.add(
                found_up[k], k, [(j * n_up, n_up, o_up, j, 4 * n_up, n_up, 0) for j in range(4)]
            )
            third.add(found_down[k], k, [(0, n_down, o_down, 0, n_down, 0, 0)])
            full_piece(third, found_own[k], k, 0, [(0, n_time, o_time_b, 0)])
            full_piece(third, found_far[k], k, 2, [(0, n_time, o_time_b, 0)])
        up_full, down_full, time_b_full = third.run()
    else:
        place = dp
        skip_full, time_a_full, time_b_full, out_full = (
            lax.all_gather(w, ("dp", "seq"), axis=0, tiled=True)
            for w in (skip_weight, time_a, time_b, out_weight)
        )
        triple_full, up_full = (
            lax.all_gather(jnp.concatenate(by_place(parts, me), axis=0), "dp", axis=0, tiled=True)
            for parts in (qkv_parts, up_parts)
        )
        down_full = lax.all_gather(down_weight, "dp", axis=0, tiled=True)

    marks = jnp.concatenate(spread(jnp.concatenate([segment_ids, positions, valid_mask])), axis=1)
    cosine, sine, query_marks, key_marks = frame_tables(marks[0], marks[1], marks[2])
    first_in, second_in = layer_input.reshape(frames, width), skip_input.reshape(frames, width)
    joined = jnp.concatenate([first_in, second_in], axis=1)
    base = dot_nn(joined, skip_full)
    time_value = time_embed.reshape(frames, width).astype(f32)
    time_act = (time_value * jax.nn.sigmoid(time_value)).astype(bf16)
    shift_a, scale_a = jnp.split(dot_nn(time_act, time_a_full), 2, axis=1)
    normed_a, inverse_a = norm_rows(base)
    hidden_a = spread((normed_a * (1.0 + scale_a) + shift_a).astype(bf16))
    qkv = [dot_nn(h, triple_full).astype(bf16) for h in hidden_a]
    att, logsum, query_rot, key_rot = attend(qkv, cosine, sine, query_marks, key_marks)
    attended = jnp.concatenate(
        by_place(exchange([att[j * frames : (j + 1) * frames] for j in range(4)]), me), axis=1
    )

    shift_b, scale_b, gate_b = jnp.split(dot_nn(time_act, time_b_full), 3, axis=1)
    upstream = cotangent.reshape(frames, width).astype(f32)
    ffn_grad = spread((upstream * gate_b).astype(bf16))
    middle = base + dot_nn(attended, out_full)
    normed_b, inverse_b = norm_rows(middle)
    hidden_b = spread((normed_b * (1.0 + scale_b) + shift_b).astype(bf16))
    hb = [jnp.concatenate(hidden_b[:2]), jnp.concatenate(hidden_b[2:])]
    fg = [jnp.concatenate(ffn_grad[:2]), jnp.concatenate(ffn_grad[2:])]
    upper = [dot_nn(h, up_full) for h in hb]
    acted = [gelu_value(u).astype(bf16) for u in upper]
    ug = [(dot_nt(g, down_full) * gelu_slope(u)).astype(bf16) for g, u in zip(fg, upper)]
    back = [dot_nt(u, up_full) for u in ug]
    hidden_b_grad = collect(
        [back[0][:frames], back[0][frames:], back[1][:frames], back[1][frames:]]
    )
    part = [dot_nn(a, down_full) for a in acted]
    ffn = collect([part[0][:frames], part[0][frames:], part[1][:frames], part[1][frames:]])
    grad_down = dot_tn(acted[0], fg[0]) + dot_tn(acted[1], fg[1])
    grad_up = dot_tn(hb[0], ug[0]) + dot_tn(hb[1], ug[1])
    output = (middle + gate_b * ffn).astype(bf16).reshape(rows, frames, width)
    gate_b_grad = upstream * ffn

    scale_b_grad = hidden_b_grad * normed_b
    middle_grad = upstream + norm_back(hidden_b_grad * (1.0 + scale_b), normed_b, inverse_b)
    branch_grad = middle_grad.astype(bf16)
    attended_grad = dot_nt(branch_grad, out_full).astype(bf16)
    att_grad = exchange(
        by_place([attended_grad[:, t * local : (t + 1) * local] for t in range(4)], me)
    )
    grad_out = dot_tn(attended, branch_grad)
    modul_b_grad = jnp.concatenate([hidden_b_grad, scale_b_grad, gate_b_grad], axis=1).astype(bf16)
    grad_time_b = dot_tn(time_act, modul_b_grad)
    time_back_b = dot_nt(modul_b_grad, time_b_full)
    triple_grad = attend_back(
        att_grad, qkv, query_rot, key_rot, att, logsum, cosine, sine, query_marks, key_marks
    )
    back = dot_nt(triple_grad, triple_full)
    hidden_a_grad = collect([back[j * frames : (j + 1) * frames] for j in range(4)])
    grad_triple = dot_tn(jnp.concatenate(hidden_a), triple_grad)

    scale_a_grad = hidden_a_grad * normed_a
    base_grad = (
        middle_grad + norm_back(hidden_a_grad * (1.0 + scale_a), normed_a, inverse_a)
    ).astype(bf16)
    grad_skip = dot_tn(joined, base_grad)
    joined_grad = dot_nt(base_grad, skip_full)
    modul_a_grad = jnp.concatenate([hidden_a_grad, scale_a_grad], axis=1).astype(bf16)
    grad_time_a = dot_tn(time_act, modul_a_grad)
    time_back = dot_nt(modul_a_grad, time_a_full) + time_back_b
    time_grad = (time_back * silu_slope(time_value)).reshape(rows, frames, width)

    by_dp = lambda grad: grad.reshape(groups, grad.shape[0] // groups, grad.shape[1])
    down_sum = scatter_dp(by_dp(grad_down), place, groups, 1)
    up_sum = to_rows(scatter_dp(by_dp(grad_up), place, groups, -1), me)
    up_sum = jnp.stack(
        [u.reshape(-1, groups, hidden // (groups * 4)) for u in up_sum], axis=2
    ).reshape(-1, hidden)
    out_sum = scatter_full(grad_out, me, place, groups, 1)
    time_b_sum = scatter_full(grad_time_b, me, place, groups, -1)
    qkv_sum = to_rows(scatter_dp(by_dp(grad_triple), place, groups, 1), me)
    qkv_sum = [
        jnp.concatenate([q[:, i * local : (i + 1) * local] for q in qkv_sum], axis=1)
        for i in range(3)
    ]
    skip_sum = scatter_full(grad_skip, me, place, groups, 1)
    time_a_sum = scatter_full(grad_time_a, me, place, groups, -1)
    return (
        output,
        joined_grad[:, :width].reshape(rows, frames, width),
        joined_grad[:, width:].reshape(rows, frames, width),
        time_grad,
        skip_sum,
        jnp.concatenate([time_a_sum, time_b_sum], axis=1),
        qkv_sum[0].astype(f32),
        qkv_sum[1].astype(f32),
        qkv_sum[2].astype(f32),
        out_sum,
        up_sum.astype(f32),
        down_sum,
    )


def solution(mesh):
    frames = P("dp", "seq", None)
    marks = P("dp", "seq")
    weight = P(("dp", "seq"), None)
    return jax.shard_map(
        on_device,
        mesh=mesh,
        in_specs=(frames,) * 3 + (marks,) * 3 + (weight,) * 8 + (frames,),
        out_specs=(frames,) * 4 + (weight,) * 8,
        check_vma=False,
    )
```

time: 1810 us -> 1350 us (0.75)
  waiting for transfers between devices: 1240 us -> 249 us
  Pallas kernels: 0 us -> 749 us
  starting transfers between devices: 29.3 us -> 159 us
  local copies, waits for them, and re-layouts: 145 us -> 22.7 us
  matrix products: 204 us -> 84.9 us
  other arithmetic: 116 us -> 53 us
  blocking collectives: 42.2 us -> 0 us
    reduce_scatter x16 -> x0, waiting for transfers between devices: 891 us -> none  [the longest x1 167 us: on_device(): lax.psum_scatter(stack_rows(grad_time, groups, parts).astype(jnp.bfloat16...]
    pallas_call x0 -> x5, Pallas kernels: none -> 749 us  [the longest x3 690 us: assemble(): pl.pallas_call(functools.partial(assemble_kernel, tuple(copies), len(arra...]
    all_gather x8 -> x0, waiting for transfers between devices: 323 us -> none  [the longest x1 83.6 us: on_device(): lax.all_gather(time_weight, ('dp', 'seq'), axis=0, tiled=True)]
    ppermute x0 -> x195, waiting for transfers between devices: none -> 249 us  [the longest x105 185 us: ring_step(): lax.ppermute(v, 'dp', [(RING[i], RING[(i + step) % 8]) for i in range(8)])]
    ppermute x0 -> x195, starting transfers between devices: none -> 159 us  [the longest x105 124 us: ring_step(): lax.ppermute(v, 'dp', [(RING[i], RING[(i + step) % 8]) for i in range(8)])]
    dot_general x39 -> x30, matrix products: 204 us -> 84.9 us  [the longest x9 28.7 us: dot_nt(): lax.dot_general(a, b, (((1,), (1,)), ((), ())), preferred_element_type=f32)]
    unnamed x14 -> x3, other arithmetic: 58.2 us -> 0.01 us
    unnamed x133 -> x320, local copies, waits for them, and re-layouts: 47.9 us -> 9.73 us
  transfers between devices with their start and end apart: 31 -> 195, of which waited for: 27 -> 89; matrix products, arithmetic and copies ran while one was open for 23% -> 9% of each run, Pallas kernels for 0% -> 51%
where the time goes in v1:
time: 1350 us; the launch traced here: 1340 us
  Pallas kernels  749 us (55%)
  waiting for transfers between devices  249 us (18%)
  starting transfers between devices  159 us (12%)
  matrix products  84.9 us (6%)
  other arithmetic  53 us (4%)
  between operations  26.9 us (2%)
  local copies, waits for them, and re-layouts  22.7 us (2%)
    pallas_call x3, Pallas kernels, assemble(): pl.pallas_call(functools.partial(assemble_kernel, tuple(copies), len(arra...  690 us
    ppermute x105, waiting for transfers between devices, ring_step(): lax.ppermute(v, 'dp', [(RING[i], RING[(i + step) % 8]) for i in range(8)])  185 us
    ppermute x105, starting transfers between devices, ring_step(): lax.ppermute(v, 'dp', [(RING[i], RING[(i + step) % 8]) for i in range(8)])  124 us
    ppermute x90, waiting for transfers between devices, swap(): return lax.ppermute(v, 'seq', [(i, i ^ mask) for i in range(4)])  63.7 us
    ppermute x90, starting transfers between devices, swap(): return lax.ppermute(v, 'seq', [(i, i ^ mask) for i in range(4)])  35.7 us
    pallas_call x1, Pallas kernels, attend_back(): pl.pallas_call(functools.partial(attend_back_kernel, pieces, block, scale...  34.9 us
    dot_general x9, matrix products, dot_nt(): lax.dot_general(a, b, (((1,), (1,)), ((), ())), preferred_element_type=f32)  28.7 us
    dot_general x9, matrix products, dot_tn(): lax.dot_general(a, b, (((0,), (0,)), ((), ())), preferred_element_type=f32)  28.5 us
  transfers between devices with their start and end apart: 195, of which 89 were waited for; matrix products, arithmetic and copies ran while one was open for 9% of the time, Pallas kernels for 51%

profile of v1, /device:TPU:0, one launch (start us, length us, event | category | flops | bytes accessed | tf_op | source)
XLA Modules:
  0.0 1344.4 jit_solution(13423891249032670450)
XLA Ops:
  2.5 3.0 collective-permute-start.1
  20.6 3.1 collective-permute-done.3.refs_4_
  27.8 4.3 collective-permute-done.17.refs_30_
  39.6 4.4 collective-permute-done.18.refs_26_
  45.5 4.0 collective-permute-done.11.refs_12_
  54.9 3.6 collective-permute-done.19.refs_22_
  58.6 2.8 collective-permute-done.13.refs_14_
  73.3 256.8 %assemble.3 = (bf16[2048,1024]{1,0:T(8,128)(2,1)}, bf16[1024,2048]{1,0:T(8,128)(2,1)}) custom-call(s32[9]{0:T(128)} %pad_add_fusion.6.index_ref, bf16[128,1024]{1,0:T(8,128)(2,1)} %copy-done.24, bf16[128,1024]{1,0:T(8,128)(2,1)} %copy-done.36, bf16[128,1024]{1,0:T(8,128)(2,1)} %copy-done.33, bf16[128,1024]{1,0:T(8,128)(2,1)} %copy-done.41, ...), custom_call_target="tpu_custom_call" | custom-call | tf_op jit(solution)/shard_map/assemble/pallas_call | solution.py:354
  330.1 4.4 fusion.126
  345.2 2.9 collective-permute-done.46.refs_22_
  357.1 4.4 collective-permute-done.48.refs_16_
  364.9 12.5 collective-permute-start.45
  388.8 2.9 collective-permute-done.97.refs_46_
  403.5 3.8 collective-permute-done.72.refs_6_
  408.7 4.9 collective-permute-done.91.refs_43_
  418.0 2.8 fusion.98
  431.3 2.9 collective-permute-done.78.refs_12_
  436.3 4.0 collective-permute-done.103.refs_36_
  442.3 4.8 collective-permute-done.99.refs_34_
  453.1 113.5 %assemble.4 = (bf16[1024,768]{1,0:T(8,128)(2,1)}, bf16[1024,1024]{1,0:T(8,128)(2,1)}) custom-call(s32[9]{0:T(128)} %pad_add_fusion.6.index_ref, bf16[128,768]{1,0:T(8,128)(2,1)} %copy-done.29, bf16[64,1024]{1,0:T(8,128)(2,1)} %copy-done.31, bf16[64,1024]{1,0:T(8,128)(2,1)} %copy-done.102, bf16[128,768]{1,0:T(8,128)(2,1)} %collective-permute-done.36.refs_3_, ...), custom_call_target="tpu_custom_call" | custom-call | tf_op jit(solution)/shard_map/assemble/pallas_call | solution.py:354
  573.2 2.9 collective-permute-done.104.refs_30_
  587.2 5.0 collective-permute-done.90.refs_24_
  593.6 320.1 %assemble.5 = (bf16[1024,1024]{1,0:T(8,128)(2,1)}, bf16[1024,1024]{1,0:T(8,128)(2,1)}, bf16[1024,3072]{1,0:T(8,128)(2,1)}) custom-call(s32[9]{0:T(128)} %pad_add_fusion.6.index_ref, bf16[128,1024]{1,0:T(8,128)(2,1)} %copy-done.25, bf16[128,1024]{1,0:T(8,128)(2,1)} %refs_1_, bf16[32,3072]{1,0:T(8,128)(2,1)} %copy-done.30, ...), custom_call_target="tpu_custom_call" | custom-call | tf_op jit(solution)/shard_map/assemble/pallas_call | solution.py:354
  916.4 23.3 %attend.1 = (bf16[1536,256]{1,0:T(8,128)(2,1)S(1)}, f32[1536,256]{1,0:T(8,128)}, bf16[1536,256]{1,0:T(8,128)(2,1)S(1)}, bf16[1536,256]{1,0:T(8,128)(2,1)S(1)}) custom-call(bf16[384,768]{1,0:T(8,128)(2,1)S(1)} %convolution_convert_fusion.10.refs_0_.refs_4_, bf16[384,768]{1,0:T(8,128)(2,1)S(1)} %convolution_convert_fusion.9.refs_1_.refs_5_, ...), custom_call_target="tpu_custom_call" | custom-call | flops 4831838208 | bytes 6291456 | tf_op jit(solution)/shard_map/attend/pallas_call | solution.py:139
  947.0 4.1 collective-permute-done.64
  982.3 4.0 fusion.48
  986.4 4.8 fusion.11
  993.0 7.9 collective-permute-done.122
  1000.9 3.4 fusion.47
  1006.4 10.6 collective-permute-done.116
  1016.9 3.5 fusion.46
  1024.5 3.5 fusion.16
  1047.6 3.6 collective-permute-done.189
  1056.0 5.1 collective-permute-done.180
  1062.2 3.6 collective-permute-done.183
  1076.6 3.8 collective-permute-done.191
  1082.7 6.3 collective-permute-done.185
  1098.9 10.9 collective-permute-done.119
  1109.8 3.5 convert_add_fusion.3
  1113.3 4.5 convolution_convert_fusion
  1117.9 3.9 fusion.50
  1128.1 3.1 collective-permute-done.127.refs_2_
  1131.2 3.4 collective-permute-done.128.refs_3_
  1135.4 34.9 %attend_back.1 = bf16[1536,768]{1,0:T(8,128)(2,1)} custom-call(bf16[384,256]{1,0:T(8,128)(2,1)} %get-tuple-element.119.refs_0_, bf16[384,256]{1,0:T(8,128)(2,1)} %copy-done.147, bf16[384,256]{1,0:T(8,128)(2,1)} %copy-done.148, bf16[384,256]{1,0:T(8,128)(2,1)} %copy-done.149, bf16[384,768]{1,0:T(8,128)(2,1)} %copy-done.3, bf16[384,768]{1,0:T(8,128)(2,1)} %copy-done.5, ...), custom_call_target="tpu_custom_call" | custom-call | flops 12079595520 | bytes 12582912 | tf_op jit(solution)/shard_map/attend_back/pallas_call | solution.py:239
  1170.3 5.4 fusion.26
  1178.2 4.8 collective-permute-done.159
  1184.0 4.6 fusion.142
  1191.6 3.4 collective-permute-done.161
  1198.6 3.2 collective-permute-done.162
  1211.1 3.1 collective-permute-done.170
  1214.8 4.5 collective-permute-done.171
  1221.5 2.9 collective-permute-done.172
  1251.3 3.3 fusion.36
  1257.3 4.0 fusion.145
  1264.7 3.4 collective-permute-done.151
  1268.7 2.8 fusion.1
  1273.7 3.1 fusion.2
  1278.4 5.8 collective-permute-done.142
  1289.4 9.7 collective-permute-done.143
  1299.9 7.7 collective-permute-done.153
  1313.7 3.1 collective-permute-done.147
  1317.5 4.1 collective-permute-done.154
  1326.1 4.1 collective-permute-done.135
  1340.6 2.9 collective-permute-done.140
  (822 shorter events, 306.1 us)
Async XLA Ops:
  2.5 16.0 %collective-permute-start.1 = (bf16[128,1024]{1,0:T(8,128)(2,1)S(1)}, bf16[128,1024]{1,0:T(8,128)(2,1)S(1)}, u32[]{:S(2)}, u32[]{:S(2)}) collective-permute-start(bf16[128,1024]{1,0:T(8,128)(2,1)S(1)} %pad_maximum_fusion.19.refs_0_), channel_id=1, source_target_pairs={{0,2},{1,3},{2,0},{3,1},{4,6},{5,7},{6,4},{7,5},{8,10},{9,11},{10,... | collective-permute-start | bytes 786440 | tf_op jit(solution)/shard_map/ppermute | solution.py:269
  5.5 14.7 %collective-permute-start.34 = (bf16[32,1024]{1,0:T(8,128)(2,1)}, bf16[32,1024]{1,0:T(8,128)(2,1)S(1)}, u32[]{:S(2)}, u32[]{:S(2)}) collective-permute-start(bf16[32,1024]{1,0:T(8,128)(2,1)} %param.35), channel_id=1, source_target_pairs={{0,2},{1,3},{2,0},{3,1},{4,6},{5,7},{6,4},{7,5},{8,10},{9,11},{10,... | collective-permute-start | bytes 196616 | tf_op jit(solution)/shard_map/ppermute | solution.py:269
  18.5 13.6 %collective-permute-start.17 = (bf16[128,1024]{1,0:T(8,128)(2,1)S(1)}, bf16[128,1024]{1,0:T(8,128)(2,1)S(1)}, u32[]{:S(2)}, u32[]{:S(2)}) collective-permute-start(bf16[128,1024]{1,0:T(8,128)(2,1)S(1)} %collective-permute-done.1.refs_2_), channel_id=1, source_target_pairs={{0,4},{8,0},{16,8},{24,16},{28,24},{20,28},{12,20},{4,12},{1,5},{9... | collective-permute-start | bytes 786440 | tf_op jit(solution)/shard_map/ppermute | solution.py:297
  53.5 12.7 collective-permute-start.10
  53.6 13.1 collective-permute-start.28
  70.1 266.3 %collective-permute-start.60 = (s32[3,384]{1,0:T(4,128)}, s32[3,384]{1,0:T(4,128)}, u32[]{:S(2)}, u32[]{:S(2)}) collective-permute-start(s32[3,384]{1,0:T(4,128)} %pad_add_fusion.5), channel_id=1, source_target_pairs={{0,1},{1,0},{2,3},{3,2},{4,5},{5,4},{6,7},{7,6},{8,9},{9,8},{10,11... | collective-permute-start | bytes 13832 | tf_op jit(solution)/shard_map/ppermute | solution.py:269
  70.7 267.5 %collective-permute-start.66 = (bf16[32,1024]{1,0:T(8,128)(2,1)}, bf16[32,1024]{1,0:T(8,128)(2,1)S(1)}, u32[]{:S(2)}, u32[]{:S(2)}) collective-permute-start(bf16[32,1024]{1,0:T(8,128)(2,1)} %get-tuple-element.134), channel_id=1, source_target_pairs={{0,1},{1,0},{2,3},{3,2},{4,5},{5,4},{6,7},{7,6},{8,9},{9,8},{10,11... | collective-permute-start | bytes 196616 | tf_op jit(solution)/shard_map/ppermute | solution.py:269
  70.8 269.0 %collective-permute-start.67 = (bf16[32,1024]{1,0:T(8,128)(2,1)}, bf16[32,1024]{1,0:T(8,128)(2,1)}, u32[]{:S(2)}, u32[]{:S(2)}) collective-permute-start(bf16[32,1024]{1,0:T(8,128)(2,1)} %get-tuple-element.135), channel_id=1, source_target_pairs={{0,2},{1,3},{2,0},{3,1},{4,6},{5,7},{6,4},{7,5},{8,10},{9,11},{10,... | collective-permute-start | bytes 196616 | tf_op jit(solution)/shard_map/ppermute | solution.py:269
  71.3 266.3 %collective-permute-start.62 = (s32[3,384]{1,0:T(4,128)S(1)}, s32[3,384]{1,0:T(4,128)}, u32[]{:S(2)}, u32[]{:S(2)}) collective-permute-start(s32[3,384]{1,0:T(4,128)S(1)} %collective-permute-done.61), channel_id=1, source_target_pairs={{0,1},{1,0},{2,3},{3,2},{4,5},{5,4},{6,7},{7,6},{8,9},{9,8},{10,11... | collective-permute-start | bytes 13832 | tf_op jit(solution)/shard_map/ppermute | solution.py:269
  72.7 268.8 %collective-permute-start.36 = (bf16[128,768]{1,0:T(8,128)(2,1)S(1)}, bf16[128,768]{1,0:T(8,128)(2,1)}, u32[]{:S(2)}, u32[]{:S(2)}) collective-permute-start(bf16[128,768]{1,0:T(8,128)(2,1)S(1)} %pad_maximum_fusion.22.refs_0_), channel_id=1, source_target_pairs={{0,8},{8,16},{16,24},{24,28},{28,20},{20,12},{12,4},{4,0},{1,9},{9... | collective-permute-start | bytes 589832 | tf_op jit(solution)/shard_map/ppermute | solution.py:297
  338.2 13.2 collective-permute-start.51
  341.6 13.2 collective-permute-start.39
  355.9 22.0 %collective-permute-start.56 = (bf16[64,1024]{1,0:T(8,128)(2,1)S(1)}, bf16[64,1024]{1,0:T(8,128)(2,1)S(1)}, u32[]{:S(2)}, u32[]{:S(2)}) collective-permute-start(bf16[64,1024]{1,0:T(8,128)(2,1)S(1)} %collective-permute-done.46.refs_22_), channel_id=1, source_target_pairs={{0,1},{1,0},{2,3},{3,2},{4,5},{5,4},{6,7},{7,6},{8,9},{9,8},{10,11... | collective-permute-start | bytes 393224 | tf_op jit(solution)/shard_map/ppermute | solution.py:269
  355.9 23.8 %collective-permute-start.43 = (bf16[64,1024]{1,0:T(8,128)(2,1)S(1)}, bf16[64,1024]{1,0:T(8,128)(2,1)S(1)}, u32[]{:S(2)}, u32[]{:S(2)}) collective-permute-start(bf16[64,1024]{1,0:T(8,128)(2,1)S(1)} %collective-permute-done.40.refs_7_), channel_id=1, source_target_pairs={{0,8},{8,16},{16,24},{24,28},{28,20},{20,12},{12,4},{4,0},{1,9},{9... | collective-permute-start | bytes 393224 | tf_op jit(solution)/shard_map/ppermute | solution.py:297
  361.5 18.3 %collective-permute-start.49 = (bf16[64,1024]{1,0:T(8,128)(2,1)S(1)}, bf16[64,1024]{1,0:T(8,128)(2,1)S(1)}, u32[]{:S(2)}, u32[]{:S(2)}) collective-permute-start(bf16[64,1024]{1,0:T(8,128)(2,1)S(1)} %collective-permute-done.48.refs_16_), channel_id=1, source_target_pairs={{0,4},{8,0},{16,8},{24,16},{28,24},{20,28},{12,20},{4,12},{1,5},{9... | collective-permute-start | bytes 393224 | tf_op jit(solution)/shard_map/ppermute | solution.py:297
  363.1 17.2 %collective-permute-start.53 = (bf16[128,768]{1,0:T(8,128)(2,1)S(1)}, bf16[128,768]{1,0:T(8,128)(2,1)S(1)}, u32[]{:S(2)}, u32[]{:S(2)}) collective-permute-start(bf16[128,768]{1,0:T(8,128)(2,1)S(1)} %collective-permute-done.52.refs_18_), channel_id=1, source_target_pairs={{0,4},{8,0},{16,8},{24,16},{28,24},{20,28},{12,20},{4,12},{1,5},{9... | collective-permute-start | bytes 589832 | tf_op jit(solution)/shard_map/ppermute | solution.py:297
  364.9 18.1 %collective-permute-start.45 = (bf16[128,768]{1,0:T(8,128)(2,1)S(1)}, bf16[128,768]{1,0:T(8,128)(2,1)S(1)}, u32[]{:S(2)}, u32[]{:S(2)}) collective-permute-start(bf16[128,768]{1,0:T(8,128)(2,1)S(1)} %collective-permute-done.42.refs_9_), channel_id=1, source_target_pairs={{0,8},{8,16},{16,24},{24,28},{28,20},{20,12},{12,4},{4,0},{1,9},{9... | collective-permute-start | bytes 589832 | tf_op jit(solution)/shard_map/ppermute | solution.py:297
  377.9 23.5 %collective-permute-start.58 = (bf16[384,1024]{1,0:T(8,128)(2,1)S(1)}, bf16[384,1024]{1,0:T(8,128)(2,1)}, u32[]{:S(2)}, u32[]{:S(2)}) collective-permute-start(bf16[384,1024]{1,0:T(8,128)(2,1)S(1)} %fusion.43), channel_id=1, source_target_pairs={{0,2},{1,3},{2,0},{3,1},{4,6},{5,7},{6,4},{7,5},{8,10},{9,11},{10,... | collective-permute-start | bytes 2359304 | tf_op jit(solution)/shard_map/ppermute | solution.py:269
  379.8 22.4 %collective-permute-start.57 = (bf16[384,1024]{1,0:T(8,128)(2,1)S(1)}, bf16[384,1024]{1,0:T(8,128)(2,1)S(1)}, u32[]{:S(2)}, u32[]{:S(2)}) collective-permute-start(bf16[384,1024]{1,0:T(8,128)(2,1)S(1)} %fusion.43), channel_id=1, source_target_pairs={{0,1},{1,0},{2,3},{3,2},{4,5},{5,4},{6,7},{7,6},{8,9},{9,8},{10,11... | collective-permute-start | bytes 2359304 | tf_op jit(solution)/shard_map/ppermute | solution.py:269
  398.7 16.3 %collective-permute-start.102 = (bf16[128,1024]{1,0:T(8,128)(2,1)S(1)}, bf16[128,1024]{1,0:T(8,128)(2,1)S(1)}, u32[]{:S(2)}, u32[]{:S(2)}) collective-permute-start(bf16[128,1024]{1,0:T(8,128)(2,1)S(1)} %pad_maximum_fusion.21.refs_0_), channel_id=1, source_target_pairs={{0,4},{8,0},{16,8},{24,16},{28,24},{20,28},{12,20},{4,12},{1,5},{9... | collective-permute-start | bytes 786440 | tf_op jit(solution)/shard_map/ppermute | solution.py:297
  400.1 13.5 %collective-permute-start.91 = (bf16[128,1024]{1,0:T(8,128)(2,1)S(1)}, bf16[128,1024]{1,0:T(8,128)(2,1)S(1)}, u32[]{:S(2)}, u32[]{:S(2)}) collective-permute-start(bf16[128,1024]{1,0:T(8,128)(2,1)S(1)} %copy-done.51), channel_id=1, source_target_pairs={{0,4},{8,0},{16,8},{24,16},{28,24},{20,28},{12,20},{4,12},{1,5},{9... | collective-permute-start | bytes 786440 | tf_op jit(solution)/shard_map/ppermute | solution.py:297
  401.4 13.6 %collective-permute-start.73 = (bf16[128,1024]{1,0:T(8,128)(2,1)S(1)}, bf16[128,1024]{1,0:T(8,128)(2,1)S(1)}, u32[]{:S(2)}, u32[]{:S(2)}) collective-permute-start(bf16[128,1024]{1,0:T(8,128)(2,1)S(1)} %copy-done.51), channel_id=1, source_target_pairs={{0,8},{8,16},{16,24},{24,28},{28,20},{20,12},{12,4},{4,0},{1,9},{9... | collective-permute-start | bytes 786440 | tf_op jit(solution)/shard_map/ppermute | solution.py:297
  402.2 15.4 %collective-permute-start.98 = (bf16[32,3072]{1,0:T(8,128)(2,1)S(1)}, bf16[32,3072]{1,0:T(8,128)(2,1)}, u32[]{:S(2)}, u32[]{:S(2)}) collective-permute-start(bf16[32,3072]{1,0:T(8,128)(2,1)S(1)} %collective-permute-done.97.refs_46_), channel_id=1, source_target_pairs={{0,4},{8,0},{16,8},{24,16},{28,24},{20,28},{12,20},{4,12},{1,5},{9... | collective-permute-start | bytes 589832 | tf_op jit(solution)/shard_map/ppermute | solution.py:297
  427.1 13.2 collective-permute-start.103
  430.3 17.4 %collective-permute-start.107 = (bf16[32,3072]{1,0:T(8,128)(2,1)S(1)}, bf16[32,3072]{1,0:T(8,128)(2,1)S(1)}, u32[]{:S(2)}, u32[]{:S(2)}) collective-permute-start(bf16[32,3072]{1,0:T(8,128)(2,1)S(1)} %collective-permute-done.106.refs_38_), channel_id=1, source_target_pairs={{0,4},{8,0},{16,8},{24,16},{28,24},{20,28},{12,20},{4,12},{1,5},{9... | collective-permute-start | bytes 589832 | tf_op jit(solution)/shard_map/ppermute | solution.py:297
  434.2 14.5 %collective-permute-start.110 = (bf16[32,3072]{1,0:T(8,128)(2,1)S(1)}, bf16[32,3072]{1,0:T(8,128)(2,1)S(1)}, u32[]{:S(2)}, u32[]{:S(2)}) collective-permute-start(bf16[32,3072]{1,0:T(8,128)(2,1)S(1)} %collective-permute-done.106.refs_38_), channel_id=1, source_target_pairs={{0,1},{1,0},{2,3},{3,2},{4,5},{5,4},{6,7},{7,6},{8,9},{9,8},{10,11... | collective-permute-start | bytes 589832 | tf_op jit(solution)/shard_map/ppermute | solution.py:269
  447.1 119.5 %collective-permute-start.111 = (bf16[32,3072]{1,0:T(8,128)(2,1)}, bf16[32,3072]{1,0:T(8,128)(2,1)}, u32[]{:S(2)}, u32[]{:S(2)}) collective-permute-start(bf16[32,3072]{1,0:T(8,128)(2,1)} %collective-permute-done.98.refs_40_), channel_id=1, source_target_pairs={{0,1},{1,0},{2,3},{3,2},{4,5},{5,4},{6,7},{7,6},{8,9},{9,8},{10,11... | collective-permute-start | bytes 589832 | tf_op jit(solution)/shard_map/ppermute | solution.py:269
  447.1 119.6 %collective-permute-start.81 = (bf16[32,3072]{1,0:T(8,128)(2,1)}, bf16[32,3072]{1,0:T(8,128)(2,1)}, u32[]{:S(2)}, u32[]{:S(2)}) collective-permute-start(bf16[32,3072]{1,0:T(8,128)(2,1)} %collective-permute-done.80.refs_14_), channel_id=1, source_target_pairs={{0,1},{1,0},{2,3},{3,2},{4,5},{5,4},{6,7},{7,6},{8,9},{9,8},{10,11... | collective-permute-start | bytes 589832 | tf_op jit(solution)/shard_map/ppermute | solution.py:269
  447.6 120.8 %collective-permute-start.83 = (bf16[32,3072]{1,0:T(8,128)(2,1)}, bf16[32,3072]{1,0:T(8,128)(2,1)}, u32[]{:S(2)}, u32[]{:S(2)}) collective-permute-start(bf16[32,3072]{1,0:T(8,128)(2,1)} %collective-permute-done.82.refs_16_), channel_id=1, source_target_pairs={{0,1},{1,0},{2,3},{3,2},{4,5},{5,4},{6,7},{7,6},{8,9},{9,8},{10,11... | collective-permute-start | bytes 589832 | tf_op jit(solution)/shard_map/ppermute | solution.py:269
  448.4 120.4 %collective-permute-start.84 = (bf16[128,1024]{1,0:T(8,128)(2,1)S(1)}, bf16[128,1024]{1,0:T(8,128)(2,1)}, u32[]{:S(2)}, u32[]{:S(2)}) collective-permute-start(bf16[128,1024]{1,0:T(8,128)(2,1)S(1)} %collective-permute-done.78.refs_12_), channel_id=1, source_target_pairs={{0,8},{8,16},{16,24},{24,28},{28,20},{20,12},{12,4},{4,0},{1,9},{9... | collective-permute-start | bytes 786440 | tf_op jit(solution)/shard_map/ppermute | solution.py:297
  448.7 121.7 %collective-permute-start.93 = (bf16[128,1024]{1,0:T(8,128)(2,1)S(1)}, bf16[128,1024]{1,0:T(8,128)(2,1)}, u32[]{:S(2)}, u32[]{:S(2)}) collective-permute-start(bf16[128,1024]{1,0:T(8,128)(2,1)S(1)} %collective-permute-done.92.refs_37_), channel_id=1, source_target_pairs={{0,4},{8,0},{16,8},{24,16},{28,24},{20,28},{12,20},{4,12},{1,5},{9... | collective-permute-start | bytes 786440 | tf_op jit(solution)/shard_map/ppermute | solution.py:297
  566.7 347.0 %collective-permute-start.59 = (bf16[384,1024]{1,0:T(8,128)(2,1)}, bf16[384,1024]{1,0:T(8,128)(2,1)}, u32[]{:S(2)}, u32[]{:S(2)}) collective-permute-start(bf16[384,1024]{1,0:T(8,128)(2,1)} %collective-permute-done.58), channel_id=1, source_target_pairs={{0,1},{1,0},{2,3},{3,2},{4,5},{5,4},{6,7},{7,6},{8,9},{9,8},{10,11... | collective-permute-start | bytes 2359304 | tf_op jit(solution)/shard_map/ppermute | solution.py:269
  955.7 26.7 %collective-permute-start.114 = (bf16[384,1024]{1,0:T(8,128)(2,1)}, bf16[384,1024]{1,0:T(8,128)(2,1)}, u32[]{:S(2)}, u32[]{:S(2)}) collective-permute-start(bf16[384,1024]{1,0:T(8,128)(2,1)} %get-tuple-element.64), channel_id=1, source_target_pairs={{0,1},{1,0},{2,3},{3,2},{4,5},{5,4},{6,7},{7,6},{8,9},{9,8},{10,11... | collective-permute-start | bytes 2359304 | tf_op jit(solution)/shard_map/ppermute | solution.py:269
  955.8 30.6 %collective-permute-start.120 = (bf16[384,1024]{1,0:T(8,128)(2,1)}, bf16[384,1024]{1,0:T(8,128)(2,1)}, u32[]{:S(2)}, u32[]{:S(2)}) collective-permute-start(bf16[384,1024]{1,0:T(8,128)(2,1)} %get-tuple-element.63), channel_id=1, source_target_pairs={{0,1},{1,0},{2,3},{3,2},{4,5},{5,4},{6,7},{7,6},{8,9},{9,8},{10,11... | collective-permute-start | bytes 2359304 | tf_op jit(solution)/shard_map/ppermute | solution.py:269
  980.2 20.7 %collective-permute-start.122 = (bf16[384,1024]{1,0:T(8,128)(2,1)}, bf16[384,1024]{1,0:T(8,128)(2,1)S(1)}, u32[]{:S(2)}, u32[]{:S(2)}) collective-permute-start(bf16[384,1024]{1,0:T(8,128)(2,1)} %get-tuple-element.63), channel_id=1, source_target_pairs={{0,2},{1,3},{2,0},{3,1},{4,6},{5,7},{6,4},{7,5},{8,10},{9,11},{10,... | collective-permute-start | bytes 2359304 | tf_op jit(solution)/shard_map/ppermute | solution.py:269
  981.5 35.5 %collective-permute-start.116 = (bf16[384,1024]{1,0:T(8,128)(2,1)}, bf16[384,1024]{1,0:T(8,128)(2,1)S(1)}, u32[]{:S(2)}, u32[]{:S(2)}) collective-permute-start(bf16[384,1024]{1,0:T(8,128)(2,1)} %get-tuple-element.64), channel_id=1, source_target_pairs={{0,2},{1,3},{2,0},{3,1},{4,6},{5,7},{6,4},{7,5},{8,10},{9,11},{10,... | collective-permute-start | bytes 2359304 | tf_op jit(solution)/shard_map/ppermute | solution.py:269
  1000.9 23.5 %collective-permute-start.123 = (bf16[384,1024]{1,0:T(8,128)(2,1)S(1)}, bf16[384,1024]{1,0:T(8,128)(2,1)S(1)}, u32[]{:S(2)}, u32[]{:S(2)}) collective-permute-start(bf16[384,1024]{1,0:T(8,128)(2,1)S(1)} %collective-permute-done.122), channel_id=1, source_target_pairs={{0,1},{1,0},{2,3},{3,2},{4,5},{5,4},{6,7},{7,6},{8,9},{9,8},{10,11... | collective-permute-start | bytes 2359304 | tf_op jit(solution)/shard_map/ppermute | solution.py:269
  1037.7 13.7 %collective-permute-start.182 = (bf16[128,1024]{1,0:T(8,128)(2,1)S(1)}, bf16[128,1024]{1,0:T(8,128)(2,1)S(1)}, u32[]{:S(2)}, u32[]{:S(2)}) collective-permute-start(bf16[128,1024]{1,0:T(8,128)(2,1)S(1)} %get-tuple-element.89), channel_id=1, source_target_pairs={{0,8},{8,16},{16,24},{24,28},{28,20},{20,12},{12,4},{4,0},{1,9},{9... | collective-permute-start | bytes 786440 | tf_op jit(solution)/shard_map/ppermute | solution.py:297
  1038.7 15.8 %collective-permute-start.118 = (bf16[384,1024]{1,0:T(8,128)(2,1)S(1)}, bf16[384,1024]{1,0:T(8,128)(2,1)S(1)}, u32[]{:S(2)}, u32[]{:S(2)}) collective-permute-start(bf16[384,1024]{1,0:T(8,128)(2,1)S(1)} %slice.329), channel_id=1, source_target_pairs={{0,1},{1,0},{2,3},{3,2},{4,5},{5,4},{6,7},{7,6},{8,9},{9,8},{10,11... | collective-permute-start | bytes 2359304 | tf_op jit(solution)/shard_map/ppermute | solution.py:269
  1047.6 46.5 %collective-permute-start.121 = (bf16[384,1024]{1,0:T(8,128)(2,1)}, bf16[384,1024]{1,0:T(8,128)(2,1)}, u32[]{:S(2)}, u32[]{:S(2)}) collective-permute-start(bf16[384,1024]{1,0:T(8,128)(2,1)} %slice.650), channel_id=1, source_target_pairs={{0,1},{1,0},{2,3},{3,2},{4,5},{5,4},{6,7},{7,6},{8,9},{9,8},{10,11... | collective-permute-start | bytes 2359304 | tf_op jit(solution)/shard_map/ppermute | solution.py:269
  1051.2 15.9 %collective-permute-start.124 = (bf16[384,1024]{1,0:T(8,128)(2,1)S(1)}, bf16[384,1024]{1,0:T(8,128)(2,1)S(1)}, u32[]{:S(2)}, u32[]{:S(2)}) collective-permute-start(bf16[384,1024]{1,0:T(8,128)(2,1)S(1)} %slice.333), channel_id=1, source_target_pairs={{0,1},{1,0},{2,3},{3,2},{4,5},{5,4},{6,7},{7,6},{8,9},{9,8},{10,11... | collective-permute-start | bytes 2359304 | tf_op jit(solution)/shard_map/ppermute | solution.py:269
  1051.4 17.9 %collective-permute-start.190 = (bf16[128,1024]{1,0:T(8,128)(2,1)S(1)}, bf16[128,1024]{1,0:T(8,128)(2,1)S(1)}, u32[]{:S(2)}, u32[]{:S(2)}) collective-permute-start(bf16[128,1024]{1,0:T(8,128)(2,1)S(1)} %get-tuple-element.80), channel_id=1, source_target_pairs={{0,8},{8,16},{16,24},{24,28},{28,20},{20,12},{12,4},{4,0},{1,9},{9... | collective-permute-start | bytes 786440 | tf_op jit(solution)/shard_map/ppermute | solution.py:297
  1069.3 24.9 %collective-permute-start.125 = (bf16[384,1024]{1,0:T(8,128)(2,1)}, bf16[384,1024]{1,0:T(8,128)(2,1)}, u32[]{:S(2)}, u32[]{:S(2)}) collective-permute-start(bf16[384,1024]{1,0:T(8,128)(2,1)} %add_convert_fusion.4), channel_id=1, source_target_pairs={{0,2},{1,3},{2,0},{3,1},{4,6},{5,7},{6,4},{7,5},{8,10},{9,11},{10,... | collective-permute-start | bytes 2359304 | tf_op jit(solution)/shard_map/ppermute | solution.py:269
  1090.9 18.9 %collective-permute-start.119 = (bf16[384,1024]{1,0:T(8,128)(2,1)}, bf16[384,1024]{1,0:T(8,128)(2,1)}, u32[]{:S(2)}, u32[]{:S(2)}) collective-permute-start(bf16[384,1024]{1,0:T(8,128)(2,1)} %add_convert_fusion.6), channel_id=1, source_target_pairs={{0,2},{1,3},{2,0},{3,1},{4,6},{5,7},{6,4},{7,5},{8,10},{9,11},{10,... | collective-permute-start | bytes 2359304 | tf_op jit(solution)/shard_map/ppermute | solution.py:269
  1176.9 31.4 %collective-permute-start.169 = (bf16[8,2,32,1024]{3,2,1,0:T(8,128)(2,1)S(1)}, bf16[8,2,32,1024]{3,2,1,0:T(8,128)(2,1)S(1)}, u32[]{:S(2)}, u32[]{:S(2)}) collective-permute-start(bf16[8,2,32,1024]{3,2,1,0:T(8,128)(2,1)S(1)} %select_bitcast_fusion.3), channel_id=1, source_target_pairs={{0,1},{1,0},{2,3},{3,2},{4,5},{5,4},{6,7},{7,6},{8,9},{9,8},{10,11... | collective-permute-start | bytes 3145736 | tf_op jit(solution)/shard_map/ppermute | solution.py:269
  1198.5 56.1 %collective-permute-start.150 = (bf16[8,2,32,3072]{3,2,1,0:T(8,128)(2,1)S(1)}, bf16[8,2,32,3072]{3,2,1,0:T(8,128)(2,1)S(1)}, u32[]{:S(2)}, u32[]{:S(2)}) collective-permute-start(bf16[8,2,32,3072]{3,2,1,0:T(8,128)(2,1)S(1)} %select_bitcast_fusion), channel_id=1, source_target_pairs={{0,1},{1,0},{2,3},{3,2},{4,5},{5,4},{6,7},{7,6},{8,9},{9,8},{10,11... | collective-permute-start | bytes 9437192 | tf_op jit(solution)/shard_map/ppermute | solution.py:269
  1206.4 30.5 %collective-permute-start.129 = (bf16[384,1024]{1,0:T(8,128)(2,1)S(1)}, bf16[384,1024]{1,0:T(8,128)(2,1)S(1)}, u32[]{:S(2)}, u32[]{:S(2)}) collective-permute-start(bf16[384,1024]{1,0:T(8,128)(2,1)S(1)} %get-tuple-element.76), channel_id=1, source_target_pairs={{0,1},{1,0},{2,3},{3,2},{4,5},{5,4},{6,7},{7,6},{8,9},{9,8},{10,11... | collective-permute-start | bytes 2359304 | tf_op jit(solution)/shard_map/ppermute | solution.py:269
  1207.3 29.7 %collective-permute-start.131 = (bf16[384,1024]{1,0:T(8,128)(2,1)S(1)}, bf16[384,1024]{1,0:T(8,128)(2,1)S(1)}, u32[]{:S(2)}, u32[]{:S(2)}) collective-permute-start(bf16[384,1024]{1,0:T(8,128)(2,1)S(1)} %add_convert_fusion.3), channel_id=1, source_target_pairs={{0,2},{1,3},{2,0},{3,1},{4,6},{5,7},{6,4},{7,5},{8,10},{9,11},{10,... | collective-permute-start | bytes 2359304 | tf_op jit(solution)/shard_map/ppermute | solution.py:269
  1245.9 22.8 %collective-permute-start.141 = (bf16[8,2,32,2048]{3,2,1,0:T(8,128)(2,1)}, bf16[8,2,32,2048]{3,2,1,0:T(8,128)(2,1)}, u32[]{:S(2)}, u32[]{:S(2)}) collective-permute-start(bf16[8,2,32,2048]{3,2,1,0:T(8,128)(2,1)} %select_bitcast_fusion.1), channel_id=1, source_target_pairs={{0,1},{1,0},{2,3},{3,2},{4,5},{5,4},{6,7},{7,6},{8,9},{9,8},{10,11... | collective-permute-start | bytes 6291464 | tf_op jit(solution)/shard_map/ppermute | solution.py:269
  1248.8 24.9 %collective-permute-start.132 = (bf16[8,2,64,1024]{3,2,1,0:T(8,128)(2,1)S(1)}, bf16[8,2,64,1024]{3,2,1,0:T(8,128)(2,1)}, u32[]{:S(2)}, u32[]{:S(2)}) collective-permute-start(bf16[8,2,64,1024]{3,2,1,0:T(8,128)(2,1)S(1)} %select_bitcast_fusion.2), channel_id=1, source_target_pairs={{0,1},{1,0},{2,3},{3,2},{4,5},{5,4},{6,7},{7,6},{8,9},{9,8},{10,11... | collective-permute-start | bytes 6291464 | tf_op jit(solution)/shard_map/ppermute | solution.py:269
  1263.2 21.7 %collective-permute-start.155 = (bf16[2,32,3072]{2,1,0:T(8,128)(2,1)S(1)}, bf16[2,32,3072]{2,1,0:T(8,128)(2,1)S(1)}, u32[]{:S(2)}, u32[]{:S(2)}) collective-permute-start(bf16[2,32,3072]{2,1,0:T(8,128)(2,1)S(1)} %get-tuple-element.73), channel_id=1, source_target_pairs={{0,8},{8,16},{16,24},{24,28},{28,20},{20,12},{12,4},{4,0},{1,9},{9... | collective-permute-start | bytes 1179656 | tf_op jit(solution)/shard_map/ppermute | solution.py:297
  1268.1 18.4 %collective-permute-start.152 = (bf16[2,32,3072]{2,1,0:T(8,128)(2,1)S(1)}, bf16[2,32,3072]{2,1,0:T(8,128)(2,1)S(1)}, u32[]{:S(2)}, u32[]{:S(2)}) collective-permute-start(bf16[2,32,3072]{2,1,0:T(8,128)(2,1)S(1)} %fusion.56), channel_id=1, source_target_pairs={{0,4},{8,0},{16,8},{24,16},{28,24},{20,28},{12,20},{4,12},{1,5},{9... | collective-permute-start | bytes 1179656 | tf_op jit(solution)/shard_map/ppermute | solution.py:297
  1271.6 12.6 collective-permute-start.142
  1273.3 15.6 %collective-permute-start.146 = (bf16[2,32,2048]{2,1,0:T(8,128)(2,1)S(1)}, bf16[2,32,2048]{2,1,0:T(8,128)(2,1)S(1)}, u32[]{:S(2)}, u32[]{:S(2)}) collective-permute-start(bf16[2,32,2048]{2,1,0:T(8,128)(2,1)S(1)} %get-tuple-element.95), channel_id=1, source_target_pairs={{0,8},{8,16},{16,24},{24,28},{28,20},{20,12},{12,4},{4,0},{1,9},{9... | collective-permute-start | bytes 786440 | tf_op jit(solution)/shard_map/ppermute | solution.py:297
  1284.3 25.6 %collective-permute-start.137 = (bf16[2,64,1024]{2,1,0:T(8,128)(2,1)S(1)}, bf16[2,64,1024]{2,1,0:T(8,128)(2,1)S(1)}, u32[]{:S(2)}, u32[]{:S(2)}) collective-permute-start(bf16[2,64,1024]{2,1,0:T(8,128)(2,1)S(1)} %get-tuple-element.101), channel_id=1, source_target_pairs={{0,4},{8,0},{16,8},{24,16},{28,24},{20,28},{12,20},{4,12},{1,5},{9... | collective-permute-start | bytes 786440 | tf_op jit(solution)/shard_map/ppermute | solution.py:297
  1284.9 14.2 %collective-permute-start.143 = (bf16[2,32,2048]{2,1,0:T(8,128)(2,1)S(1)}, bf16[2,32,2048]{2,1,0:T(8,128)(2,1)S(1)}, u32[]{:S(2)}, u32[]{:S(2)}) collective-permute-start(bf16[2,32,2048]{2,1,0:T(8,128)(2,1)S(1)} %fusion.75), channel_id=1, source_target_pairs={{0,4},{8,0},{16,8},{24,16},{28,24},{20,28},{12,20},{4,12},{1,5},{9... | collective-permute-start | bytes 786440 | tf_op jit(solution)/shard_map/ppermute | solution.py:297
  1286.7 20.8 %collective-permute-start.153 = (bf16[2,32,3072]{2,1,0:T(8,128)(2,1)S(1)}, bf16[2,32,3072]{2,1,0:T(8,128)(2,1)S(1)}, u32[]{:S(2)}, u32[]{:S(2)}) collective-permute-start(bf16[2,32,3072]{2,1,0:T(8,128)(2,1)S(1)} %get-tuple-element.70), channel_id=1, source_target_pairs={{0,4},{8,0},{16,8},{24,16},{28,24},{20,28},{12,20},{4,12},{1,5},{9... | collective-permute-start | bytes 1179656 | tf_op jit(solution)/shard_map/ppermute | solution.py:297
  1288.3 20.8 %collective-permute-start.156 = (bf16[2,32,3072]{2,1,0:T(8,128)(2,1)S(1)}, bf16[2,32,3072]{2,1,0:T(8,128)(2,1)S(1)}, u32[]{:S(2)}, u32[]{:S(2)}) collective-permute-start(bf16[2,32,3072]{2,1,0:T(8,128)(2,1)S(1)} %get-tuple-element.71), channel_id=1, source_target_pairs={{0,8},{8,16},{16,24},{24,28},{28,20},{20,12},{12,4},{4,0},{1,9},{9... | collective-permute-start | bytes 1179656 | tf_op jit(solution)/shard_map/ppermute | solution.py:297
  1288.9 22.4 %collective-permute-start.134 = (bf16[2,64,1024]{2,1,0:T(8,128)(2,1)S(1)}, bf16[2,64,1024]{2,1,0:T(8,128)(2,1)S(1)}, u32[]{:S(2)}, u32[]{:S(2)}) collective-permute-start(bf16[2,64,1024]{2,1,0:T(8,128)(2,1)S(1)} %fusion.81), channel_id=1, source_target_pairs={{0,8},{8,16},{16,24},{24,28},{28,20},{20,12},{12,4},{4,0},{1,9},{9... | collective-permute-start | bytes 786440 | tf_op jit(solution)/shard_map/ppermute | solution.py:297
  1299.3 13.9 %collective-permute-start.144 = (bf16[2,32,2048]{2,1,0:T(8,128)(2,1)S(1)}, bf16[2,32,2048]{2,1,0:T(8,128)(2,1)S(1)}, u32[]{:S(2)}, u32[]{:S(2)}) collective-permute-start(bf16[2,32,2048]{2,1,0:T(8,128)(2,1)S(1)} %get-tuple-element.92), channel_id=1, source_target_pairs={{0,4},{8,0},{16,8},{24,16},{28,24},{20,28},{12,20},{4,12},{1,5},{9... | collective-permute-start | bytes 786440 | tf_op jit(solution)/shard_map/ppermute | solution.py:297
  1309.8 15.0 %collective-permute-start.157 = (bf16[2,32,3072]{2,1,0:T(8,128)(2,1)S(1)}, bf16[2,32,3072]{2,1,0:T(8,128)(2,1)S(1)}, u32[]{:S(2)}, u32[]{:S(2)}) collective-permute-start(bf16[2,32,3072]{2,1,0:T(8,128)(2,1)S(1)} %get-tuple-element.69), channel_id=1, source_target_pairs={{0,8},{8,16},{16,24},{24,28},{28,20},{20,12},{12,4},{4,0},{1,9},{9... | collective-permute-start | bytes 1179656 | tf_op jit(solution)/shard_map/ppermute | solution.py:297
  1311.5 18.7 %collective-permute-start.135 = (bf16[2,64,1024]{2,1,0:T(8,128)(2,1)S(1)}, bf16[2,64,1024]{2,1,0:T(8,128)(2,1)S(1)}, u32[]{:S(2)}, u32[]{:S(2)}) collective-permute-start(bf16[2,64,1024]{2,1,0:T(8,128)(2,1)S(1)} %get-tuple-element.98), channel_id=1, source_target_pairs={{0,8},{8,16},{16,24},{24,28},{28,20},{20,12},{12,4},{4,0},{1,9},{9... | collective-permute-start | bytes 786440 | tf_op jit(solution)/shard_map/ppermute | solution.py:297
  1313.2 17.0 %collective-permute-start.138 = (bf16[2,64,1024]{2,1,0:T(8,128)(2,1)S(1)}, bf16[2,64,1024]{2,1,0:T(8,128)(2,1)S(1)}, u32[]{:S(2)}, u32[]{:S(2)}) collective-permute-start(bf16[2,64,1024]{2,1,0:T(8,128)(2,1)S(1)} %get-tuple-element.99), channel_id=1, source_target_pairs={{0,4},{8,0},{16,8},{24,16},{28,24},{20,28},{12,20},{4,12},{1,5},{9... | collective-permute-start | bytes 786440 | tf_op jit(solution)/shard_map/ppermute | solution.py:297
  1316.9 15.9 %collective-permute-start.145 = (bf16[2,32,2048]{2,1,0:T(8,128)(2,1)S(1)}, bf16[2,32,2048]{2,1,0:T(8,128)(2,1)S(1)}, u32[]{:S(2)}, u32[]{:S(2)}) collective-permute-start(bf16[2,32,2048]{2,1,0:T(8,128)(2,1)S(1)} %get-tuple-element.90), channel_id=1, source_target_pairs={{0,4},{8,0},{16,8},{24,16},{28,24},{20,28},{12,20},{4,12},{1,5},{9... | collective-permute-start | bytes 786440 | tf_op jit(solution)/shard_map/ppermute | solution.py:297
  (290 other events, 7048.7 us)

commit v2 on v1

--- a/solution.py
+++ b/solution.py
@@ -275,8 +275,10 @@
     return [v, near, far, swap(far, 1)]
 
 
-def collect(parts):
+def collect(parts, wait=()):
     low = [part.astype(bf16) for part in parts]
+    if wait:
+        low = list(after(tuple(low), *wait))
     far_near = swap(low[3], 1)
     near = swap(low[1], 1)
     far = swap((low[2].astype(f32) + far_near.astype(f32)).astype(bf16), 2)
@@ -357,10 +359,11 @@
             num_scalar_prefetch=1,
             grid=(1,),
             in_specs=[anywhere] * len(arrays),
-            out_specs=[anywhere] * len(shapes),
+            out_specs=[pl.BlockSpec(shape, lambda i, index: (0, 0)) for shape in shapes],
             scratch_shapes=[pltpu.SemaphoreType.DMA((len(copies),))],
         ),
         out_shape=[jax.ShapeDtypeStruct(shape, bf16) for shape in shapes],
+        compiler_params=pltpu.CompilerParams(vmem_limit_bytes=40 * 2**20),
         name="assemble",
     )(index, *arrays)
 
@@ -384,20 +387,19 @@
         return assemble(self.index, self.arrays, self.copies, self.shapes)
 
 
-def scatter_full(grad, me, place, groups, way):
-    rows, columns = grad.shape
-    if groups != 8:
-        low = grad.astype(bf16).reshape(groups * 4, rows // (groups * 4), columns)
-        return lax.psum_scatter(low, ("dp", "seq"), scatter_dimension=0).astype(f32)
-    low = grad.astype(bf16).reshape(groups, 2, 2, rows // (groups * 4), columns)
-    odd, high = (me & 1) == 1, (me & 2) == 2
-    keep = jnp.where(odd, low[:, :, 1], low[:, :, 0])
-    send = jnp.where(odd, low[:, :, 0], low[:, :, 1])
-    both = (keep.astype(f32) + swap(send, 1).astype(f32)).astype(bf16)
-    mine = ring_scatter(both, place, way)
-    keep = jnp.where(high, mine[1], mine[0])
-    send = jnp.where(high, mine[0], mine[1]).astype(bf16)
-    return keep + swap(send, 2).astype(f32)
+def half(v, which):
+    middle = v.shape[1] // 2
+    return jnp.where(which == 1, v[:, middle:], v[:, :middle])
+
+
+def merge(mine, other, core):
+    return jnp.concatenate(
+        [jnp.where(core == 1, other, mine), jnp.where(core == 1, mine, other)], axis=1
+    )
+
+
+def by_dp(grad, groups):
+    return grad.reshape(groups, grad.shape[0] // groups, grad.shape[1])
 
 
 def scatter_dp(grad, place, groups, way):
@@ -407,11 +409,16 @@
     return ring_scatter(low, place, way)
 
 
-def to_rows(block, me):
+def finish(block, me):
     rows = block.shape[0] // 4
     low = block.astype(bf16)
     parts = by_place([low[t * rows : (t + 1) * rows] for t in range(4)], me)
     return by_place(exchange(parts), me)
+
+
+def halves_sum(parts):
+    total = [parts[c].astype(f32) + parts[2 + c].astype(f32) for c in range(2)]
+    return jnp.concatenate(total, axis=1)
 
 
 def on_device(
@@ -438,30 +445,32 @@
     local = width // 4
     local_hidden = hidden // 4
 
-    triple = jnp.stack(
-        [w.reshape(-1, 4, local) for w in (query_weight, key_weight, value_weight)], axis=2
-    )
-    triple = triple.reshape(-1, 4, 3 * local)
-    upper_w = up_weight.reshape(-1, groups, 4, hidden // (groups * 4)).transpose(0, 2, 1, 3)
-    upper_w = upper_w.reshape(-1, 4, local_hidden)
-    qkv_parts = exchange(by_place([triple[:, t] for t in range(4)], me))
-    up_parts = exchange(by_place([upper_w[:, t] for t in range(4)], me))
-
+    core = me & 1
+    hidden_block = hidden // (groups * 4)
+
+    triple = [
+        jnp.concatenate(
+            [w[:, t * local : (t + 1) * local] for w in (query_weight, key_weight, value_weight)],
+            axis=1,
+        )
+        for t in range(4)
+    ]
+    upper_w = [
+        jnp.concatenate(
+            [
+                up_weight[:, (g * 4 + t) * hidden_block : (g * 4 + t + 1) * hidden_block]
+                for g in range(groups)
+            ],
+            axis=1,
+        )
+        for t in range(4)
+    ]
     time_a, time_b = time_weight[:, : 2 * width], time_weight[:, 2 * width :]
     if groups == 8:
         place = jnp.asarray(PLACE, jnp.int32)[dp]
         order = jnp.asarray(RING, jnp.int32)[(place - jnp.arange(8)) % 8]
         index = jnp.concatenate([order, me[None].astype(jnp.int32)])
-        n_skip, n_time, n_out = skip_weight.shape[0], time_weight.shape[0], out_weight.shape[0]
-
-        def full_piece(gather, piece, k, j, layout):
-            near = swap(piece, 1)
-            for array, jj in ((piece, j), (near, j ^ 1)):
-                gather.add(
-                    array,
-                    k,
-                    [(row, count, out, jj, 4 * count, count, column) for row, count, out, column in layout],
-                )
+        n_skip, n_time = skip_weight.shape[0], time_weight.shape[0]
 
         first = Gather(index)
         o_skip, o_time_a = first.out(32 * n_skip, width), first.out(32 * n_time, 2 * width)
@@ -473,57 +482,49 @@
         ]
         found_own, found_far = ring_gather(own, 1), ring_gather(swap(own, 2), -1)
         for k in range(8):
-            full_piece(first, found_own[k], k, 0, layout)
-            full_piece(first, found_far[k], k, 2, layout)
+            for piece, j in ((found_own[k], 0), (found_far[k], 2)):
+                for array, jj in ((piece, j), (swap(piece, 1), j ^ 1)):
+                    first.add(
+                        array,
+                        k,
+                        [(row, count, out, jj, 4 * count, count, column) for row, count, out, column in layout],
+                    )
         skip_full, time_a_full = first.run()
 
+        rest = []
+        for t in range(4):
+            sides = jnp.concatenate(
+                [
+                    w[:, (t & 1) * (w.shape[1] // 2) : ((t & 1) + 1) * (w.shape[1] // 2)]
+                    for w in (time_b, out_weight)
+                ],
+                axis=1,
+            )
+            rest.append(jnp.concatenate([triple[t], upper_w[t], sides], axis=1))
+        rest = jnp.concatenate(by_place(exchange(by_place(rest, me)), me), axis=0)
+        split = 3 * local, 3 * local + local_hidden
+        wide = lax.all_gather(rest[:, split[1] :], "dp", axis=0, tiled=True)
+        wide = (wide, swap(wide, 1))
+        time_b_sides = [w[:, : 3 * width // 2] for w in wide]
+        out_sides = [w[:, 3 * width // 2 :] for w in wide]
+
         second = Gather(index)
-        o_triple, o_out = second.out(width, 3 * local), second.out(width, width)
-        triple_own = jnp.concatenate(qkv_parts, axis=0)
-        out_own = jnp.concatenate([out_weight, swap(out_weight, 2)], axis=0)
-        triple_own, out_own = after(
-            (triple_own, out_own), found_own[4], found_far[4], found_own[5], found_far[3]
-        )
-        found_triple, found_out = ring_gather(triple_own, 1), ring_gather(out_own, -1)
-        n_triple = query_weight.shape[0]
+        o_triple = second.out(width, 3 * local)
+        triple_own = after(rest[:, : split[0]], found_own[4], found_far[4], found_own[5], found_far[3])
+        found = ring_gather(triple_own, 1)
         for k in range(8):
-            second.add(
-                found_triple[k],
-                k,
-                [(j * n_triple, n_triple, o_triple, j, 4 * n_triple, n_triple, 0) for j in range(4)],
-            )
-            near = swap(found_out[k], 1)
-            for array, flip in ((found_out[k], 0), (near, 1)):
-                second.add(
-                    array,
-                    k,
-                    [(jj * n_out, n_out, o_out, (2 * jj) ^ flip, 4 * n_out, n_out, 0) for jj in range(2)],
-                )
-        triple_full, out_full = second.run()
+            second.add(found[k], k, [(0, width // 8, o_triple, 0, width // 8, 0, 0)])
+        (triple_full,) = second.run()
 
         third = Gather(index)
         o_up, o_down = third.out(width, local_hidden), third.out(local_hidden, width)
-        o_time_b = third.out(32 * n_time, 3 * width)
-        up_own = jnp.concatenate(up_parts, axis=0)
-        down_own, time_own = down_weight, time_b
-        up_own, down_own, time_own, time_far = after(
-            (up_own, down_own, time_own, swap(time_b, 2)),
-            found_triple[4],
-            found_out[4],
-            found_triple[5],
-            found_out[3],
-        )
+        up_own, down_own = after((rest[:, split[0] : split[1]], down_weight), found[4], found[5])
         found_up, found_down = ring_gather(up_own, 1), ring_gather(down_own, -1)
-        found_own, found_far = ring_gather(time_own, 1), ring_gather(time_far, -1)
-        n_up, n_down = up_weight.shape[0], down_weight.shape[0]
+        n_down = down_weight.shape[0]
         for k in range(8):
-            third.add(
-                found_up[k], k, [(j * n_up, n_up, o_up, j, 4 * n_up, n_up, 0) for j in range(4)]
-            )
+            third.add(found_up[k], k, [(0, width // 8, o_up, 0, width // 8, 0, 0)])
             third.add(found_down[k], k, [(0, n_down, o_down, 0, n_down, 0, 0)])
-            full_piece(third, found_own[k], k, 0, [(0, n_time, o_time_b, 0)])
-            full_piece(third, found_far[k], k, 2, [(0, n_time, o_time_b, 0)])
-        up_full, down_full, time_b_full = third.run()
+        up_full, down_full = third.run()
     else:
         place = dp
         skip_full, time_a_full, time_b_full, out_full = (
@@ -531,10 +532,17 @@
             for w in (skip_weight, time_a, time_b, out_weight)
         )
         triple_full, up_full = (
-            lax.all_gather(jnp.concatenate(by_place(parts, me), axis=0), "dp", axis=0, tiled=True)
-            for parts in (qkv_parts, up_parts)
+            lax.all_gather(
+                jnp.concatenate(by_place(exchange(by_place(parts, me)), me), axis=0),
+                "dp",
+                axis=0,
+                tiled=True,
+            )
+            for parts in (triple, upper_w)
         )
         down_full = lax.all_gather(down_weight, "dp", axis=0, tiled=True)
+        time_b_sides = [half(time_b_full, core), half(time_b_full, 1 - core)]
+        out_sides = [half(out_full, core), half(out_full, 1 - core)]
 
     marks = jnp.concatenate(spread(jnp.concatenate([segment_ids, positions, valid_mask])), axis=1)
     cosine, sine, query_marks, key_marks = frame_tables(marks[0], marks[1], marks[2])
@@ -552,10 +560,14 @@
         by_place(exchange([att[j * frames : (j + 1) * frames] for j in range(4)]), me), axis=1
     )
 
-    shift_b, scale_b, gate_b = jnp.split(dot_nn(time_act, time_b_full), 3, axis=1)
+    shift_b, scale_b, gate_b = jnp.split(
+        merge(dot_nn(time_act, time_b_sides[0]), dot_nn(time_act, time_b_sides[1]), core),
+        3,
+        axis=1,
+    )
     upstream = cotangent.reshape(frames, width).astype(f32)
     ffn_grad = spread((upstream * gate_b).astype(bf16))
-    middle = base + dot_nn(attended, out_full)
+    middle = base + merge(dot_nn(attended, out_sides[0]), dot_nn(attended, out_sides[1]), core)
     normed_b, inverse_b = norm_rows(middle)
     hidden_b = spread((normed_b * (1.0 + scale_b) + shift_b).astype(bf16))
     hb = [jnp.concatenate(hidden_b[:2]), jnp.concatenate(hidden_b[2:])]
@@ -568,7 +580,9 @@
         [back[0][:frames], back[0][frames:], back[1][:frames], back[1][frames:]]
     )
     part = [dot_nn(a, down_full) for a in acted]
-    ffn = collect([part[0][:frames], part[0][frames:], part[1][:frames], part[1][frames:]])
+    ffn = collect(
+        [part[0][:frames], part[0][frames:], part[1][:frames], part[1][frames:]], (hidden_b_grad,)
+    )
     grad_down = dot_tn(acted[0], fg[0]) + dot_tn(acted[1], fg[1])
     grad_up = dot_tn(hb[0], ug[0]) + dot_tn(hb[1], ug[1])
     output = (middle + gate_b * ffn).astype(bf16).reshape(rows, frames, width)
@@ -577,14 +591,30 @@
     scale_b_grad = hidden_b_grad * normed_b
     middle_grad = upstream + norm_back(hidden_b_grad * (1.0 + scale_b), normed_b, inverse_b)
     branch_grad = middle_grad.astype(bf16)
-    attended_grad = dot_nt(branch_grad, out_full).astype(bf16)
+    branch_sides = [half(branch_grad, core), half(branch_grad, 1 - core)]
+    attended_grad = (
+        dot_nt(branch_sides[0], out_sides[0]) + dot_nt(branch_sides[1], out_sides[1])
+    ).astype(bf16)
     att_grad = exchange(
         by_place([attended_grad[:, t * local : (t + 1) * local] for t in range(4)], me)
     )
-    grad_out = dot_tn(attended, branch_grad)
     modul_b_grad = jnp.concatenate([hidden_b_grad, scale_b_grad, gate_b_grad], axis=1).astype(bf16)
-    grad_time_b = dot_tn(time_act, modul_b_grad)
-    time_back_b = dot_nt(modul_b_grad, time_b_full)
+    modul_sides = [half(modul_b_grad, core), half(modul_b_grad, 1 - core)]
+    time_back_b = dot_nt(modul_sides[0], time_b_sides[0]) + dot_nt(modul_sides[1], time_b_sides[1])
+    grad_wide = [
+        jnp.concatenate(
+            [dot_tn(time_act, modul_sides[i]).astype(bf16), dot_tn(attended, branch_sides[i]).astype(bf16)],
+            axis=1,
+        )
+        for i in (0, 1)
+    ]
+    grad_wide = grad_wide[0].astype(f32) + swap(grad_wide[1], 1).astype(f32)
+    wide_sum = scatter_dp(by_dp(grad_wide, groups), place, groups, 1)
+    ffn_sum = lax.psum_scatter(
+        by_dp(jnp.concatenate([grad_up.astype(bf16), grad_down.astype(bf16)], axis=1), groups),
+        "dp",
+        scatter_dimension=0,
+    ).astype(f32)
     triple_grad = attend_back(
         att_grad, qkv, query_rot, key_rot, att, logsum, cosine, sine, query_marks, key_marks
     )
@@ -596,28 +626,49 @@
     base_grad = (
         middle_grad + norm_back(hidden_a_grad * (1.0 + scale_a), normed_a, inverse_a)
     ).astype(bf16)
-    grad_skip = dot_tn(joined, base_grad)
     joined_grad = dot_nt(base_grad, skip_full)
     modul_a_grad = jnp.concatenate([hidden_a_grad, scale_a_grad], axis=1).astype(bf16)
-    grad_time_a = dot_tn(time_act, modul_a_grad)
     time_back = dot_nt(modul_a_grad, time_a_full) + time_back_b
     time_grad = (time_back * silu_slope(time_value)).reshape(rows, frames, width)
 
-    by_dp = lambda grad: grad.reshape(groups, grad.shape[0] // groups, grad.shape[1])
-    down_sum = scatter_dp(by_dp(grad_down), place, groups, 1)
-    up_sum = to_rows(scatter_dp(by_dp(grad_up), place, groups, -1), me)
-    up_sum = jnp.stack(
-        [u.reshape(-1, groups, hidden // (groups * 4)) for u in up_sum], axis=2
-    ).reshape(-1, hidden)
-    out_sum = scatter_full(grad_out, me, place, groups, 1)
-    time_b_sum = scatter_full(grad_time_b, me, place, groups, -1)
-    qkv_sum = to_rows(scatter_dp(by_dp(grad_triple), place, groups, 1), me)
+    grad_last = []
+    for i in (0, 1):
+        skip_side = by_dp(dot_tn(joined, half(base_grad, core ^ i)).astype(bf16), groups)
+        rows_skip = skip_side.shape[1] // 8
+        skip_side = skip_side.reshape(groups, 4, 2, rows_skip, -1)
+        skip_side = jnp.concatenate([skip_side[:, :, 0], skip_side[:, :, 1]], axis=3)
+        time_side = by_dp(dot_tn(time_act, half(modul_a_grad, core ^ i)).astype(bf16), groups)
+        grad_last.append(
+            jnp.concatenate([skip_side.reshape(groups, 4 * rows_skip, -1), time_side], axis=2)
+        )
+    grad_last = grad_last[0].astype(f32) + swap(grad_last[1], 1).astype(f32)
+    qkv_sum = scatter_dp(by_dp(grad_triple, groups), place, groups, -1)
+    last_sum = scatter_dp(grad_last, place, groups, 1)
+
+    parts = finish(jnp.concatenate([ffn_sum[:, :local_hidden], wide_sum], axis=1), me)
+    up_sum = jnp.concatenate(
+        [
+            p[:, g * hidden_block : (g + 1) * hidden_block]
+            for g in range(groups)
+            for p in parts
+        ],
+        axis=1,
+    )
+    split = local_hidden, local_hidden + 3 * width // 2
+    time_b_sum = halves_sum([p[:, split[0] : split[1]] for p in parts])
+    out_sum = halves_sum([p[:, split[1] :] for p in parts])
+    parts = finish(jnp.concatenate([qkv_sum, last_sum], axis=1), me)
     qkv_sum = [
-        jnp.concatenate([q[:, i * local : (i + 1) * local] for q in qkv_sum], axis=1)
-        for i in range(3)
+        jnp.concatenate([p[:, i * local : (i + 1) * local] for p in parts], axis=1) for i in range(3)
     ]
-    skip_sum = scatter_full(grad_skip, me, place, groups, 1)
-    time_a_sum = scatter_full(grad_time_a, me, place, groups, -1)
+    split = 3 * local, 3 * local + width // 2, 3 * local + width
+    skip_sum = jnp.concatenate(
+        [
+            halves_sum([p[:, split[i] : split[i + 1]] for p in parts]) for i in range(2)
+        ],
+        axis=0,
+    )
+    time_a_sum = halves_sum([p[:, split[2] :] for p in parts])
     return (
         output,
         joined_grad[:, :width].reshape(rows, frames, width),
@@ -630,7 +681,7 @@
         qkv_sum[2].astype(f32),
         out_sum,
         up_sum.astype(f32),
-        down_sum,
+        ffn_sum[:, local_hidden:],
     )
 
 

time: 1350 us -> 648 us (0.48)
  Pallas kernels: 749 us -> 71.4 us
  starting transfers between devices: 159 us -> 86.9 us
  local copies, waits for them, and re-layouts: 22.7 us -> 54.4 us
  between operations: 26.9 us -> 40.6 us
    pallas_call x3, Pallas kernels: 690 us -> 13.6 us  [assemble(): pl.pallas_call(functools.partial(assemble_kernel, tuple(copies), len(arra...]
    ppermute x105 -> x56, starting transfers between devices: 124 us -> 62.2 us  [ring_step(): lax.ppermute(v, 'dp', [(RING[i], RING[(i + step) % 8]) for i in range(8)])]
    unnamed x320 -> x291, local copies, waits for them, and re-layouts: 9.73 us -> 39.3 us
    ppermute x90 -> x56, starting transfers between devices: 35.7 us -> 24.6 us  [swap(): return lax.ppermute(v, 'seq', [(i, i ^ mask) for i in range(4)])]
    ppermute x90 -> x56, waiting for transfers between devices: 63.7 us -> 73.2 us  [swap(): return lax.ppermute(v, 'seq', [(i, i ^ mask) for i in range(4)])]
    ppermute x105 -> x56, waiting for transfers between devices: 185 us -> 179 us  [ring_step(): lax.ppermute(v, 'dp', [(RING[i], RING[(i + step) % 8]) for i in range(8)])]
    dot_general x12 -> x14, matrix products: 27.6 us -> 23 us  [dot_nn(): lax.dot_general(a, b, (((1,), (0,)), ((), ())), preferred_element_type=f32)]
    dot_general x9 -> x13, matrix products: 28.5 us -> 27.1 us  [dot_tn(): lax.dot_general(a, b, (((0,), (0,)), ((), ())), preferred_element_type=f32)]
  transfers between devices with their start and end apart: 195 -> 114, of which waited for: 89 -> 48; matrix products, arithmetic and copies ran while one was open for 9% -> 21% of each run, Pallas kernels for 51% -> 11%
where the time goes in v2:
time: 648 us; the launch traced here: 638 us
  waiting for transfers between devices  253 us (39%)
  starting transfers between devices  86.9 us (13%)
  matrix products  78.4 us (12%)
  Pallas kernels  71.4 us (11%)
  local copies, waits for them, and re-layouts  54.4 us (8%)
  other arithmetic  53.6 us (8%)
  between operations  40.6 us (6%)
    ppermute x56, waiting for transfers between devices, ring_step(): lax.ppermute(v, 'dp', [(RING[i], RING[(i + step) % 8]) for i in range(8)])  179 us
    ppermute x56, waiting for transfers between devices, swap(): return lax.ppermute(v, 'seq', [(i, i ^ mask) for i in range(4)])  73.2 us
    ppermute x56, starting transfers between devices, ring_step(): lax.ppermute(v, 'dp', [(RING[i], RING[(i + step) % 8]) for i in range(8)])  62.2 us
    unnamed x291, local copies, waits for them, and re-layouts  39.3 us
    pallas_call x1, Pallas kernels, attend_back(): pl.pallas_call(functools.partial(attend_back_kernel, pieces, block, scale...  35 us
    dot_general x11, matrix products, dot_nt(): lax.dot_general(a, b, (((1,), (1,)), ((), ())), preferred_element_type=f32)  28.3 us
    dot_general x13, matrix products, dot_tn(): lax.dot_general(a, b, (((0,), (0,)), ((), ())), preferred_element_type=f32)  27.1 us
    ppermute x56, starting transfers between devices, swap(): return lax.ppermute(v, 'seq', [(i, i ^ mask) for i in range(4)])  24.6 us
  transfers between devices with their start and end apart: 114, of which 48 were waited for; matrix products, arithmetic and copies ran while one was open for 21% of the time, Pallas kernels for 11%

profile of v2, /device:TPU:0, one launch (start us, length us, event | category | flops | bytes accessed | tf_op | source)
XLA Modules:
  0.0 637.9 jit_solution(12065579859859254439)
XLA Ops:
  18.9 2.4 collective-permute-start.31
  22.0 5.7 collective-permute-done.31
  27.7 5.4 collective-permute-done.32
  40.6 4.5 collective-permute-done.45
  50.1 15.4 %collective-permute-done.17.refs_30_ = bf16[128,1024]{1,0:T(8,128)(2,1)S(1)} collective-permute-done((bf16[128,1024]{1,0:T(8,128)(2,1)S(1)}, bf16[128,1024]{1,0:T(8,128)(2,1)S(1)}, u32[]{:S(2)}, u32[]{:S(2)}) %collective-permute-start.17) | collective-permute-done | bytes 262176 | tf_op jit(solution)/shard_map/ppermute | solution.py:299
  66.0 5.3 collective-permute-done.7.refs_8_
  71.3 6.6 %collective-permute-start.18 = (bf16[128,1024]{1,0:T(8,128)(2,1)S(1)}, bf16[128,1024]{1,0:T(8,128)(2,1)}, u32[]{:S(2)}, u32[]{:S(2)}) collective-permute-start(bf16[128,1024]{1,0:T(8,128)(2,1)S(1)} %collective-permute-done.17.refs_30_), channel_id=1, source_target_pairs={{0,4},{8,0},{16,8},{24,16},{28,24},{20,28},{12,20},{4,12},{1,5},{9... | collective-permute-start | bytes 786440 | tf_op jit(solution)/shard_map/ppermute | solution.py:299
  78.8 7.2 %collective-permute-done.18.refs_26_ = bf16[128,1024]{1,0:T(8,128)(2,1)} collective-permute-done((bf16[128,1024]{1,0:T(8,128)(2,1)S(1)}, bf16[128,1024]{1,0:T(8,128)(2,1)}, u32[]{:S(2)}, u32[]{:S(2)}) %collective-permute-start.18) | collective-permute-done | bytes 262176 | tf_op jit(solution)/shard_map/ppermute | solution.py:299
  86.1 2.6 collective-permute-start.24
  90.0 2.9 collective-permute-start.19
  94.2 5.6 collective-permute-done.11.refs_12_
  99.8 7.9 %collective-permute-done.24.refs_20_ = bf16[128,1024]{1,0:T(8,128)(2,1)} collective-permute-done((bf16[128,1024]{1,0:T(8,128)(2,1)S(1)}, bf16[128,1024]{1,0:T(8,128)(2,1)}, u32[]{:S(2)}, u32[]{:S(2)}) %collective-permute-start.24) | collective-permute-done | bytes 262176 | tf_op jit(solution)/shard_map/ppermute | solution.py:299
  107.9 17.5 %collective-permute-done.19.refs_22_ = bf16[128,1024]{1,0:T(8,128)(2,1)} collective-permute-done((bf16[128,1024]{1,0:T(8,128)(2,1)}, bf16[128,1024]{1,0:T(8,128)(2,1)}, u32[]{:S(2)}, u32[]{:S(2)}) %collective-permute-start.19) | collective-permute-done | bytes 262176 | tf_op jit(solution)/shard_map/ppermute | solution.py:299
  128.8 6.2 collective-permute-done.20.refs_18_
  135.0 4.4 fusion.101
  144.2 4.1 collective-permute-done.34.refs_1_
  152.3 8.9 %assemble.3 = (bf16[2048,1024]{1,0:T(8,128)(2,1)S(1)}, bf16[1024,2048]{1,0:T(8,128)(2,1)}) custom-call(s32[9]{0:T(128)S(1)} %pad_add_fusion.6.index_ref, bf16[128,1024]{1,0:T(8,128)(2,1)S(1)} %pad_maximum_fusion.22.refs_0_, bf16[128,1024]{1,0:T(8,128)(2,1)S(1)} %collective-permute-done.refs_1_, bf16[128,1024]{1,0:T(8,128)(2,1)S(1)} %collective-permute-done.1.refs_2_, ...), custom_call_target="tpu_custom_call" | custom-call | tf_op jit(solution)/shard_map/assemble/pallas_call | solution.py:356
  165.7 3.5 fusion.129
  169.3 2.4 fusion.48
  175.7 4.6 collective-permute-done.36.refs_3_
  180.9 2.5 pad_maximum_fusion.14
  183.4 3.2 collective-permute-done.37.refs_4_
  188.6 2.7 assemble.4
  194.9 7.1 %collective-permute-done.52.refs_2_ = bf16[128,1024]{1,0:T(8,128)(2,1)S(1)} collective-permute-done((bf16[128,1024]{1,0:T(8,128)(2,1)S(1)}, bf16[128,1024]{1,0:T(8,128)(2,1)S(1)}, u32[]{:S(2)}, u32[]{:S(2)}) %collective-permute-start.52) | collective-permute-done | bytes 262176 | tf_op jit(solution)/shard_map/ppermute | solution.py:299
  206.9 22.8 %attend.1 = (bf16[1536,256]{1,0:T(8,128)(2,1)S(1)}, f32[1536,256]{1,0:T(8,128)}, bf16[1536,256]{1,0:T(8,128)(2,1)S(1)}, bf16[1536,256]{1,0:T(8,128)(2,1)S(1)}) custom-call(bf16[384,768]{1,0:T(8,128)(2,1)S(1)} %convolution_convert_fusion.13.refs_0_.refs_4_, bf16[384,768]{1,0:T(8,128)(2,1)S(1)} %convolution_convert_fusion.12.refs_1_.refs_5_, ...), custom_call_target="tpu_custom_call" | custom-call | flops 4831838208 | bytes 6291456 | tf_op jit(solution)/shard_map/attend/pallas_call | solution.py:139
  233.6 3.6 collective-permute-done.47
  237.8 3.5 collective-permute-done.48
  261.3 4.5 collective-permute-done.65.refs_10_
  303.8 3.2 fusion.72
  307.0 4.6 fusion.8
  318.5 3.7 fusion.13
  327.8 3.3 fusion.70
  333.8 17.3 %collective-permute-done.73 = bf16[384,1024]{1,0:T(8,128)(2,1)S(1)} collective-permute-done((bf16[384,1024]{1,0:T(8,128)(2,1)S(1)}, bf16[384,1024]{1,0:T(8,128)(2,1)S(1)}, u32[]{:S(2)}, u32[]{:S(2)}) %collective-permute-start.73) | collective-permute-done | bytes 786464 | tf_op jit(solution)/shard_map/ppermute | solution.py:269
  352.9 3.2 fusion.71
  362.3 2.4 pad_maximum_fusion.1
  364.7 6.5 %copy.51 = bf16[1024,2048]{1,0:T(8,128)(2,1)} copy(bf16[1024,2048]{0,1:T(8,128)(2,1)} %pad_maximum_fusion.1) | data formatting | bytes 8388608 | tf_op jit(solution)/shard_map/reshape | solution.py:402
  371.3 8.6 %collective-permute-done.76 = bf16[384,1024]{1,0:T(8,128)(2,1)} collective-permute-done((bf16[384,1024]{1,0:T(8,128)(2,1)}, bf16[384,1024]{1,0:T(8,128)(2,1)}, u32[]{:S(2)}, u32[]{:S(2)}) %collective-permute-start.76) | collective-permute-done | bytes 786464 | tf_op jit(solution)/shard_map/ppermute | solution.py:269
  379.9 5.3 fusion.42
  385.3 3.7 convolution_convert_fusion.1
  399.3 2.6 pad_maximum_fusion.2
  402.2 3.0 collective-permute-done.78.refs_2_
  405.1 3.4 collective-permute-done.79.refs_3_
  409.2 35.0 %attend_back.1 = bf16[1536,768]{1,0:T(8,128)(2,1)} custom-call(bf16[384,256]{1,0:T(8,128)(2,1)} %get-tuple-element.133.refs_0_, bf16[384,256]{1,0:T(8,128)(2,1)} %copy-done.117, bf16[384,256]{1,0:T(8,128)(2,1)} %copy-done.118, bf16[384,256]{1,0:T(8,128)(2,1)} %copy-done.119, bf16[384,768]{1,0:T(8,128)(2,1)} %copy-done.35, bf16[384,768]{1,0:T(8,128)(2,1)} %copy-done.37, ...), custom_call_target="tpu_custom_call" | custom-call | flops 12079595520 | bytes 12582912 | tf_op jit(solution)/shard_map/attend_back/pallas_call | solution.py:239
  444.3 4.5 fusion.157
  448.9 2.7 fusion.30
  454.1 7.2 %collective-permute-done.83 = bf16[128,768]{1,0:T(8,128)(2,1)S(1)} collective-permute-done((bf16[128,768]{1,0:T(8,128)(2,1)S(1)}, bf16[128,768]{1,0:T(8,128)(2,1)S(1)}, u32[]{:S(2)}, u32[]{:S(2)}) %collective-permute-start.83) | collective-permute-done | bytes 196640 | tf_op jit(solution)/shard_map/ppermute | solution.py:299
  463.0 5.2 collective-permute-done.84
  477.9 2.7 collective-permute-done.86
  482.3 6.7 %collective-permute-done.82 = bf16[384,1024]{1,0:T(8,128)(2,1)S(1)} collective-permute-done((bf16[384,1024]{1,0:T(8,128)(2,1)S(1)}, bf16[384,1024]{1,0:T(8,128)(2,1)S(1)}, u32[]{:S(2)}, u32[]{:S(2)}) %collective-permute-start.82) | collective-permute-done | bytes 786464 | tf_op jit(solution)/shard_map/ppermute | solution.py:269
  500.8 3.4 fusion.40
  504.2 3.1 add_convert_fusion
  513.2 7.3 %collective-permute-done.102 = bf16[128,2048]{1,0:T(8,128)(2,1)S(1)} collective-permute-done((bf16[128,2048]{1,0:T(8,128)(2,1)S(1)}, bf16[128,2048]{1,0:T(8,128)(2,1)S(1)}, u32[]{:S(2)}, u32[]{:S(2)}) %collective-permute-start.102) | collective-permute-done | bytes 524320 | tf_op jit(solution)/shard_map/ppermute | solution.py:299
  523.7 2.8 convolution_convert_fusion.5
  526.5 6.5 %collective-permute-done.103 = bf16[128,2048]{1,0:T(8,128)(2,1)S(1)} collective-permute-done((bf16[128,2048]{1,0:T(8,128)(2,1)S(1)}, bf16[128,2048]{1,0:T(8,128)(2,1)S(1)}, u32[]{:S(2)}, u32[]{:S(2)}) %collective-permute-start.103) | collective-permute-done | bytes 524320 | tf_op jit(solution)/shard_map/ppermute | solution.py:299
  538.6 7.1 %collective-permute-done.104 = bf16[128,2048]{1,0:T(8,128)(2,1)S(1)} collective-permute-done((bf16[128,2048]{1,0:T(8,128)(2,1)}, bf16[128,2048]{1,0:T(8,128)(2,1)S(1)}, u32[]{:S(2)}, u32[]{:S(2)}) %collective-permute-start.104) | collective-permute-done | bytes 524320 | tf_op jit(solution)/shard_map/ppermute | solution.py:299
  550.6 3.1 add_convert_fusion.1
  553.6 4.9 collective-permute-done.105
  565.6 3.0 collective-permute-done.110
  570.3 7.0 %collective-permute-done.91 = bf16[128,2048]{1,0:T(8,128)(2,1)S(1)} collective-permute-done((bf16[128,2048]{1,0:T(8,128)(2,1)S(1)}, bf16[128,2048]{1,0:T(8,128)(2,1)S(1)}, u32[]{:S(2)}, u32[]{:S(2)}) %collective-permute-start.91) | collective-permute-done | bytes 524320 | tf_op jit(solution)/shard_map/ppermute | solution.py:299
  578.4 12.2 %collective-permute-done.92 = bf16[128,2048]{1,0:T(8,128)(2,1)S(1)} collective-permute-done((bf16[128,2048]{1,0:T(8,128)(2,1)S(1)}, bf16[128,2048]{1,0:T(8,128)(2,1)S(1)}, u32[]{:S(2)}, u32[]{:S(2)}) %collective-permute-start.92) | collective-permute-done | bytes 524320 | tf_op jit(solution)/shard_map/ppermute | solution.py:299
  593.0 10.0 %collective-permute-done.93 = bf16[128,2048]{1,0:T(8,128)(2,1)S(1)} collective-permute-done((bf16[128,2048]{1,0:T(8,128)(2,1)S(1)}, bf16[128,2048]{1,0:T(8,128)(2,1)S(1)}, u32[]{:S(2)}, u32[]{:S(2)}) %collective-permute-start.93) | collective-permute-done | bytes 524320 | tf_op jit(solution)/shard_map/ppermute | solution.py:299
  606.1 8.8 %collective-permute-done.94 = bf16[128,2048]{1,0:T(8,128)(2,1)S(1)} collective-permute-done((bf16[128,2048]{1,0:T(8,128)(2,1)S(1)}, bf16[128,2048]{1,0:T(8,128)(2,1)S(1)}, u32[]{:S(2)}, u32[]{:S(2)}) %collective-permute-start.94) | collective-permute-done | bytes 524320 | tf_op jit(solution)/shard_map/ppermute | solution.py:299
  619.8 4.0 collective-permute-done.99
  623.8 3.0 collective-permute-done.98
  (613 shorter events, 203.3 us)
Async XLA Ops:
  7.2 162.0 %all-gather.2.cloned.1.call-start = ((), (), s32[]{:S(2)}) async-start(), calls=%async_computation.1 | async-start | bytes 4718592 | tf_op jit(solution)/shard_map/all_gather | solution.py:506
  21.3 11.8 %collective-permute-start.32 = (bf16[32,3840]{1,0:T(8,128)(2,1)S(1)}, bf16[32,3840]{1,0:T(8,128)(2,1)S(1)}, u32[]{:S(2)}, u32[]{:S(2)}) collective-permute-start(bf16[32,3840]{1,0:T(8,128)(2,1)S(1)} %get-tuple-element.128), channel_id=1, source_target_pairs={{0,2},{1,3},{2,0},{3,1},{4,6},{5,7},{6,4},{7,5},{8,10},{9,11},{10,... | collective-permute-start | bytes 737288 | tf_op jit(solution)/shard_map/ppermute | solution.py:269
  35.1 501.4 %reduce-scatter.2.cloned.1.call-start = ((), (), s32[]{:S(2)}) async-start(), calls=%async_computation.2 | async-start | bytes 4718592 | tf_op jit(solution)/shard_map/reduce_scatter | solution.py:613
  45.6 19.9 %collective-permute-start.17 = (bf16[128,1024]{1,0:T(8,128)(2,1)S(1)}, bf16[128,1024]{1,0:T(8,128)(2,1)S(1)}, u32[]{:S(2)}, u32[]{:S(2)}) collective-permute-start(bf16[128,1024]{1,0:T(8,128)(2,1)S(1)} %collective-permute-done.1.refs_2_), channel_id=1, source_target_pairs={{0,4},{8,0},{16,8},{24,16},{28,24},{20,28},{12,20},{4,12},{1,5},{9... | collective-permute-start | bytes 786440 | tf_op jit(solution)/shard_map/ppermute | solution.py:299
  47.4 18.1 %collective-permute-start.5 = (bf16[128,1024]{1,0:T(8,128)(2,1)S(1)}, bf16[128,1024]{1,0:T(8,128)(2,1)S(1)}, u32[]{:S(2)}, u32[]{:S(2)}) collective-permute-start(bf16[128,1024]{1,0:T(8,128)(2,1)S(1)} %collective-permute-done.1.refs_2_), channel_id=1, source_target_pairs={{0,8},{8,16},{16,24},{24,28},{28,20},{20,12},{12,4},{4,0},{1,9},{9... | collective-permute-start | bytes 786440 | tf_op jit(solution)/shard_map/ppermute | solution.py:299
  48.1 23.2 %collective-permute-start.7 = (bf16[128,1024]{1,0:T(8,128)(2,1)S(1)}, bf16[128,1024]{1,0:T(8,128)(2,1)S(1)}, u32[]{:S(2)}, u32[]{:S(2)}) collective-permute-start(bf16[128,1024]{1,0:T(8,128)(2,1)S(1)} %collective-permute-done.3.refs_4_), channel_id=1, source_target_pairs={{0,8},{8,16},{16,24},{24,28},{28,20},{20,12},{12,4},{4,0},{1,9},{9... | collective-permute-start | bytes 786440 | tf_op jit(solution)/shard_map/ppermute | solution.py:299
  49.7 28.3 %collective-permute-start.23 = (bf16[128,1024]{1,0:T(8,128)(2,1)S(1)}, bf16[128,1024]{1,0:T(8,128)(2,1)S(1)}, u32[]{:S(2)}, u32[]{:S(2)}) collective-permute-start(bf16[128,1024]{1,0:T(8,128)(2,1)S(1)} %collective-permute-done.22.refs_28_), channel_id=1, source_target_pairs={{0,4},{8,0},{16,8},{24,16},{28,24},{20,28},{12,20},{4,12},{1,5},{9... | collective-permute-start | bytes 786440 | tf_op jit(solution)/shard_map/ppermute | solution.py:299
  50.1 27.8 %collective-permute-start.2 = (bf16[128,1024]{1,0:T(8,128)(2,1)S(1)}, bf16[128,1024]{1,0:T(8,128)(2,1)S(1)}, u32[]{:S(2)}, u32[]{:S(2)}) collective-permute-start(bf16[128,1024]{1,0:T(8,128)(2,1)S(1)} %collective-permute-done.1.refs_2_), channel_id=1, source_target_pairs={{0,1},{1,0},{2,3},{3,2},{4,5},{5,4},{6,7},{7,6},{8,9},{9,8},{10,11... | collective-permute-start | bytes 786440 | tf_op jit(solution)/shard_map/ppermute | solution.py:269
  65.5 12.5 %collective-permute-start.29 = (bf16[128,1024]{1,0:T(8,128)(2,1)S(1)}, bf16[128,1024]{1,0:T(8,128)(2,1)S(1)}, u32[]{:S(2)}, u32[]{:S(2)}) collective-permute-start(bf16[128,1024]{1,0:T(8,128)(2,1)S(1)} %collective-permute-done.22.refs_28_), channel_id=1, source_target_pairs={{0,1},{1,0},{2,3},{3,2},{4,5},{5,4},{6,7},{7,6},{8,9},{9,8},{10,11... | collective-permute-start | bytes 786440 | tf_op jit(solution)/shard_map/ppermute | solution.py:269
  65.5 13.0 %collective-permute-start.4 = (bf16[128,1024]{1,0:T(8,128)(2,1)S(1)}, bf16[128,1024]{1,0:T(8,128)(2,1)S(1)}, u32[]{:S(2)}, u32[]{:S(2)}) collective-permute-start(bf16[128,1024]{1,0:T(8,128)(2,1)S(1)} %collective-permute-done.3.refs_4_), channel_id=1, source_target_pairs={{0,1},{1,0},{2,3},{3,2},{4,5},{5,4},{6,7},{7,6},{8,9},{9,8},{10,11... | collective-permute-start | bytes 786440 | tf_op jit(solution)/shard_map/ppermute | solution.py:269
  71.3 14.7 %collective-permute-start.18 = (bf16[128,1024]{1,0:T(8,128)(2,1)S(1)}, bf16[128,1024]{1,0:T(8,128)(2,1)}, u32[]{:S(2)}, u32[]{:S(2)}) collective-permute-start(bf16[128,1024]{1,0:T(8,128)(2,1)S(1)} %collective-permute-done.17.refs_30_), channel_id=1, source_target_pairs={{0,4},{8,0},{16,8},{24,16},{28,24},{20,28},{12,20},{4,12},{1,5},{9... | collective-permute-start | bytes 786440 | tf_op jit(solution)/shard_map/ppermute | solution.py:299
  77.9 12.0 %collective-permute-start.9 = (bf16[128,1024]{1,0:T(8,128)(2,1)S(1)}, bf16[128,1024]{1,0:T(8,128)(2,1)}, u32[]{:S(2)}, u32[]{:S(2)}) collective-permute-start(bf16[128,1024]{1,0:T(8,128)(2,1)S(1)} %collective-permute-done.5.refs_6_), channel_id=1, source_target_pairs={{0,8},{8,16},{16,24},{24,28},{28,20},{20,12},{12,4},{4,0},{1,9},{9... | collective-permute-start | bytes 786440 | tf_op jit(solution)/shard_map/ppermute | solution.py:299
  78.0 29.8 %collective-permute-start.30 = (bf16[128,1024]{1,0:T(8,128)(2,1)S(1)}, bf16[128,1024]{1,0:T(8,128)(2,1)S(1)}, u32[]{:S(2)}, u32[]{:S(2)}) collective-permute-start(bf16[128,1024]{1,0:T(8,128)(2,1)S(1)} %collective-permute-done.17.refs_30_), channel_id=1, source_target_pairs={{0,1},{1,0},{2,3},{3,2},{4,5},{5,4},{6,7},{7,6},{8,9},{9,8},{10,11... | collective-permute-start | bytes 786440 | tf_op jit(solution)/shard_map/ppermute | solution.py:269
  78.0 29.8 %collective-permute-start.6 = (bf16[128,1024]{1,0:T(8,128)(2,1)S(1)}, bf16[128,1024]{1,0:T(8,128)(2,1)}, u32[]{:S(2)}, u32[]{:S(2)}) collective-permute-start(bf16[128,1024]{1,0:T(8,128)(2,1)S(1)} %collective-permute-done.5.refs_6_), channel_id=1, source_target_pairs={{0,1},{1,0},{2,3},{3,2},{4,5},{5,4},{6,7},{7,6},{8,9},{9,8},{10,11... | collective-permute-start | bytes 786440 | tf_op jit(solution)/shard_map/ppermute | solution.py:269
  78.5 21.2 %collective-permute-start.11 = (bf16[128,1024]{1,0:T(8,128)(2,1)S(1)}, bf16[128,1024]{1,0:T(8,128)(2,1)}, u32[]{:S(2)}, u32[]{:S(2)}) collective-permute-start(bf16[128,1024]{1,0:T(8,128)(2,1)S(1)} %collective-permute-done.7.refs_8_), channel_id=1, source_target_pairs={{0,8},{8,16},{16,24},{24,28},{28,20},{20,12},{12,4},{4,0},{1,9},{9... | collective-permute-start | bytes 786440 | tf_op jit(solution)/shard_map/ppermute | solution.py:299
  86.1 21.6 %collective-permute-start.24 = (bf16[128,1024]{1,0:T(8,128)(2,1)S(1)}, bf16[128,1024]{1,0:T(8,128)(2,1)}, u32[]{:S(2)}, u32[]{:S(2)}) collective-permute-start(bf16[128,1024]{1,0:T(8,128)(2,1)S(1)} %collective-permute-done.23.refs_24_), channel_id=1, source_target_pairs={{0,4},{8,0},{16,8},{24,16},{28,24},{20,28},{12,20},{4,12},{1,5},{9... | collective-permute-start | bytes 786440 | tf_op jit(solution)/shard_map/ppermute | solution.py:299
  90.0 35.4 %collective-permute-start.19 = (bf16[128,1024]{1,0:T(8,128)(2,1)}, bf16[128,1024]{1,0:T(8,128)(2,1)}, u32[]{:S(2)}, u32[]{:S(2)}) collective-permute-start(bf16[128,1024]{1,0:T(8,128)(2,1)} %collective-permute-done.18.refs_26_), channel_id=1, source_target_pairs={{0,4},{8,0},{16,8},{24,16},{28,24},{20,28},{12,20},{4,12},{1,5},{9... | collective-permute-start | bytes 786440 | tf_op jit(solution)/shard_map/ppermute | solution.py:299
  99.8 26.4 %collective-permute-start.27 = (bf16[128,1024]{1,0:T(8,128)(2,1)S(1)}, bf16[128,1024]{1,0:T(8,128)(2,1)}, u32[]{:S(2)}, u32[]{:S(2)}) collective-permute-start(bf16[128,1024]{1,0:T(8,128)(2,1)S(1)} %collective-permute-done.23.refs_24_), channel_id=1, source_target_pairs={{0,1},{1,0},{2,3},{3,2},{4,5},{5,4},{6,7},{7,6},{8,9},{9,8},{10,11... | collective-permute-start | bytes 786440 | tf_op jit(solution)/shard_map/ppermute | solution.py:269
  107.7 18.6 %collective-permute-start.8 = (bf16[128,1024]{1,0:T(8,128)(2,1)S(1)}, bf16[128,1024]{1,0:T(8,128)(2,1)}, u32[]{:S(2)}, u32[]{:S(2)}) collective-permute-start(bf16[128,1024]{1,0:T(8,128)(2,1)S(1)} %collective-permute-done.7.refs_8_), channel_id=1, source_target_pairs={{0,1},{1,0},{2,3},{3,2},{4,5},{5,4},{6,7},{7,6},{8,9},{9,8},{10,11... | collective-permute-start | bytes 786440 | tf_op jit(solution)/shard_map/ppermute | solution.py:269
  107.7 19.1 %collective-permute-start.13 = (bf16[128,1024]{1,0:T(8,128)(2,1)}, bf16[128,1024]{1,0:T(8,128)(2,1)}, u32[]{:S(2)}, u32[]{:S(2)}) collective-permute-start(bf16[128,1024]{1,0:T(8,128)(2,1)} %collective-permute-done.9.refs_10_), channel_id=1, source_target_pairs={{0,8},{8,16},{16,24},{24,28},{28,20},{20,12},{12,4},{4,0},{1,9},{9... | collective-permute-start | bytes 786440 | tf_op jit(solution)/shard_map/ppermute | solution.py:299
  107.8 21.0 %collective-permute-start.15 = (bf16[128,1024]{1,0:T(8,128)(2,1)}, bf16[128,1024]{1,0:T(8,128)(2,1)}, u32[]{:S(2)}, u32[]{:S(2)}) collective-permute-start(bf16[128,1024]{1,0:T(8,128)(2,1)} %collective-permute-done.11.refs_12_), channel_id=1, source_target_pairs={{0,8},{8,16},{16,24},{24,28},{28,20},{20,12},{12,4},{4,0},{1,9},{9... | collective-permute-start | bytes 786440 | tf_op jit(solution)/shard_map/ppermute | solution.py:299
  126.2 13.3 %collective-permute-start.10 = (bf16[128,1024]{1,0:T(8,128)(2,1)}, bf16[128,1024]{1,0:T(8,128)(2,1)S(1)}, u32[]{:S(2)}, u32[]{:S(2)}) collective-permute-start(bf16[128,1024]{1,0:T(8,128)(2,1)} %collective-permute-done.9.refs_10_), channel_id=1, source_target_pairs={{0,1},{1,0},{2,3},{3,2},{4,5},{5,4},{6,7},{7,6},{8,9},{9,8},{10,11... | collective-permute-start | bytes 786440 | tf_op jit(solution)/shard_map/ppermute | solution.py:269
  126.3 13.8 %collective-permute-start.28 = (bf16[128,1024]{1,0:T(8,128)(2,1)}, bf16[128,1024]{1,0:T(8,128)(2,1)S(1)}, u32[]{:S(2)}, u32[]{:S(2)}) collective-permute-start(bf16[128,1024]{1,0:T(8,128)(2,1)} %collective-permute-done.18.refs_26_), channel_id=1, source_target_pairs={{0,1},{1,0},{2,3},{3,2},{4,5},{5,4},{6,7},{7,6},{8,9},{9,8},{10,11... | collective-permute-start | bytes 786440 | tf_op jit(solution)/shard_map/ppermute | solution.py:269
  126.8 13.4 %collective-permute-start.12 = (bf16[128,1024]{1,0:T(8,128)(2,1)}, bf16[128,1024]{1,0:T(8,128)(2,1)S(1)}, u32[]{:S(2)}, u32[]{:S(2)}) collective-permute-start(bf16[128,1024]{1,0:T(8,128)(2,1)} %collective-permute-done.11.refs_12_), channel_id=1, source_target_pairs={{0,1},{1,0},{2,3},{3,2},{4,5},{5,4},{6,7},{7,6},{8,9},{9,8},{10,11... | collective-permute-start | bytes 786440 | tf_op jit(solution)/shard_map/ppermute | solution.py:269
  128.8 12.9 %collective-permute-start.25 = (bf16[128,1024]{1,0:T(8,128)(2,1)}, bf16[128,1024]{1,0:T(8,128)(2,1)S(1)}, u32[]{:S(2)}, u32[]{:S(2)}) collective-permute-start(bf16[128,1024]{1,0:T(8,128)(2,1)} %collective-permute-done.24.refs_20_), channel_id=1, source_target_pairs={{0,1},{1,0},{2,3},{3,2},{4,5},{5,4},{6,7},{7,6},{8,9},{9,8},{10,11... | collective-permute-start | bytes 786440 | tf_op jit(solution)/shard_map/ppermute | solution.py:269
  148.3 25.0 %collective-permute-start.35 = (bf16[128,768]{1,0:T(8,128)(2,1)}, bf16[128,768]{1,0:T(8,128)(2,1)}, u32[]{:S(2)}, u32[]{:S(2)}) collective-permute-start(bf16[128,768]{1,0:T(8,128)(2,1)} %collective-permute-done.34.refs_1_), channel_id=1, source_target_pairs={{0,8},{8,16},{16,24},{24,28},{28,20},{20,12},{12,4},{4,0},{1,9},{9... | collective-permute-start | bytes 589832 | tf_op jit(solution)/shard_map/ppermute | solution.py:299
  149.1 24.6 %collective-permute-start.39 = (bf16[128,768]{1,0:T(8,128)(2,1)}, bf16[128,768]{1,0:T(8,128)(2,1)}, u32[]{:S(2)}, u32[]{:S(2)}) collective-permute-start(bf16[128,768]{1,0:T(8,128)(2,1)} %collective-permute-done.38.refs_7_), channel_id=1, source_target_pairs={{0,4},{8,0},{16,8},{24,16},{28,24},{20,28},{12,20},{4,12},{1,5},{9... | collective-permute-start | bytes 589832 | tf_op jit(solution)/shard_map/ppermute | solution.py:299
  169.2 78.8 %collective-permute-start.50 = (bf16[1024,2048]{1,0:T(8,128)(2,1)}, bf16[1024,2048]{1,0:T(8,128)(2,1)S(1)}, u32[]{:S(2)}, u32[]{:S(2)}) collective-permute-start(bf16[1024,2048]{1,0:T(8,128)(2,1)} %all-gather.2.cloned.1.call-done), channel_id=1, source_target_pairs={{0,1},{1,0},{2,3},{3,2},{4,5},{5,4},{6,7},{7,6},{8,9},{9,8},{10,11... | collective-permute-start | bytes 12582920 | tf_op jit(solution)/shard_map/ppermute | solution.py:269
  171.7 19.8 %collective-permute-start.42 = (bf16[384,1024]{1,0:T(8,128)(2,1)S(1)}, bf16[384,1024]{1,0:T(8,128)(2,1)S(1)}, u32[]{:S(2)}, u32[]{:S(2)}) collective-permute-start(bf16[384,1024]{1,0:T(8,128)(2,1)S(1)} %fusion.48), channel_id=1, source_target_pairs={{0,2},{1,3},{2,0},{3,1},{4,6},{5,7},{6,4},{7,5},{8,10},{9,11},{10,... | collective-permute-start | bytes 2359304 | tf_op jit(solution)/shard_map/ppermute | solution.py:269
  173.6 19.7 %collective-permute-start.41 = (bf16[384,1024]{1,0:T(8,128)(2,1)S(1)}, bf16[384,1024]{1,0:T(8,128)(2,1)S(1)}, u32[]{:S(2)}, u32[]{:S(2)}) collective-permute-start(bf16[384,1024]{1,0:T(8,128)(2,1)S(1)} %fusion.48), channel_id=1, source_target_pairs={{0,1},{1,0},{2,3},{3,2},{4,5},{5,4},{6,7},{7,6},{8,9},{9,8},{10,11... | collective-permute-start | bytes 2359304 | tf_op jit(solution)/shard_map/ppermute | solution.py:269
  186.5 17.2 %collective-permute-start.59 = (bf16[128,1024]{1,0:T(8,128)(2,1)S(1)}, bf16[128,1024]{1,0:T(8,128)(2,1)S(1)}, u32[]{:S(2)}, u32[]{:S(2)}) collective-permute-start(bf16[128,1024]{1,0:T(8,128)(2,1)S(1)} %copy-done.3), channel_id=1, source_target_pairs={{0,4},{8,0},{16,8},{24,16},{28,24},{20,28},{12,20},{4,12},{1,5},{9... | collective-permute-start | bytes 786440 | tf_op jit(solution)/shard_map/ppermute | solution.py:299
  188.3 15.7 %collective-permute-start.53 = (bf16[128,1024]{1,0:T(8,128)(2,1)S(1)}, bf16[128,1024]{1,0:T(8,128)(2,1)S(1)}, u32[]{:S(2)}, u32[]{:S(2)}) collective-permute-start(bf16[128,1024]{1,0:T(8,128)(2,1)S(1)} %copy-done.3), channel_id=1, source_target_pairs={{0,8},{8,16},{16,24},{24,28},{28,20},{20,12},{12,4},{4,0},{1,9},{9... | collective-permute-start | bytes 786440 | tf_op jit(solution)/shard_map/ppermute | solution.py:299
  191.6 14.2 %collective-permute-start.43 = (bf16[384,1024]{1,0:T(8,128)(2,1)S(1)}, bf16[384,1024]{1,0:T(8,128)(2,1)S(1)}, u32[]{:S(2)}, u32[]{:S(2)}) collective-permute-start(bf16[384,1024]{1,0:T(8,128)(2,1)S(1)} %collective-permute-done.42), channel_id=1, source_target_pairs={{0,1},{1,0},{2,3},{3,2},{4,5},{5,4},{6,7},{7,6},{8,9},{9,8},{10,11... | collective-permute-start | bytes 2359304 | tf_op jit(solution)/shard_map/ppermute | solution.py:269
  202.0 27.9 %collective-permute-start.63 = (bf16[128,1024]{1,0:T(8,128)(2,1)S(1)}, bf16[128,1024]{1,0:T(8,128)(2,1)S(1)}, u32[]{:S(2)}, u32[]{:S(2)}) collective-permute-start(bf16[128,1024]{1,0:T(8,128)(2,1)S(1)} %pad_maximum_fusion.21.refs_0_), channel_id=1, source_target_pairs={{0,4},{8,0},{16,8},{24,16},{28,24},{20,28},{12,20},{4,12},{1,5},{9... | collective-permute-start | bytes 786440 | tf_op jit(solution)/shard_map/ppermute | solution.py:299
  203.7 26.2 %collective-permute-start.54 = (bf16[128,1024]{1,0:T(8,128)(2,1)S(1)}, bf16[128,1024]{1,0:T(8,128)(2,1)S(1)}, u32[]{:S(2)}, u32[]{:S(2)}) collective-permute-start(bf16[128,1024]{1,0:T(8,128)(2,1)S(1)} %collective-permute-done.52.refs_2_), channel_id=1, source_target_pairs={{0,8},{8,16},{16,24},{24,28},{28,20},{20,12},{12,4},{4,0},{1,9},{9... | collective-permute-start | bytes 786440 | tf_op jit(solution)/shard_map/ppermute | solution.py:299
  204.0 27.5 %collective-permute-start.60 = (bf16[128,1024]{1,0:T(8,128)(2,1)S(1)}, bf16[128,1024]{1,0:T(8,128)(2,1)S(1)}, u32[]{:S(2)}, u32[]{:S(2)}) collective-permute-start(bf16[128,1024]{1,0:T(8,128)(2,1)S(1)} %collective-permute-done.59.refs_15_), channel_id=1, source_target_pairs={{0,4},{8,0},{16,8},{24,16},{28,24},{20,28},{12,20},{4,12},{1,5},{9... | collective-permute-start | bytes 786440 | tf_op jit(solution)/shard_map/ppermute | solution.py:299
  205.8 26.1 %collective-permute-start.55 = (bf16[128,1024]{1,0:T(8,128)(2,1)S(1)}, bf16[128,1024]{1,0:T(8,128)(2,1)S(1)}, u32[]{:S(2)}, u32[]{:S(2)}) collective-permute-start(bf16[128,1024]{1,0:T(8,128)(2,1)S(1)} %collective-permute-done.53.refs_3_), channel_id=1, source_target_pairs={{0,8},{8,16},{16,24},{24,28},{28,20},{20,12},{12,4},{4,0},{1,9},{9... | collective-permute-start | bytes 786440 | tf_op jit(solution)/shard_map/ppermute | solution.py:299
  231.8 23.2 %collective-permute-start.64 = (bf16[128,1024]{1,0:T(8,128)(2,1)S(1)}, bf16[128,1024]{1,0:T(8,128)(2,1)S(1)}, u32[]{:S(2)}, u32[]{:S(2)}) collective-permute-start(bf16[128,1024]{1,0:T(8,128)(2,1)S(1)} %collective-permute-done.63.refs_14_), channel_id=1, source_target_pairs={{0,4},{8,0},{16,8},{24,16},{28,24},{20,28},{12,20},{4,12},{1,5},{9... | collective-permute-start | bytes 786440 | tf_op jit(solution)/shard_map/ppermute | solution.py:299
  237.1 19.9 %collective-permute-start.56 = (bf16[128,1024]{1,0:T(8,128)(2,1)S(1)}, bf16[128,1024]{1,0:T(8,128)(2,1)S(1)}, u32[]{:S(2)}, u32[]{:S(2)}) collective-permute-start(bf16[128,1024]{1,0:T(8,128)(2,1)S(1)} %collective-permute-done.54.refs_4_), channel_id=1, source_target_pairs={{0,8},{8,16},{16,24},{24,28},{28,20},{20,12},{12,4},{4,0},{1,9},{9... | collective-permute-start | bytes 786440 | tf_op jit(solution)/shard_map/ppermute | solution.py:299
  241.4 15.7 %collective-permute-start.61 = (bf16[128,1024]{1,0:T(8,128)(2,1)S(1)}, bf16[128,1024]{1,0:T(8,128)(2,1)}, u32[]{:S(2)}, u32[]{:S(2)}) collective-permute-start(bf16[128,1024]{1,0:T(8,128)(2,1)S(1)} %collective-permute-done.60.refs_13_), channel_id=1, source_target_pairs={{0,4},{8,0},{16,8},{24,16},{28,24},{20,28},{12,20},{4,12},{1,5},{9... | collective-permute-start | bytes 786440 | tf_op jit(solution)/shard_map/ppermute | solution.py:299
  243.1 16.5 %collective-permute-start.57 = (bf16[128,1024]{1,0:T(8,128)(2,1)S(1)}, bf16[128,1024]{1,0:T(8,128)(2,1)S(1)}, u32[]{:S(2)}, u32[]{:S(2)}) collective-permute-start(bf16[128,1024]{1,0:T(8,128)(2,1)S(1)} %collective-permute-done.55.refs_5_), channel_id=1, source_target_pairs={{0,8},{8,16},{16,24},{24,28},{28,20},{20,12},{12,4},{4,0},{1,9},{9... | collective-permute-start | bytes 786440 | tf_op jit(solution)/shard_map/ppermute | solution.py:299
  255.0 48.2 %collective-permute-start.70 = (bf16[384,1024]{1,0:T(8,128)(2,1)}, bf16[384,1024]{1,0:T(8,128)(2,1)}, u32[]{:S(2)}, u32[]{:S(2)}) collective-permute-start(bf16[384,1024]{1,0:T(8,128)(2,1)} %get-tuple-element.101), channel_id=1, source_target_pairs={{0,2},{1,3},{2,0},{3,1},{4,6},{5,7},{6,4},{7,5},{8,10},{9,11},{10,... | collective-permute-start | bytes 2359304 | tf_op jit(solution)/shard_map/ppermute | solution.py:269
  255.0 48.3 %collective-permute-start.66 = (bf16[384,1024]{1,0:T(8,128)(2,1)}, bf16[384,1024]{1,0:T(8,128)(2,1)}, u32[]{:S(2)}, u32[]{:S(2)}) collective-permute-start(bf16[384,1024]{1,0:T(8,128)(2,1)} %get-tuple-element.102), channel_id=1, source_target_pairs={{0,2},{1,3},{2,0},{3,1},{4,6},{5,7},{6,4},{7,5},{8,10},{9,11},{10,... | collective-permute-start | bytes 2359304 | tf_op jit(solution)/shard_map/ppermute | solution.py:269
  257.1 46.7 %collective-permute-start.51 = (bf16[384,1024]{1,0:T(8,128)(2,1)}, bf16[384,1024]{1,0:T(8,128)(2,1)}, u32[]{:S(2)}, u32[]{:S(2)}) collective-permute-start(bf16[384,1024]{1,0:T(8,128)(2,1)} %get-tuple-element.102), channel_id=1, source_target_pairs={{0,1},{1,0},{2,3},{3,2},{4,5},{5,4},{6,7},{7,6},{8,9},{9,8},{10,11... | collective-permute-start | bytes 2359304 | tf_op jit(solution)/shard_map/ppermute | solution.py:269
  266.5 40.5 %collective-permute-start.68 = (bf16[384,1024]{1,0:T(8,128)(2,1)}, bf16[384,1024]{1,0:T(8,128)(2,1)}, u32[]{:S(2)}, u32[]{:S(2)}) collective-permute-start(bf16[384,1024]{1,0:T(8,128)(2,1)} %get-tuple-element.101), channel_id=1, source_target_pairs={{0,1},{1,0},{2,3},{3,2},{4,5},{5,4},{6,7},{7,6},{8,9},{9,8},{10,11... | collective-permute-start | bytes 2359304 | tf_op jit(solution)/shard_map/ppermute | solution.py:269
  269.4 25.2 %collective-permute-start.62 = (bf16[128,1024]{1,0:T(8,128)(2,1)}, bf16[128,1024]{1,0:T(8,128)(2,1)}, u32[]{:S(2)}, u32[]{:S(2)}) collective-permute-start(bf16[128,1024]{1,0:T(8,128)(2,1)} %collective-permute-done.61.refs_11_), channel_id=1, source_target_pairs={{0,4},{8,0},{16,8},{24,16},{28,24},{20,28},{12,20},{4,12},{1,5},{9... | collective-permute-start | bytes 786440 | tf_op jit(solution)/shard_map/ppermute | solution.py:299
  303.2 15.3 %collective-permute-start.71 = (bf16[384,1024]{1,0:T(8,128)(2,1)}, bf16[384,1024]{1,0:T(8,128)(2,1)S(1)}, u32[]{:S(2)}, u32[]{:S(2)}) collective-permute-start(bf16[384,1024]{1,0:T(8,128)(2,1)} %collective-permute-done.70), channel_id=1, source_target_pairs={{0,1},{1,0},{2,3},{3,2},{4,5},{5,4},{6,7},{7,6},{8,9},{9,8},{10,11... | collective-permute-start | bytes 2359304 | tf_op jit(solution)/shard_map/ppermute | solution.py:269
  303.3 13.3 %collective-permute-start.67 = (bf16[384,1024]{1,0:T(8,128)(2,1)}, bf16[384,1024]{1,0:T(8,128)(2,1)S(1)}, u32[]{:S(2)}, u32[]{:S(2)}) collective-permute-start(bf16[384,1024]{1,0:T(8,128)(2,1)} %collective-permute-done.66), channel_id=1, source_target_pairs={{0,1},{1,0},{2,3},{3,2},{4,5},{5,4},{6,7},{7,6},{8,9},{9,8},{10,11... | collective-permute-start | bytes 2359304 | tf_op jit(solution)/shard_map/ppermute | solution.py:269
  331.5 19.6 %collective-permute-start.73 = (bf16[384,1024]{1,0:T(8,128)(2,1)S(1)}, bf16[384,1024]{1,0:T(8,128)(2,1)S(1)}, u32[]{:S(2)}, u32[]{:S(2)}) collective-permute-start(bf16[384,1024]{1,0:T(8,128)(2,1)S(1)} %add_convert_fusion.9), channel_id=1, source_target_pairs={{0,2},{1,3},{2,0},{3,1},{4,6},{5,7},{6,4},{7,5},{8,10},{9,11},{10,... | collective-permute-start | bytes 2359304 | tf_op jit(solution)/shard_map/ppermute | solution.py:269
  358.2 13.1 %collective-permute-start.74 = (bf16[384,1024]{1,0:T(8,128)(2,1)}, bf16[384,1024]{1,0:T(8,128)(2,1)}, u32[]{:S(2)}, u32[]{:S(2)}) collective-permute-start(bf16[384,1024]{1,0:T(8,128)(2,1)} %slice.1074), channel_id=1, source_target_pairs={{0,1},{1,0},{2,3},{3,2},{4,5},{5,4},{6,7},{7,6},{8,9},{9,8},{10,11... | collective-permute-start | bytes 2359304 | tf_op jit(solution)/shard_map/ppermute | solution.py:269
  360.2 19.8 %collective-permute-start.76 = (bf16[384,1024]{1,0:T(8,128)(2,1)}, bf16[384,1024]{1,0:T(8,128)(2,1)}, u32[]{:S(2)}, u32[]{:S(2)}) collective-permute-start(bf16[384,1024]{1,0:T(8,128)(2,1)} %add_convert_fusion.8), channel_id=1, source_target_pairs={{0,2},{1,3},{2,0},{3,1},{4,6},{5,7},{6,4},{7,5},{8,10},{9,11},{10,... | collective-permute-start | bytes 2359304 | tf_op jit(solution)/shard_map/ppermute | solution.py:269
  401.9 102.3 %collective-permute-start.101 = (bf16[1024,2048]{1,0:T(8,128)(2,1)}, bf16[1024,2048]{1,0:T(8,128)(2,1)}, u32[]{:S(2)}, u32[]{:S(2)}) collective-permute-start(bf16[1024,2048]{1,0:T(8,128)(2,1)} %pad_maximum_fusion.2), channel_id=1, source_target_pairs={{0,1},{1,0},{2,3},{3,2},{4,5},{5,4},{6,7},{7,6},{8,9},{9,8},{10,11... | collective-permute-start | bytes 12582920 | tf_op jit(solution)/shard_map/ppermute | solution.py:269
  453.9 16.6 %collective-permute-start.81 = (bf16[384,1024]{1,0:T(8,128)(2,1)S(1)}, bf16[384,1024]{1,0:T(8,128)(2,1)S(1)}, u32[]{:S(2)}, u32[]{:S(2)}) collective-permute-start(bf16[384,1024]{1,0:T(8,128)(2,1)S(1)} %get-tuple-element.100), channel_id=1, source_target_pairs={{0,1},{1,0},{2,3},{3,2},{4,5},{5,4},{6,7},{7,6},{8,9},{9,8},{10,11... | collective-permute-start | bytes 2359304 | tf_op jit(solution)/shard_map/ppermute | solution.py:269
  462.9 19.4 %collective-permute-start.80 = (bf16[384,1024]{1,0:T(8,128)(2,1)S(1)}, bf16[384,1024]{1,0:T(8,128)(2,1)S(1)}, u32[]{:S(2)}, u32[]{:S(2)}) collective-permute-start(bf16[384,1024]{1,0:T(8,128)(2,1)S(1)} %get-tuple-element.99), channel_id=1, source_target_pairs={{0,1},{1,0},{2,3},{3,2},{4,5},{5,4},{6,7},{7,6},{8,9},{9,8},{10,11... | collective-permute-start | bytes 2359304 | tf_op jit(solution)/shard_map/ppermute | solution.py:269
  470.8 18.2 %collective-permute-start.82 = (bf16[384,1024]{1,0:T(8,128)(2,1)S(1)}, bf16[384,1024]{1,0:T(8,128)(2,1)S(1)}, u32[]{:S(2)}, u32[]{:S(2)}) collective-permute-start(bf16[384,1024]{1,0:T(8,128)(2,1)S(1)} %add_convert_fusion.5), channel_id=1, source_target_pairs={{0,2},{1,3},{2,0},{3,1},{4,6},{5,7},{6,4},{7,5},{8,10},{9,11},{10,... | collective-permute-start | bytes 2359304 | tf_op jit(solution)/shard_map/ppermute | solution.py:269
  499.5 51.1 %collective-permute-start.90 = (bf16[8,128,2048]{2,1,0:T(8,128)(2,1)}, bf16[8,128,2048]{2,1,0:T(8,128)(2,1)}, u32[]{:S(2)}, u32[]{:S(2)}) collective-permute-start(bf16[8,128,2048]{2,1,0:T(8,128)(2,1)} %pad_maximum_fusion), channel_id=1, source_target_pairs={{0,1},{1,0},{2,3},{3,2},{4,5},{5,4},{6,7},{7,6},{8,9},{9,8},{10,11... | collective-permute-start | bytes 12582920 | tf_op jit(solution)/shard_map/ppermute | solution.py:269
  507.4 13.1 %collective-permute-start.102 = (bf16[128,2048]{1,0:T(8,128)(2,1)S(1)}, bf16[128,2048]{1,0:T(8,128)(2,1)S(1)}, u32[]{:S(2)}, u32[]{:S(2)}) collective-permute-start(bf16[128,2048]{1,0:T(8,128)(2,1)S(1)} %get-tuple-element.83), channel_id=1, source_target_pairs={{0,8},{8,16},{16,24},{24,28},{28,20},{20,12},{12,4},{4,0},{1,9},{9... | collective-permute-start | bytes 1572872 | tf_op jit(solution)/shard_map/ppermute | solution.py:299
  512.7 13.8 %collective-permute-start.106 = (bf16[128,2048]{1,0:T(8,128)(2,1)S(1)}, bf16[128,2048]{1,0:T(8,128)(2,1)S(1)}, u32[]{:S(2)}, u32[]{:S(2)}) collective-permute-start(bf16[128,2048]{1,0:T(8,128)(2,1)S(1)} %get-tuple-element.84), channel_id=1, source_target_pairs={{0,4},{8,0},{16,8},{24,16},{28,24},{20,28},{12,20},{4,12},{1,5},{9... | collective-permute-start | bytes 1572872 | tf_op jit(solution)/shard_map/ppermute | solution.py:299
  520.6 12.4 %collective-permute-start.103 = (bf16[128,2048]{1,0:T(8,128)(2,1)S(1)}, bf16[128,2048]{1,0:T(8,128)(2,1)S(1)}, u32[]{:S(2)}, u32[]{:S(2)}) collective-permute-start(bf16[128,2048]{1,0:T(8,128)(2,1)S(1)} %fusion.60), channel_id=1, source_target_pairs={{0,8},{8,16},{16,24},{24,28},{28,20},{20,12},{12,4},{4,0},{1,9},{9... | collective-permute-start | bytes 1572872 | tf_op jit(solution)/shard_map/ppermute | solution.py:299
  563.5 13.9 %collective-permute-start.91 = (bf16[128,2048]{1,0:T(8,128)(2,1)S(1)}, bf16[128,2048]{1,0:T(8,128)(2,1)S(1)}, u32[]{:S(2)}, u32[]{:S(2)}) collective-permute-start(bf16[128,2048]{1,0:T(8,128)(2,1)S(1)} %get-tuple-element.89), channel_id=1, source_target_pairs={{0,8},{8,16},{16,24},{24,28},{28,20},{20,12},{12,4},{4,0},{1,9},{9... | collective-permute-start | bytes 1572872 | tf_op jit(solution)/shard_map/ppermute | solution.py:299
  564.3 14.1 %collective-permute-start.95 = (bf16[128,2048]{1,0:T(8,128)(2,1)S(1)}, bf16[128,2048]{1,0:T(8,128)(2,1)S(1)}, u32[]{:S(2)}, u32[]{:S(2)}) collective-permute-start(bf16[128,2048]{1,0:T(8,128)(2,1)S(1)} %get-tuple-element.90), channel_id=1, source_target_pairs={{0,4},{8,0},{16,8},{24,16},{28,24},{20,28},{12,20},{4,12},{1,5},{9... | collective-permute-start | bytes 1572872 | tf_op jit(solution)/shard_map/ppermute | solution.py:299
  577.5 13.0 %collective-permute-start.92 = (bf16[128,2048]{1,0:T(8,128)(2,1)S(1)}, bf16[128,2048]{1,0:T(8,128)(2,1)S(1)}, u32[]{:S(2)}, u32[]{:S(2)}) collective-permute-start(bf16[128,2048]{1,0:T(8,128)(2,1)S(1)} %fusion.67), channel_id=1, source_target_pairs={{0,8},{8,16},{16,24},{24,28},{28,20},{20,12},{12,4},{4,0},{1,9},{9... | collective-permute-start | bytes 1572872 | tf_op jit(solution)/shard_map/ppermute | solution.py:299
  590.9 12.1 %collective-permute-start.93 = (bf16[128,2048]{1,0:T(8,128)(2,1)S(1)}, bf16[128,2048]{1,0:T(8,128)(2,1)S(1)}, u32[]{:S(2)}, u32[]{:S(2)}) collective-permute-start(bf16[128,2048]{1,0:T(8,128)(2,1)S(1)} %get-tuple-element.87), channel_id=1, source_target_pairs={{0,8},{8,16},{16,24},{24,28},{28,20},{20,12},{12,4},{4,0},{1,9},{9... | collective-permute-start | bytes 1572872 | tf_op jit(solution)/shard_map/ppermute | solution.py:299
  591.8 11.8 %collective-permute-start.96 = (bf16[128,2048]{1,0:T(8,128)(2,1)S(1)}, bf16[128,2048]{1,0:T(8,128)(2,1)S(1)}, u32[]{:S(2)}, u32[]{:S(2)}) collective-permute-start(bf16[128,2048]{1,0:T(8,128)(2,1)S(1)} %get-tuple-element.88), channel_id=1, source_target_pairs={{0,4},{8,0},{16,8},{24,16},{28,24},{20,28},{12,20},{4,12},{1,5},{9... | collective-permute-start | bytes 1572872 | tf_op jit(solution)/shard_map/ppermute | solution.py:299
  (172 other events, 1651.4 us)
Sparse Core Ops, SparseCore 0:
  35.2 99.2 all-gather.1
  371.4 87.5 reduce-scatter.1

commit v3 on v2

v3 whole, which is shorter than its diff:
```python
import functools

import jax
import jax.numpy as jnp
from jax import lax
from jax.experimental import pallas as pl
from jax.experimental.pallas import tpu as pltpu
from jax.sharding import PartitionSpec as P

HD = 64
NEG = 1e30
norm_eps = 1e-06
gelu_coef = 0.7978845608028654
f32, bf16 = jnp.float32, jnp.bfloat16

RING = (0, 2, 4, 6, 7, 5, 3, 1)
PLACE = tuple(RING.index(d) for d in range(8))


def dot_nt(a, b):
    return lax.dot_general(a, b, (((1,), (1,)), ((), ())), preferred_element_type=f32)


def dot_nn(a, b):
    return lax.dot_general(a, b, (((1,), (0,)), ((), ())), preferred_element_type=f32)


def dot_tn(a, b):
    return lax.dot_general(a, b, (((0,), (0,)), ((), ())), preferred_element_type=f32)


def silu_slope(v):
    sig = jax.nn.sigmoid(v)
    return sig * (1.0 + v * (1.0 - sig))


def gelu_value(u):
    return 0.5 * u * (1.0 + jnp.tanh(gelu_coef * (u + 0.044715 * u * u * u)))


def gelu_slope(u):
    inner = jnp.tanh(gelu_coef * (u + 0.044715 * u * u * u))
    return 0.5 * (1.0 + inner) + 0.5 * u * (1.0 - inner * inner) * gelu_coef * (
        1.0 + 3.0 * 0.044715 * u * u
    )


def norm_rows(v):
    mean = jnp.mean(v, axis=-1, keepdims=True)
    centred = v - mean
    inverse = lax.rsqrt(jnp.mean(centred * centred, axis=-1, keepdims=True) + norm_eps)
    return (centred * inverse, inverse)


def norm_back(grad, normed, inverse):
    return inverse * (
        grad
        - jnp.mean(grad, axis=-1, keepdims=True)
        - normed * jnp.mean(grad * normed, axis=-1, keepdims=True)
    )

def lanes_of(shape):
    return lax.broadcasted_iota(jnp.int32, shape, 1)


def swap_halves(v):
    lane = lanes_of(v.shape)
    return jnp.where(lane % HD < HD // 2, pltpu.roll(v, 128 - HD // 2, 1), pltpu.roll(v, HD // 2, 1))


def three_parts(v):
    hi = v.astype(bf16)
    rest = v - hi.astype(f32)
    mid = rest.astype(bf16)
    low = (rest - mid.astype(f32)).astype(bf16)
    return hi, mid, low


def attend_kernel(pieces, block, scale, *refs):
    qkv = refs[:pieces]
    cos_ref, sin_ref, qext_ref, kext_ref = refs[pieces : pieces + 4]
    att_ref, lse_ref, qrot_ref, krot_ref = refs[pieces + 4 : pieces + 8]
    kx, vx = refs[pieces + 8 :]
    step = pl.program_id(1)
    frames = qkv[0].shape[0]
    per_piece = frames // block

    @pl.when(step == 0)
    def _():
        for j in range(pieces):
            rows = pl.ds(j * frames, frames)
            k = qkv[j][:, 128:256].astype(f32)
            k = (k * cos_ref[rows, :] + swap_halves(k) * sin_ref[rows, :]).astype(bf16)
            krot_ref[rows, :] = k
            v = qkv[j][:, 256:384]
            ext = kext_ref[rows, :]
            lane = lanes_of(k.shape)
            one = jnp.where(lane % HD == 0, 1.0, 0.0).astype(bf16)
            low_lane = lane < HD
            kx[0, rows, :] = jnp.where(low_lane, k, ext)
            kx[1, rows, :] = jnp.where(low_lane, ext, k)
            vx[0, rows, :] = jnp.where(low_lane, v, one)
            vx[1, rows, :] = jnp.where(low_lane, one, v)

    rows = pl.ds(pl.multiple_of(step * block, block), block)
    for j in range(pieces):

        @pl.when(step // per_piece == j)
        def _(j=j):
            sub = pl.ds(pl.multiple_of((step - j * per_piece) * block, block), block)
            q = qkv[j][sub, 0:128].astype(f32)
            q = (q * cos_ref[rows, :] + swap_halves(q) * sin_ref[rows, :]).astype(bf16)
            qrot_ref[...] = (q.astype(f32) * scale).astype(bf16)

    q = qrot_ref[...]
    ext = qext_ref[rows, :]
    low_lane = lanes_of(q.shape) < HD
    outs = []
    for h in range(2):
        qx = jnp.where(low_lane, q, ext) if h == 0 else jnp.where(low_lane, ext, q)
        scores = dot_nt(qx, kx[h])
        top = jnp.max(scores, axis=1, keepdims=True)
        expo = jnp.exp(scores - top)
        mixed = dot_nn(expo.astype(bf16), vx[h])
        total = mixed[:, HD : HD + 1] if h == 0 else mixed[:, 0:1]
        outs.append((mixed / total, top + jnp.log(total)))
    low_out = lanes_of((block, 128)) < HD
    att_ref[...] = jnp.where(low_out, outs[0][0], outs[1][0]).astype(bf16)
    lse_ref[...] = jnp.where(low_out, outs[0][1], outs[1][1])


def attend(qkv, cosine, sine, qext, kext, block=384, scale=HD**-0.5):
    pieces = len(qkv)
    frames = qkv[0].shape[0]
    total = pieces * frames
    full = lambda a: pl.BlockSpec(a.shape, lambda p, i: (0, 0))
    tile = pl.BlockSpec((block, 128), lambda p, i: (i, p))
    return pl.pallas_call(
        functools.partial(attend_kernel, pieces, block, scale),
        grid=(2, total // block),
        in_specs=[pl.BlockSpec((frames, 384), lambda p, i: (0, p))] * pieces
        + [full(a) for a in (cosine, sine, qext, kext)],
        out_specs=[tile, tile, tile, pl.BlockSpec((total, 128), lambda p, i: (0, p))],
        out_shape=[jax.ShapeDtypeStruct((total, 256), t) for t in (bf16, f32, bf16, bf16)],
        scratch_shapes=[pltpu.VMEM((2, total, 128), bf16), pltpu.VMEM((2, total, 128), bf16)],
        compiler_params=pltpu.CompilerParams(vmem_limit_bytes=24 * 2**20),
        cost_estimate=pl.CostEstimate(
            flops=8 * total * total * 256, bytes_accessed=total * 4096, transcendentals=4 * total * total
        ),
        name="attend",
    )(*qkv, cosine, sine, qext, kext)


def attend_back_kernel(pieces, block, scale, *refs):
    grads = refs[:pieces]
    values = refs[pieces : 2 * pieces]
    qrot_ref, krot_ref, att_ref, lse_ref, cos_ref, sin_ref, qext_ref, kext_ref = refs[2 * pieces : 2 * pieces + 8]
    out_ref = refs[2 * pieces + 8]
    qx, gx, qm, gm, dq = refs[2 * pieces + 9 :]
    step = pl.program_id(1)
    last = pl.num_programs(1) - 1
    frames = grads[0].shape[0]
    per_piece = frames // block

    @pl.when(step == 0)
    def _():
        for j in range(pieces):
            rows = pl.ds(j * frames, frames)
            q = qrot_ref[rows, :]
            g = grads[j][...]
            lane = lanes_of(q.shape)
            low_lane = lane < HD
            spot = lane % HD
            prod = g.astype(f32) * att_ref[rows, :].astype(f32)
            zero = jnp.zeros_like(q)
            lse = lse_ref[rows, :]
            for h in range(2):
                own = low_lane if h == 0 else jnp.logical_not(low_lane)
                lse_h = lse[:, 0:1] if h == 0 else lse[:, HD : HD + 1]
                delta = jnp.sum(jnp.where(own, prod, 0.0), axis=1, keepdims=True)
                a, b, c = (t.astype(f32) for t in three_parts(-lse_h))
                part = jnp.where(spot == 4, a, jnp.where(spot == 5, b, jnp.where(spot == 6, c, qext_ref[rows, :].astype(f32))))
                qx[h, rows, :] = jnp.where(own, q, part.astype(bf16))
                a, b, c = (t.astype(f32) for t in three_parts(-delta))
                part = jnp.where(spot == 0, a, jnp.where(spot == 1, b, jnp.where(spot == 2, c, 0.0)))
                gx[h, rows, :] = jnp.where(own, g, part.astype(bf16))
                qm[h, rows, :] = jnp.where(own, q, zero)
                gm[h, rows, :] = jnp.where(own, g, zero)
        dq[...] = jnp.zeros_like(dq)

    rows = pl.ds(pl.multiple_of(step * block, block), block)
    for j in range(pieces):

        @pl.when(step // per_piece == j)
        def _(j=j):
            sub = pl.ds(pl.multiple_of((step - j * per_piece) * block, block), block)
            k = krot_ref[rows, :]
            v = values[j][sub, 256:384]
            ext = kext_ref[rows, :]
            lane = lanes_of(k.shape)
            low_lane = lane < HD
            three = jnp.where(lane % HD < 3, 1.0, 0.0).astype(bf16)
            zero = jnp.zeros_like(k)
            small = k.astype(f32) * scale
            dk = jnp.zeros((block, 128), f32)
            dv = jnp.zeros((block, 128), f32)
            for h in range(2):
                own = low_lane if h == 0 else jnp.logical_not(low_lane)
                kx = jnp.where(own, k, ext)
                vx = jnp.where(own, v, three)
                probs = jnp.exp(dot_nt(kx, qx[h]))
                grad = (probs * dot_nt(vx, gx[h])).astype(bf16)
                dv = dv + dot_nn(probs.astype(bf16), gm[h])
                dk = dk + dot_nn(grad, qm[h])
                turned = jnp.transpose(jnp.where(own, small, 0.0)).astype(bf16)
                dq[...] += dot_nn(turned, grad)
            dk = dk * cos_ref[rows, :] - swap_halves(dk) * sin_ref[rows, :]
            out_ref[rows, 128:256] = dk.astype(bf16)
            out_ref[rows, 256:384] = dv.astype(bf16)

    @pl.when(step == last)
    def _():
        g = jnp.transpose(dq[...])
        g = g * cos_ref[...] - swap_halves(g) * sin_ref[...]
        out_ref[:, 0:128] = g.astype(bf16)


def attend_back(grads, qkv, qrot, krot, att, lse, cosine, sine, qext, kext, block=384, scale=HD**-0.5):
    pieces = len(grads)
    frames = grads[0].shape[0]
    total = pieces * frames
    full = lambda a: pl.BlockSpec(a.shape, lambda p, i: (0, 0))
    return pl.pallas_call(
        functools.partial(attend_back_kernel, pieces, block, scale),
        grid=(2, total // block),
        in_specs=[pl.BlockSpec((frames, 128), lambda p, i: (0, p))] * pieces
        + [pl.BlockSpec((frames, 384), lambda p, i: (0, p))] * pieces
        + [pl.BlockSpec((total, 128), lambda p, i: (0, p))] * 4
        + [full(a) for a in (cosine, sine, qext, kext)],
        out_specs=pl.BlockSpec((total, 384), lambda p, i: (0, p)),
        out_shape=jax.ShapeDtypeStruct((total, 768), bf16),
        scratch_shapes=[pltpu.VMEM((2, total, 128), bf16)] * 4 + [pltpu.VMEM((128, total), f32)],
        compiler_params=pltpu.CompilerParams(vmem_limit_bytes=34 * 2**20),
        cost_estimate=pl.CostEstimate(
            flops=20 * total * total * 256, bytes_accessed=total * 8192, transcendentals=4 * total * total
        ),
        name="attend_back",
    )(*grads, *qkv, qrot, krot, att, lse, cosine, sine, qext, kext)


def frame_tables(seg, pos, valid):
    half = HD // 2
    freq = 10000.0 ** (-jnp.arange(half, dtype=f32) / half)
    angle = pos.astype(f32)[:, None] * freq
    cosine, sine = jnp.cos(angle), jnp.sin(angle)
    cosine = jnp.concatenate([cosine] * 4, axis=1)
    sine = jnp.concatenate([-sine, sine, -sine, sine], axis=1)
    spot = jnp.arange(128)[None, :] % HD
    seg, valid = seg[:, None], valid[:, None] > 0
    qext = jnp.where((spot < 3) & (spot != seg) | (spot == 3), -NEG, 0.0).astype(bf16)
    kext = ((spot == seg) & (spot < 3) | (spot == 3) & ~valid | (spot >= 4) & (spot < 7)).astype(bf16)
    return cosine, sine, qext, kext


def swap(v, mask):
    return lax.ppermute(v, "seq", [(i, i ^ mask) for i in range(4)])


def spread(v, before=()):
    near = swap(v, 1)
    far = swap(v, 2)
    return [v, near, far, swap(after(far, *before) if before else far, 1)]


def collect(parts, wait=()):
    low = [part.astype(bf16) for part in parts]
    if wait:
        low = list(after(tuple(low), *wait))
    far_near = swap(low[3], 1)
    near = swap(low[1], 1)
    sent = (low[2].astype(f32) + far_near.astype(f32)).astype(bf16)
    far = swap(sent, 2)
    return parts[0] + near.astype(f32) + far.astype(f32), sent


def exchange(parts):
    return [parts[0], swap(parts[1], 1), swap(parts[2], 2), swap(parts[3], 3)]


def by_place(parts, me):
    odd, high = (me & 1) == 1, (me & 2) == 2
    parts = [jnp.where(odd, parts[t ^ 1], parts[t]) for t in range(4)]
    return [jnp.where(high, parts[t ^ 2], parts[t]) for t in range(4)]


def ring_step(v, step):
    return lax.ppermute(v, "dp", [(RING[i], RING[(i + step) % 8]) for i in range(8)])


class RingGather:
    def __init__(self, v):
        self.found, self.front, self.count = [(0, 0, v)], (v, v), 0

    def step(self, *before):
        one, other = after(self.front, *before) if before else self.front
        self.count += 1
        k = self.count
        if k < 4:
            self.front = ring_step(one, 1), ring_step(other, -1)
            self.found += [(k, 0, self.front[0]), (8 - k, 0, self.front[1])]
        else:
            middle = one.shape[0] // 2
            self.front = ring_step(one[:middle], 1), ring_step(other[middle:], -1)
            self.found += [(4, 0, self.front[0]), (4, middle, self.front[1])]
        return self.front


def ring_add_kernel(k, count, index_ref, *refs):
    plus, minus = refs[:count], refs[count : 2 * count]
    moving = refs[2 * count : -1 if k == 0 else -2]
    outs = refs[-1:] if k == 0 else refs[-2:]
    rows = plus[0].shape[1]
    middle = rows // 2
    upper, lower = slice(0, middle), slice(middle, rows)
    start = 0
    for i in range(count):
        columns = slice(start, start + plus[i].shape[2])
        start += plus[i].shape[2]
        if k == 4:
            outs[0][:, columns] = plus[i][0, upper, :].astype(bf16)
            outs[1][:, columns] = plus[i][0, lower, :].astype(bf16)
            continue
        ahead = plus[i][0].astype(f32)
        if k == 0:
            outs[0][:, columns] = (
                ahead + moving[0][:, columns].astype(f32) + moving[1][:, columns].astype(f32)
            )
            continue
        behind = minus[i][0].astype(f32)
        one, other = moving[0][:, columns].astype(f32), moving[1][:, columns].astype(f32)
        if k == 3:
            outs[0][upper, columns] = (ahead[upper] + one).astype(bf16)
            outs[0][lower, columns] = ahead[lower].astype(bf16)
            outs[1][upper, columns] = behind[upper].astype(bf16)
            outs[1][lower, columns] = (behind[lower] + other).astype(bf16)
        else:
            outs[0][:, columns] = (ahead + one).astype(bf16)
            outs[1][:, columns] = (behind + other).astype(bf16)


def ring_add(index, arrays, moving, k):
    rows, columns = arrays[0].shape[1], sum(a.shape[2] for a in arrays)
    ahead = [pl.BlockSpec((1, rows, a.shape[2]), lambda i, index: (index[(8 - k) % 8], 0, 0)) for a in arrays]
    behind = [pl.BlockSpec((1, rows, a.shape[2]), lambda i, index: (index[k], 0, 0)) for a in arrays]
    whole = lambda shape: pl.BlockSpec(shape, lambda i, index: (0, 0))
    height = rows // 2 if k == 4 else rows
    n_out = 1 if k == 0 else 2
    return pl.pallas_call(
        functools.partial(ring_add_kernel, k, len(arrays)),
        grid_spec=pltpu.PrefetchScalarGridSpec(
            num_scalar_prefetch=1,
            grid=(1,),
            in_specs=ahead + behind + [whole(m.shape) for m in moving],
            out_specs=[whole((height, columns))] * n_out,
        ),
        out_shape=[jax.ShapeDtypeStruct((height, columns), f32 if k == 0 else bf16)] * n_out,
        compiler_params=pltpu.CompilerParams(vmem_limit_bytes=16 * 2**20),
        name="ring_add",
    )(index, *arrays, *arrays, *moving)


class RingSum:
    def __init__(self, arrays, index, ringed):
        self.arrays, self.index, self.ringed = arrays, index, ringed
        self.front, self.count = (), 4

    def step(self, *before):
        if self.ringed:
            arrays, front = self.arrays, self.front
            if before:
                arrays, front = after((arrays, front), *before)
            moving = ring_add(self.index, arrays, front, self.count)
            self.front = ring_step(moving[0], 1), ring_step(moving[1], -1)
            self.count -= 1
        return self.front

    def total(self):
        if self.ringed:
            return ring_add(self.index, self.arrays, self.front, 0)[0]
        low = jnp.concatenate([a.astype(bf16) for a in self.arrays], axis=2)
        return lax.psum_scatter(low, "dp", scatter_dimension=0).astype(f32)


def after(v, *others):
    return lax.optimization_barrier((v, *others))[0]


def assemble_kernel(copies, n_in, n_out, index_ref, *refs):
    arrays, outs, sems = refs[:n_in], refs[n_in : n_in + n_out], refs[-1]
    moves = []
    me = index_ref[8]
    for number, (a, row, count, out, k, j, per_dp, per_seq, column, more) in enumerate(copies):
        start = index_ref[k] * per_dp + jnp.bitwise_xor(me, j) * per_seq + more
        target = outs[out].at[
            pl.ds(pl.multiple_of(start, count), count), pl.ds(column, arrays[a].shape[1])
        ]
        moves.append(
            pltpu.make_async_copy(arrays[a].at[pl.ds(row, count), :], target, sems.at[number])
        )
    for move in moves:
        move.start()
    for move in moves:
        move.wait()


def assemble(index, arrays, copies, shapes):
    anywhere = pl.BlockSpec(memory_space=pl.ANY)
    return pl.pallas_call(
        functools.partial(assemble_kernel, tuple(copies), len(arrays), len(shapes)),
        grid_spec=pltpu.PrefetchScalarGridSpec(
            num_scalar_prefetch=1,
            grid=(1,),
            in_specs=[anywhere] * len(arrays),
            out_specs=[pl.BlockSpec(shape, lambda i, index: (0, 0)) for shape in shapes],
            scratch_shapes=[pltpu.SemaphoreType.DMA((len(copies),))],
        ),
        out_shape=[jax.ShapeDtypeStruct(shape, bf16) for shape in shapes],
        compiler_params=pltpu.CompilerParams(vmem_limit_bytes=8 * 2**20 + 5 * sum(r * c for r, c in shapes)),
        name="assemble",
    )(index, *arrays)


class Gather:
    def __init__(self, index):
        self.index, self.arrays, self.copies, self.shapes = index, [], [], []

    def out(self, rows, columns):
        self.shapes.append((rows, columns))
        return len(self.shapes) - 1

    def add(self, piece, k, blocks):
        self.arrays.append(piece)
        for row, count, out, j, per_dp, per_seq, column, more in blocks:
            self.copies.append(
                (len(self.arrays) - 1, row, count, out, k, j, per_dp, per_seq, column, more)
            )

    def run(self):
        return assemble(self.index, self.arrays, self.copies, self.shapes)


def half(v, which):
    middle = v.shape[1] // 2
    return jnp.where(which == 1, v[:, middle:], v[:, :middle])


def merge(mine, other, core):
    return jnp.concatenate(
        [jnp.where(core == 1, other, mine), jnp.where(core == 1, mine, other)], axis=1
    )


def by_dp(grad, groups):
    return grad.reshape(groups, grad.shape[0] // groups, grad.shape[1])


def finish(block, me):
    rows = block.shape[0] // 4
    low = block.astype(bf16)
    parts = by_place([low[t * rows : (t + 1) * rows] for t in range(4)], me)
    return by_place(exchange(parts), me)


def halves_sum(parts):
    total = [parts[c].astype(f32) + parts[2 + c].astype(f32) for c in range(2)]
    return jnp.concatenate(total, axis=1)


def on_device(
    layer_input,
    skip_input,
    time_embed,
    segment_ids,
    positions,
    valid_mask,
    skip_weight,
    time_weight,
    query_weight,
    key_weight,
    value_weight,
    out_weight,
    up_weight,
    down_weight,
    cotangent,
):
    rows, frames, width = layer_input.shape
    hidden = up_weight.shape[1]
    groups = lax.axis_size("dp")
    me, dp = lax.axis_index("seq"), lax.axis_index("dp")
    local = width // 4
    local_hidden = hidden // 4

    core = me & 1
    hidden_block = hidden // (groups * 4)
    ringed = groups == 8
    first_in, second_in = layer_input.reshape(frames, width), skip_input.reshape(frames, width)
    time_a, time_b = time_weight[:, : 2 * width], time_weight[:, 2 * width :]
    n_skip, n_time = skip_weight.shape[0], time_weight.shape[0]

    def needed():
        triple = [
            jnp.concatenate(
                [
                    w[:, t * local + p * 128 : t * local + (p + 1) * 128]
                    for p in range(2)
                    for w in (query_weight, key_weight, value_weight)
                ],
                axis=1,
            )
            for t in range(4)
        ]
        upper_w = [
            jnp.concatenate(
                [
                    up_weight[:, (g * 4 + t) * hidden_block : (g * 4 + t + 1) * hidden_block]
                    for g in range(groups)
                ],
                axis=1,
            )
            for t in range(4)
        ]
        return triple, upper_w

    triple, upper_w = needed()
    index = None
    marks = jnp.concatenate(spread(jnp.concatenate([segment_ids, positions, valid_mask])), axis=1)
    tables = frame_tables(marks[0], marks[1], marks[2])
    time_value = time_embed.reshape(frames, width).astype(f32)
    time_act = (time_value * jax.nn.sigmoid(time_value)).astype(bf16)
    joined = jnp.concatenate([first_in, second_in], axis=1)
    row_own = jnp.concatenate([first_in, second_in, time_act], axis=1)

    if ringed:
        place = jnp.asarray(PLACE, jnp.int32)[dp]
        order = jnp.asarray(RING, jnp.int32)[(place - jnp.arange(8)) % 8]
        index = jnp.concatenate([order, me[None].astype(jnp.int32)])

        first = Gather(index)
        o_skip, o_time_a = first.out(32 * n_skip, width), first.out(32 * n_time, 2 * width)
        own = jnp.concatenate([skip_weight, time_a[:, :width], time_a[:, width:]], axis=0)
        layout = [
            (0, n_skip, o_skip, 0),
            (n_skip, n_time, o_time_a, 0),
            (n_skip + n_time, n_time, o_time_a, width),
        ]
        n_own = own.shape[0]
        ring_a = RingGather(jnp.concatenate([own, swap(own, 2)], axis=0))
        ring_a.step()
        triple, upper_w, time_b, out_weight = after(
            (triple, upper_w, time_b, out_weight), ring_a.found[0][2]
        )

        def to_core(entries):
            near = [swap(piece, 1) for _, _, piece in entries]
            for (k, row, piece), other in zip(entries, near):
                for array, flip in ((piece, 0), (other, 1)):
                    for part in range(row // n_own, (row + piece.shape[0]) // n_own):
                        at_row = part * n_own - row
                        first.add(
                            array,
                            k,
                            [
                                (at_row + at, count, out, (2 * part) ^ flip, 4 * count, count, column, 0)
                                for at, count, out, column in layout
                            ],
                        )
            return near

        rest = []
        for t in range(4):
            sides = jnp.concatenate(
                [
                    w[:, (t & 1) * (w.shape[1] // 2) : ((t & 1) + 1) * (w.shape[1] // 2)]
                    for w in (out_weight, time_b)
                ],
                axis=1,
            )
            rest.append(jnp.concatenate([triple[t], sides, upper_w[t]], axis=1))
        rest = by_place(rest, me)
        near = to_core(ring_a.found[:1])
        ring_a.step(*near, *rest)
        near = to_core(ring_a.found[1:3])
        time_far = swap(after(time_act, *rest), 2)
        second_far = swap(after(second_in, *rest), 2)
        first_far = swap(after(first_in, *rest), 2)
        rest = exchange(rest)
        ring_a.step(*near, *rest, time_act)
        near = to_core(ring_a.found[3:5])
        ring_a.step(*near, *tables, time_far)
        rest = jnp.concatenate(by_place(rest, me), axis=0)
        cut = 3 * local + width // 2, 3 * local + width // 2 + 3 * width // 2
        ring_b_own, ring_c_own, ring_d_own = after(
            (
                rest[:, : cut[0]],
                rest[:, cut[0] : cut[1]],
                jnp.concatenate([rest[:, cut[1] :], down_weight], axis=1),
            ),
            *ring_a.found[5][2:],
            *ring_a.found[6][2:],
        )
        ring_b, ring_c, ring_d = (RingGather(v) for v in (ring_b_own, ring_c_own, ring_d_own))
        step = ring_b.step()
        near = to_core(ring_a.found[5:9])
        first.arrays[0] = after(first.arrays[0], *step)
        step = ring_b.step()
        ring_c.step(*ring_b.found[1][2:])
        skip_full, time_a_full = first.run()

        def block_rows(ring, shape):
            gather = Gather(index)
            out = gather.out(*shape)
            for k, row, piece in ring.found:
                gather.add(piece, k, [(0, piece.shape[0], out, 0, width // 8, 0, 0, row)])
            return gather.run()[0]

        joined, time_act = after((joined, time_act), *step)
    else:
        first_far, second_far, time_far = swap(first_in, 2), swap(second_in, 2), swap(time_act, 2)
        skip_full, time_a_full, time_b_full, out_full = (
            lax.all_gather(w, ("dp", "seq"), axis=0, tiled=True)
            for w in (skip_weight, time_a, time_b, out_weight)
        )
        triple_full, up_full = (
            lax.all_gather(
                jnp.concatenate(by_place(exchange(by_place(parts, me)), me), axis=0),
                "dp",
                axis=0,
                tiled=True,
            )
            for parts in (triple, upper_w)
        )
        down_full = lax.all_gather(down_weight, "dp", axis=0, tiled=True)
        time_b_sides = [half(time_b_full, core), half(time_b_full, 1 - core)]
        out_sides = [half(out_full, core), half(out_full, 1 - core)]

    base = dot_nn(joined, skip_full)
    shift_a, scale_a = jnp.split(dot_nn(time_act, time_a_full), 2, axis=1)
    normed_a, inverse_a = norm_rows(base)
    hidden_own = (normed_a * (1.0 + scale_a) + shift_a).astype(bf16)
    if ringed:
        step = ring_b.step()
        hidden_own = after(hidden_own, second_far, *step)
        ring_c.step()
        ring_b.step(hidden_own)
        ring_c.step(hidden_own)
        hidden_a = spread(hidden_own, ring_b.front)
        wide = block_rows(ring_b, (width, cut[0]))
        triple_full = wide[:, : 3 * local]
        out_mine = wide[:, 3 * local :]
        out_sides = [out_mine, swap(out_mine, 1)]
    else:
        hidden_a = spread(hidden_own)
    qkv = [dot_nn(h, triple_full).astype(bf16) for h in hidden_a]
    if ringed:
        ring_c.step(qkv[0])
        ring_d.step(qkv[0])
        mine = block_rows(ring_c, (width, 3 * width // 2))
        time_b_sides = [mine, swap(mine, 1)]
        qkv = list(after(tuple(qkv), mine))
    att, logsum, query_rot, key_rot = attend(qkv, *tables)
    if ringed:
        att = after(att, time_b_sides[1], *ring_d.front)
    att = after(att, first_far)
    att_parts = [att[j * frames : (j + 1) * frames] for j in range(4)]
    attended = exchange(att_parts)
    row_near = swap(after(row_own, att), 1)
    row_far = jnp.concatenate([first_far, second_far, time_far], axis=1)
    row_inputs = [row_own, row_near, row_far, swap(row_far, 1)]
    upstream = cotangent.reshape(frames, width).astype(f32)
    time_act_b = time_act
    if ringed:
        ring_d.step(att)
        time_act_b = after(time_act, att)
    shift_b, scale_b, gate_b = jnp.split(
        merge(dot_nn(time_act_b, time_b_sides[0]), dot_nn(time_act_b, time_b_sides[1]), core),
        3,
        axis=1,
    )
    ffn_grad = (upstream * gate_b).astype(bf16)
    attended = list(after(tuple(attended), ffn_grad))
    ffn_grad = spread(ffn_grad)
    attended = jnp.concatenate(by_place(attended, me), axis=1)
    if ringed:
        step = ring_d.front
        ring_d.step(attended)
        attended = after(attended, *step)
    middle = base + merge(dot_nn(attended, out_sides[0]), dot_nn(attended, out_sides[1]), core)
    normed_b, inverse_b = norm_rows(middle)

    hidden_own = (normed_b * (1.0 + scale_b) + shift_b).astype(bf16)
    if ringed:
        hidden_own = after(hidden_own, *ring_d.front)
        ring_d.step()
    hidden_b = spread(hidden_own)
    if ringed:
        ffn_full = block_rows(ring_d, (width, 2 * local_hidden))
        up_full, down_full = ffn_full[:, :local_hidden], ffn_full[:, local_hidden:]
    hb = [jnp.concatenate(hidden_b[:2]), jnp.concatenate(hidden_b[2:])]
    fg = [jnp.concatenate(ffn_grad[:2]), jnp.concatenate(ffn_grad[2:])]
    upper = dot_nn(hb[1], up_full)
    acted_far = gelu_value(upper).astype(bf16)
    ug_far = (dot_nt(fg[1], down_full) * gelu_slope(upper)).astype(bf16)
    far = dot_nt(ug_far, up_full)
    far_low = far.astype(bf16)
    hb[0] = after(hb[0], far_low)
    upper = dot_nn(hb[0], up_full)
    sent = (far[:frames] + swap(far_low[frames:], 1).astype(f32)).astype(bf16)
    fg[0] = after(fg[0], sent)
    acted = [gelu_value(upper).astype(bf16), acted_far]
    ug = [(dot_nt(fg[0], down_full) * gelu_slope(upper)).astype(bf16), ug_far]
    own = dot_nt(ug[0], up_full)
    hidden_b_grad = (
        own[:frames] + swap(own[frames:].astype(bf16), 1).astype(f32) + swap(sent, 2).astype(f32)
    )
    acted, fg, ug, hb = after((acted, fg, ug, hb), own)
    part = [dot_nn(a, down_full) for a in acted]
    grad_down = dot_tn(acted[0], fg[0]) + dot_tn(acted[1], fg[1])
    grad_up = dot_tn(hb[0], ug[0]) + dot_tn(hb[1], ug[1])
    grad_ffn = jnp.concatenate([grad_up.astype(bf16), grad_down.astype(bf16)], axis=1)
    hidden_b_grad = after(hidden_b_grad, grad_ffn, *part)
    ffn, _ = collect(
        [part[0][:frames], part[0][frames:], part[1][:frames], part[1][frames:]], (hidden_b_grad,)
    )
    ffn_sum = lax.psum_scatter(grad_ffn, "dp", scatter_dimension=0, tiled=True).astype(f32)

    scale_b_grad = hidden_b_grad * normed_b
    middle_grad = upstream + norm_back(hidden_b_grad * (1.0 + scale_b), normed_b, inverse_b)
    branch_grad = middle_grad.astype(bf16)
    branch_sides = [half(branch_grad, core), half(branch_grad, 1 - core)]
    attended_grad = (
        dot_nt(branch_sides[0], out_sides[0]) + dot_nt(branch_sides[1], out_sides[1])
    ).astype(bf16)
    att_grad_parts = by_place([attended_grad[:, t * local : (t + 1) * local] for t in range(4)], me)
    att_grad = exchange(att_grad_parts)
    def to_columns(grads):
        return [
            jnp.concatenate([g[:, t * local : (t + 1) * local] for g in grads], axis=1) for t in range(4)
        ]

    modul_sent = by_place(to_columns([hidden_b_grad.astype(bf16), scale_b_grad.astype(bf16)]), me)
    modul_b_parts = exchange(after(tuple(modul_sent), *att_grad_parts))
    grad_out = [dot_tn(attended, side).astype(bf16) for side in branch_sides]
    near_out = swap(grad_out[1], 1)
    att_grad = after(tuple(att_grad), *modul_sent, *grad_out)
    triple_grad = attend_back(att_grad, qkv, query_rot, key_rot, att, logsum, *tables)
    triple_grad = after(triple_grad, *modul_b_parts, near_out)
    back = dot_nt(triple_grad, triple_full)
    far_low = back[3 * frames :].astype(bf16)
    triple_grad, ffn, hidden_a_all = after((triple_grad, ffn, jnp.concatenate(hidden_a)), far_low)
    grad_triple = dot_tn(hidden_a_all, triple_grad).astype(bf16)
    sent = (back[2 * frames : 3 * frames] + swap(far_low, 1).astype(f32)).astype(bf16)
    hidden_a_grad = (
        back[:frames]
        + swap(back[frames : 2 * frames].astype(bf16), 1).astype(f32)
        + swap(sent, 2).astype(f32)
    )
    modul_b_parts = after(tuple(modul_b_parts), sent, grad_triple)
    grad_time_b = sum(dot_tn(v[:, 2 * width :], g) for v, g in zip(row_inputs, modul_b_parts))
    grad_out = (grad_out[0].astype(f32) + near_out.astype(f32)).astype(bf16)
    ring_w = RingSum(
        [by_dp(g, groups) for g in (grad_time_b.astype(bf16), grad_out, grad_triple)], index, ringed
    )
    ring_w.step()
    ffn = after(ffn, grad_time_b, grad_triple)
    output = (middle + gate_b * ffn).astype(bf16).reshape(rows, frames, width)
    gate_b_grad = (upstream * ffn).astype(bf16)
    modul_b_grad = jnp.concatenate(
        [hidden_b_grad.astype(bf16), scale_b_grad.astype(bf16), gate_b_grad], axis=1
    )
    modul_sides = [half(modul_b_grad, core), half(modul_b_grad, 1 - core)]
    time_back_b = dot_nt(modul_sides[0], time_b_sides[0]) + dot_nt(modul_sides[1], time_b_sides[1])
    hidden_a_grad = after(hidden_a_grad, time_back_b)

    scale_a_grad = hidden_a_grad * normed_a
    modul_a_grad = jnp.concatenate([hidden_a_grad, scale_a_grad], axis=1).astype(bf16)
    modul_sent = by_place(
        to_columns([modul_a_grad[:, :width], modul_a_grad[:, width:], gate_b_grad]), me
    )
    modul_parts = exchange(modul_sent)
    base_grad = (
        middle_grad + norm_back(hidden_a_grad * (1.0 + scale_a), normed_a, inverse_a)
    ).astype(bf16)
    base_sent = by_place([base_grad[:, t * local : (t + 1) * local] for t in range(4)], me)
    base_parts = exchange(base_sent)
    step = ring_w.step(*base_sent)
    base_grad, modul_a_grad = after((base_grad, modul_a_grad), *base_sent)
    joined_grad = dot_nt(base_grad, skip_full)
    time_back = dot_nt(modul_a_grad, time_a_full) + time_back_b
    time_grad = (time_back * silu_slope(time_value)).reshape(rows, frames, width)
    modul_parts = after(tuple(modul_parts), joined_grad, *step)
    ring_w.step()
    grad_time_a = sum(dot_tn(v[:, 2 * width :], g) for v, g in zip(row_inputs, modul_parts))
    grad_skip = sum(dot_tn(v[:, : 2 * width], g) for v, g in zip(row_inputs, base_parts))
    rows_skip = n_skip // 2
    grad_skip = grad_skip.reshape(groups, 4, 2, rows_skip, local)
    grad_skip = jnp.concatenate([grad_skip[:, :, 0], grad_skip[:, :, 1]], axis=3)
    ring_l = RingSum(
        [
            grad_skip.reshape(groups, 4 * rows_skip, 2 * local).astype(bf16),
            by_dp(grad_time_a.astype(bf16), groups),
        ],
        index,
        ringed,
    )
    ring_l.step()
    ring_w.step()
    ring_l.step()
    wide_sum = ring_w.total()
    ring_l.step(wide_sum)
    parts = finish(
        after(jnp.concatenate([ffn_sum[:, :local_hidden], wide_sum], axis=1), *ring_l.front), me
    )
    ring_l.step()
    up_sum = jnp.concatenate(
        [
            p[:, g * hidden_block : (g + 1) * hidden_block]
            for g in range(groups)
            for p in parts
        ],
        axis=1,
    )
    split = local_hidden + 2 * local, local_hidden + 2 * local + width // 2
    by_blocks = lambda parts, start, i: jnp.concatenate(
        [p[:, start + i * local : start + (i + 1) * local] for p in parts], axis=1
    ).astype(f32)
    out_sum = halves_sum([p[:, split[0] : split[1]] for p in parts])
    triples = [
        jnp.concatenate(
            [
                p[:, split[1] + i * 128 + q * 384 : split[1] + (i + 1) * 128 + q * 384]
                for p in parts
                for q in range(2)
            ],
            axis=1,
        ).astype(f32)
        for i in range(3)
    ]
    last = finish(ring_l.total(), me)
    columns = [by_blocks(last, 0, i) for i in range(5)]
    time_b_sum = jnp.concatenate(
        [by_blocks(parts, local_hidden, 0), by_blocks(parts, local_hidden, 1), columns[4]], axis=1
    )
    skip_sum = jnp.concatenate(columns[:2], axis=0)
    time_a_sum = jnp.concatenate(columns[2:4], axis=1)
    return (
        output,
        joined_grad[:, :width].reshape(rows, frames, width),
        joined_grad[:, width:].reshape(rows, frames, width),
        time_grad,
        skip_sum,
        jnp.concatenate([time_a_sum, time_b_sum], axis=1),
        *triples,
        out_sum,
        up_sum.astype(f32),
        ffn_sum[:, local_hidden:],
    )


def solution(mesh):
    frames = P("dp", "seq", None)
    marks = P("dp", "seq")
    weight = P(("dp", "seq"), None)
    return jax.shard_map(
        on_device,
        mesh=mesh,
        in_specs=(frames,) * 3 + (marks,) * 3 + (weight,) * 8 + (frames,),
        out_specs=(frames,) * 4 + (weight,) * 8,
        check_vma=False,
    )
```

time: 648 us -> 539 us (0.83)
  waiting for transfers between devices: 253 us -> 194 us
  local copies, waits for them, and re-layouts: 54.4 us -> 26.2 us
  between operations: 40.6 us -> 17 us
    ppermute x56 -> x48, waiting for transfers between devices: 179 us -> 103 us  [ring_step(): lax.ppermute(v, 'dp', [(RING[i], RING[(i + step) % 8]) for i in range(8)])]
    unnamed x291 -> x295, local copies, waits for them, and re-layouts: 39.3 us -> 11.4 us
    ppermute x56 -> x63, waiting for transfers between devices: 73.2 us -> 90.8 us  [swap(): return lax.ppermute(v, 'seq', [(i, i ^ mask) for i in range(4)])]
    ppermute x56 -> x63, starting transfers between devices: 24.6 us -> 36.8 us  [swap(): return lax.ppermute(v, 'seq', [(i, i ^ mask) for i in range(4)])]
    ppermute x56 -> x48, starting transfers between devices: 62.2 us -> 51.1 us  [ring_step(): lax.ppermute(v, 'dp', [(RING[i], RING[(i + step) % 8]) for i in range(8)])]
    another operation x5 -> x1, other arithmetic: 8.8 us -> 0.77 us
    convert_element_type x19 -> x12, other arithmetic: 18.3 us -> 10.7 us  [the longest x1 2.52 us: on_device(): time_act = (time_value * jax.nn.sigmoid(time_value)).astype(bf16)]
    pallas_call x0 -> x10, Pallas kernels: none -> 6.7 us  [ring_add(): pl.pallas_call(functools.partial(ring_add_kernel, k, len(arrays)), grid_s...]
  transfers between devices with their start and end apart: 114 -> 112, of which waited for: 48 -> 52; matrix products, arithmetic and copies ran while one was open for 21% -> 27% of each run, Pallas kernels for 11% -> 14%
where the time goes in v3:
time: 539 us; the launch traced here: 530 us
  waiting for transfers between devices  194 us (36%)
  starting transfers between devices  87.9 us (16%)
  matrix products  82.6 us (15%)
  Pallas kernels  74.8 us (14%)
  other arithmetic  47.8 us (9%)
  local copies, waits for them, and re-layouts  26.2 us (5%)
  between operations  17 us (3%)
    ppermute x48, waiting for transfers between devices, ring_step(): lax.ppermute(v, 'dp', [(RING[i], RING[(i + step) % 8]) for i in range(8)])  103 us
    ppermute x63, waiting for transfers between devices, swap(): return lax.ppermute(v, 'seq', [(i, i ^ mask) for i in range(4)])  90.8 us
    ppermute x48, starting transfers between devices, ring_step(): lax.ppermute(v, 'dp', [(RING[i], RING[(i + step) % 8]) for i in range(8)])  51.1 us
    ppermute x63, starting transfers between devices, swap(): return lax.ppermute(v, 'seq', [(i, i ^ mask) for i in range(4)])  36.8 us
    dot_general x19, matrix products, dot_tn(): lax.dot_general(a, b, (((0,), (0,)), ((), ())), preferred_element_type=f32)  32.1 us
    pallas_call x1, Pallas kernels, attend_back(): pl.pallas_call(functools.partial(attend_back_kernel, pieces, block, scale...  31.6 us
    dot_general x14, matrix products, dot_nn(): lax.dot_general(a, b, (((1,), (0,)), ((), ())), preferred_element_type=f32)  27.6 us
    dot_general x11, matrix products, dot_nt(): lax.dot_general(a, b, (((1,), (1,)), ((), ())), preferred_element_type=f32)  22.9 us
  transfers between devices with their start and end apart: 112, of which 52 were waited for; matrix products, arithmetic and copies ran while one was open for 27% of the time, Pallas kernels for 14%

profile of v3, /device:TPU:0, one launch (start us, length us, event | category | flops | bytes accessed | tf_op | source)
XLA Modules:
  0.0 529.9 jit_solution(5077172347833241640)
XLA Ops:
  8.0 3.0 collective-permute-start.22
  14.6 2.5 fusion.19
  18.8 2.8 fusion.80
  27.4 3.6 collective-permute-done.2
  30.9 4.1 collective-permute-done.1
  35.3 4.1 collective-permute-done.4.refs_4_.refs_5_
  43.4 2.5 pad_maximum_fusion.14
  49.1 4.4 collective-permute-done.7.refs_12_.refs_13_
  59.1 8.2 %collective-permute-done.24 = bf16[384,1024]{1,0:T(8,128)(2,1)S(1)} collective-permute-done((bf16[384,1024]{1,0:T(8,128)(2,1)}, bf16[384,1024]{1,0:T(8,128)(2,1)S(1)}, u32[]{:S(2)}, u32[]{:S(2)}) %collective-permute-start.24) | collective-permute-done | bytes 786464 | tf_op jit(solution)/shard_map/ppermute | solution.py:266
  74.7 4.1 collective-permute-done.25.refs_28_
  78.8 2.2 collective-permute-done.27.refs_30_
  92.0 8.9 %assemble.4 = (bf16[2048,1024]{1,0:T(8,128)(2,1)S(1)}, bf16[1024,2048]{1,0:T(8,128)(2,1)S(1)}) custom-call(s32[9]{0:T(128)S(1)} %pad_add_fusion.6.index_ref, bf16[256,1024]{1,0:T(8,128)(2,1)S(1)} %pad_maximum_fusion.28.refs_0_.refs_1_, bf16[256,1024]{1,0:T(8,128)(2,1)S(1)} %pad_maximum_fusion.28.refs_0_.refs_1_, bf16[256,1024]{1,0:T(8,128)(2,1)S(1)} %copy-done.4, ...), custom_call_target="tpu_custom_call" | custom-call | tf_op jit(solution)/shard_map/assemble/pallas_call | solution.py:418
  101.0 3.5 fusion.117
  111.5 5.8 %collective-permute-done.30.refs_5_ = bf16[128,1280]{1,0:T(8,128)(2,1)S(1)} collective-permute-done((bf16[128,1280]{1,0:T(8,128)(2,1)S(1)}, bf16[128,1280]{1,0:T(8,128)(2,1)S(1)}, u32[]{:S(2)}, u32[]{:S(2)}) %collective-permute-start.30) | collective-permute-done | bytes 327712 | tf_op jit(solution)/shard_map/ppermute | solution.py:297
  121.0 4.7 collective-permute-done.39.refs_3_
  132.8 3.4 collective-permute-done.41.refs_5_
  139.6 3.6 collective-permute-done.43.refs_7_
  144.9 2.6 assemble.6
  148.3 19.2 %collective-permute-done.35 = bf16[384,1024]{1,0:T(8,128)(2,1)S(1)} collective-permute-done((bf16[384,1024]{1,0:T(8,128)(2,1)S(1)}, bf16[384,1024]{1,0:T(8,128)(2,1)S(1)}, u32[]{:S(2)}, u32[]{:S(2)}) %collective-permute-start.35) | collective-permute-done | bytes 786464 | tf_op jit(solution)/shard_map/ppermute | solution.py:266
  173.7 21.2 %attend.1 = (bf16[1536,256]{1,0:T(8,128)(2,1)S(1)}, f32[1536,256]{1,0:T(8,128)S(1)}, bf16[1536,256]{1,0:T(8,128)(2,1)S(1)}, bf16[1536,256]{1,0:T(8,128)(2,1)S(1)}) custom-call(bf16[384,768]{1,0:T(8,128)(2,1)S(1)} %convolution_convert_fusion.6.refs_0_.refs_4_, bf16[384,768]{1,0:T(8,128)(2,1)S(1)} %convolution_convert_fusion.5.refs_1_.refs_5_, ...), custom_call_target="tpu_custom_call" | custom-call | flops 4831838208 | bytes 6291456 | tf_op jit(solution)/shard_map/attend/pallas_call | solution.py:138
  197.1 3.1 fusion.118
  200.3 2.6 broadcast_select_fusion
  208.0 9.1 %collective-permute-done.52.refs_3_ = bf16[128,2048]{1,0:T(8,128)(2,1)S(1)} collective-permute-done((bf16[128,2048]{1,0:T(8,128)(2,1)S(1)}, bf16[128,2048]{1,0:T(8,128)(2,1)S(1)}, u32[]{:S(2)}, u32[]{:S(2)}) %collective-permute-start.52) | collective-permute-done | bytes 524320 | tf_op jit(solution)/shard_map/ppermute | solution.py:297
  223.2 9.4 %collective-permute-done.58.refs_5_ = bf16[128,2048]{1,0:T(8,128)(2,1)} collective-permute-done((bf16[128,2048]{1,0:T(8,128)(2,1)S(1)}, bf16[128,2048]{1,0:T(8,128)(2,1)}, u32[]{:S(2)}, u32[]{:S(2)}) %collective-permute-start.58) | collective-permute-done | bytes 524320 | tf_op jit(solution)/shard_map/ppermute | solution.py:297
  235.0 3.3 pad_maximum_fusion.2
  238.4 12.9 %collective-permute-done.62 = bf16[384,1024]{1,0:T(8,128)(2,1)} collective-permute-done((bf16[384,1024]{1,0:T(8,128)(2,1)}, bf16[384,1024]{1,0:T(8,128)(2,1)}, u32[]{:S(2)}, u32[]{:S(2)}) %collective-permute-start.62) | collective-permute-done | bytes 786464 | tf_op jit(solution)/shard_map/ppermute | solution.py:266
  264.5 2.0 assemble.7
  269.0 2.4 multiply_convert_fusion
  271.4 3.5 fusion.6
  279.6 2.4 multiply_convert_fusion.1
  284.6 3.9 fusion.13
  291.7 3.4 fusion.51
  297.0 2.0 add_convert_fusion
  300.9 2.0 add_convert_fusion.1
  302.9 2.4 pad_maximum_fusion
  305.3 2.4 slice.1484
  307.7 4.0 fusion.49
  311.9 2.2 fusion.32
  321.3 2.2 collective-permute-done.76
  327.0 4.3 collective-permute-done.69.refs_2_
  331.9 2.4 collective-permute-done.70.refs_3_
  336.0 31.6 %attend_back.1 = bf16[1536,768]{1,0:T(8,128)(2,1)S(1)} custom-call(bf16[384,256]{1,0:T(8,128)(2,1)S(1)} %get-tuple-element.205.refs_0_, bf16[384,256]{1,0:T(8,128)(2,1)S(1)} %collective-permute-done.68.refs_1_, bf16[384,256]{1,0:T(8,128)(2,1)S(1)} %collective-permute-done.69.refs_2_, bf16[384,256]{1,0:T(8,128)(2,1)S(1)} %collective-permute-done.70.refs_3_, ...), custom_call_target="tpu_custom_call" | custom-call | flops 12079595520 | bytes 12582912 | tf_op jit(solution)/shard_map/attend_back/pallas_call | solution.py:233
  369.2 2.6 fusion.116
  372.5 15.1 %collective-permute-done.77 = bf16[384,1024]{1,0:T(8,128)(2,1)S(1)} collective-permute-done((bf16[384,1024]{1,0:T(8,128)(2,1)S(1)}, bf16[384,1024]{1,0:T(8,128)(2,1)S(1)}, u32[]{:S(2)}, u32[]{:S(2)}) %collective-permute-start.77) | collective-permute-done | bytes 786464 | tf_op jit(solution)/shard_map/ppermute | solution.py:266
  388.1 2.8 convolution_convert_fusion
  407.1 3.3 collective-permute-done.82
  422.4 2.2 convolution_add_fusion.1
  425.0 2.2 fusion.26
  429.9 7.5 %collective-permute-done.91.refs_6_ = bf16[128,1792]{1,0:T(8,128)(2,1)S(1)} collective-permute-done((bf16[128,1792]{1,0:T(8,128)(2,1)S(1)}, bf16[128,1792]{1,0:T(8,128)(2,1)S(1)}, u32[]{:S(2)}, u32[]{:S(2)}) %collective-permute-start.91) | collective-permute-done | bytes 458784 | tf_op jit(solution)/shard_map/ppermute | solution.py:297
  437.4 2.4 collective-permute-done.92.refs_7_
  442.8 6.5 %collective-permute-done.88 = bf16[384,768]{1,0:T(8,128)(2,1)S(1)} collective-permute-done((bf16[384,768]{1,0:T(8,128)(2,1)S(1)}, bf16[384,768]{1,0:T(8,128)(2,1)S(1)}, u32[]{:S(2)}, u32[]{:S(2)}) %collective-permute-start.88) | collective-permute-done | bytes 589856 | tf_op jit(solution)/shard_map/ppermute | solution.py:266
  449.4 2.1 fusion.125
  452.5 2.2 fusion.75
  454.7 2.4 add_convert_fusion.2
  457.8 2.0 collective-permute-start.94
  462.6 2.2 collective-permute-done.93.refs_4_
  467.6 7.0 %collective-permute-done.99.refs_6_ = bf16[128,1792]{1,0:T(8,128)(2,1)S(1)} collective-permute-done((bf16[128,1792]{1,0:T(8,128)(2,1)S(1)}, bf16[128,1792]{1,0:T(8,128)(2,1)S(1)}, u32[]{:S(2)}, u32[]{:S(2)}) %collective-permute-start.99) | collective-permute-done | bytes 458784 | tf_op jit(solution)/shard_map/ppermute | solution.py:297
  475.3 5.4 %collective-permute-done.95.refs_4_ = bf16[128,1280]{1,0:T(8,128)(2,1)S(1)} collective-permute-done((bf16[128,1280]{1,0:T(8,128)(2,1)S(1)}, bf16[128,1280]{1,0:T(8,128)(2,1)S(1)}, u32[]{:S(2)}, u32[]{:S(2)}) %collective-permute-start.95) | collective-permute-done | bytes 327712 | tf_op jit(solution)/shard_map/ppermute | solution.py:297
  483.6 6.9 %collective-permute-done.101.refs_4_ = bf16[128,1280]{1,0:T(8,128)(2,1)S(1)} collective-permute-done((bf16[128,1280]{1,0:T(8,128)(2,1)S(1)}, bf16[128,1280]{1,0:T(8,128)(2,1)S(1)}, u32[]{:S(2)}, u32[]{:S(2)}) %collective-permute-start.101) | collective-permute-done | bytes 327712 | tf_op jit(solution)/shard_map/ppermute | solution.py:297
  493.7 3.3 fusion.23
  497.0 2.6 collective-permute-done.103.refs_4_
  502.6 2.1 slice_bitcast_fusion
  510.4 4.4 collective-permute-done.109
  514.8 2.2 collective-permute-done.108
  (638 shorter events, 195.8 us)
Async XLA Ops:
  7.2 499.0 %reduce-scatter.2.cloned.1.call-start = ((), (), s32[]{:S(2)}) async-start(), calls=%async_computation.1 | async-start | bytes 4718592 | tf_op jit(solution)/shard_map/reduce_scatter | solution.py:734
  24.0 11.1 %collective-permute-start.1 = (bf16[32,3840]{1,0:T(8,128)(2,1)S(1)}, bf16[32,3840]{1,0:T(8,128)(2,1)S(1)}, u32[]{:S(2)}, u32[]{:S(2)}) collective-permute-start(bf16[32,3840]{1,0:T(8,128)(2,1)S(1)} %broadcast_select_fusion.37), channel_id=1, source_target_pairs={{0,3},{1,2},{2,1},{3,0},{4,7},{5,6},{6,5},{7,4},{8,11},{9,10},{10,... | collective-permute-start | bytes 737288 | tf_op jit(solution)/shard_map/ppermute | solution.py:266
  25.3 14.0 %collective-permute-start.4 = (bf16[256,1024]{1,0:T(8,128)(2,1)S(1)}, bf16[256,1024]{1,0:T(8,128)(2,1)S(1)}, u32[]{:S(2)}, u32[]{:S(2)}) collective-permute-start(bf16[256,1024]{1,0:T(8,128)(2,1)S(1)} %pad_maximum_fusion.28.refs_0_.refs_1_), channel_id=1, source_target_pairs={{0,8},{8,16},{16,24},{24,28},{28,20},{20,12},{12,4},{4,0},{1,9},{9... | collective-permute-start | bytes 1572872 | tf_op jit(solution)/shard_map/ppermute | solution.py:297
  27.3 13.6 %collective-permute-start.5 = (bf16[256,1024]{1,0:T(8,128)(2,1)S(1)}, bf16[256,1024]{1,0:T(8,128)(2,1)S(1)}, u32[]{:S(2)}, u32[]{:S(2)}) collective-permute-start(bf16[256,1024]{1,0:T(8,128)(2,1)S(1)} %pad_maximum_fusion.28.refs_0_.refs_1_), channel_id=1, source_target_pairs={{0,4},{8,0},{16,8},{24,16},{28,24},{20,28},{12,20},{4,12},{1,5},{9... | collective-permute-start | bytes 1572872 | tf_op jit(solution)/shard_map/ppermute | solution.py:297
  40.8 12.7 %collective-permute-start.7 = (bf16[256,1024]{1,0:T(8,128)(2,1)S(1)}, bf16[256,1024]{1,0:T(8,128)(2,1)S(1)}, u32[]{:S(2)}, u32[]{:S(2)}) collective-permute-start(bf16[256,1024]{1,0:T(8,128)(2,1)S(1)} %collective-permute-done.4.refs_4_.refs_5_), channel_id=1, source_target_pairs={{0,8},{8,16},{16,24},{24,28},{28,20},{20,12},{12,4},{4,0},{1,9},{9... | collective-permute-start | bytes 1572872 | tf_op jit(solution)/shard_map/ppermute | solution.py:297
  42.4 12.4 %collective-permute-start.8 = (bf16[256,1024]{1,0:T(8,128)(2,1)S(1)}, bf16[256,1024]{1,0:T(8,128)(2,1)S(1)}, u32[]{:S(2)}, u32[]{:S(2)}) collective-permute-start(bf16[256,1024]{1,0:T(8,128)(2,1)S(1)} %collective-permute-done.5.refs_8_.refs_9_), channel_id=1, source_target_pairs={{0,4},{8,0},{16,8},{24,16},{28,24},{20,28},{12,20},{4,12},{1,5},{9... | collective-permute-start | bytes 1572872 | tf_op jit(solution)/shard_map/ppermute | solution.py:297
  42.9 11.9 %collective-permute-start.9 = (bf16[256,1024]{1,0:T(8,128)(2,1)S(1)}, bf16[256,1024]{1,0:T(8,128)(2,1)S(1)}, u32[]{:S(2)}, u32[]{:S(2)}) collective-permute-start(bf16[256,1024]{1,0:T(8,128)(2,1)S(1)} %collective-permute-done.4.refs_4_.refs_5_), channel_id=1, source_target_pairs={{0,1},{1,0},{2,3},{3,2},{4,5},{5,4},{6,7},{7,6},{8,9},{9,8},{10,11... | collective-permute-start | bytes 1572872 | tf_op jit(solution)/shard_map/ppermute | solution.py:266
  42.9 12.8 %collective-permute-start.10 = (bf16[256,1024]{1,0:T(8,128)(2,1)S(1)}, bf16[256,1024]{1,0:T(8,128)(2,1)S(1)}, u32[]{:S(2)}, u32[]{:S(2)}) collective-permute-start(bf16[256,1024]{1,0:T(8,128)(2,1)S(1)} %collective-permute-done.5.refs_8_.refs_9_), channel_id=1, source_target_pairs={{0,1},{1,0},{2,3},{3,2},{4,5},{5,4},{6,7},{7,6},{8,9},{9,8},{10,11... | collective-permute-start | bytes 1572872 | tf_op jit(solution)/shard_map/ppermute | solution.py:266
  47.6 19.7 %collective-permute-start.24 = (bf16[384,1024]{1,0:T(8,128)(2,1)}, bf16[384,1024]{1,0:T(8,128)(2,1)S(1)}, u32[]{:S(2)}, u32[]{:S(2)}) collective-permute-start(bf16[384,1024]{1,0:T(8,128)(2,1)} %fusion.19), channel_id=1, source_target_pairs={{0,2},{1,3},{2,0},{3,1},{4,6},{5,7},{6,4},{7,5},{8,10},{9,11},{10,... | collective-permute-start | bytes 2359304 | tf_op jit(solution)/shard_map/ppermute | solution.py:266
  55.6 11.7 %collective-permute-start.11 = (bf16[256,1024]{1,0:T(8,128)(2,1)S(1)}, bf16[256,1024]{1,0:T(8,128)(2,1)S(1)}, u32[]{:S(2)}, u32[]{:S(2)}) collective-permute-start(bf16[256,1024]{1,0:T(8,128)(2,1)S(1)} %collective-permute-done.7.refs_12_.refs_13_), channel_id=1, source_target_pairs={{0,8},{8,16},{16,24},{24,28},{28,20},{20,12},{12,4},{4,0},{1,9},{9... | collective-permute-start | bytes 1572872 | tf_op jit(solution)/shard_map/ppermute | solution.py:297
  57.2 11.2 %collective-permute-start.12 = (bf16[256,1024]{1,0:T(8,128)(2,1)S(1)}, bf16[256,1024]{1,0:T(8,128)(2,1)S(1)}, u32[]{:S(2)}, u32[]{:S(2)}) collective-permute-start(bf16[256,1024]{1,0:T(8,128)(2,1)S(1)} %collective-permute-done.8.refs_16_.refs_17_), channel_id=1, source_target_pairs={{0,4},{8,0},{16,8},{24,16},{28,24},{20,28},{12,20},{4,12},{1,5},{9... | collective-permute-start | bytes 1572872 | tf_op jit(solution)/shard_map/ppermute | solution.py:297
  73.6 11.3 %collective-permute-start.15 = (bf16[128,1280]{1,0:T(8,128)(2,1)}, bf16[128,1280]{1,0:T(8,128)(2,1)}, u32[]{:S(2)}, u32[]{:S(2)}) collective-permute-start(bf16[128,1280]{1,0:T(8,128)(2,1)} %slice.987.refs_0_), channel_id=1, source_target_pairs={{0,4},{8,0},{16,8},{24,16},{28,24},{20,28},{12,20},{4,12},{1,5},{9... | collective-permute-start | bytes 983048 | tf_op jit(solution)/shard_map/ppermute | solution.py:297
  74.7 14.1 %collective-permute-start.19 = (bf16[256,1024]{1,0:T(8,128)(2,1)S(1)}, bf16[256,1024]{1,0:T(8,128)(2,1)}, u32[]{:S(2)}, u32[]{:S(2)}) collective-permute-start(bf16[256,1024]{1,0:T(8,128)(2,1)S(1)} %collective-permute-done.11.refs_20_.refs_21_), channel_id=1, source_target_pairs={{0,1},{1,0},{2,3},{3,2},{4,5},{5,4},{6,7},{7,6},{8,9},{9,8},{10,11... | collective-permute-start | bytes 1572872 | tf_op jit(solution)/shard_map/ppermute | solution.py:266
  78.8 11.6 %collective-permute-start.20 = (bf16[256,1024]{1,0:T(8,128)(2,1)S(1)}, bf16[256,1024]{1,0:T(8,128)(2,1)}, u32[]{:S(2)}, u32[]{:S(2)}) collective-permute-start(bf16[256,1024]{1,0:T(8,128)(2,1)S(1)} %collective-permute-done.12.refs_24_.refs_25_), channel_id=1, source_target_pairs={{0,1},{1,0},{2,3},{3,2},{4,5},{5,4},{6,7},{7,6},{8,9},{9,8},{10,11... | collective-permute-start | bytes 1572872 | tf_op jit(solution)/shard_map/ppermute | solution.py:266
  82.9 18.1 %collective-permute-start.14 = (bf16[128,1280]{1,0:T(8,128)(2,1)}, bf16[128,1280]{1,0:T(8,128)(2,1)S(1)}, u32[]{:S(2)}, u32[]{:S(2)}) collective-permute-start(bf16[128,1280]{1,0:T(8,128)(2,1)} %collective-permute-done.13.refs_1_), channel_id=1, source_target_pairs={{0,8},{8,16},{16,24},{24,28},{28,20},{20,12},{12,4},{4,0},{1,9},{9... | collective-permute-start | bytes 983048 | tf_op jit(solution)/shard_map/ppermute | solution.py:297
  84.9 16.1 %collective-permute-start.16 = (bf16[128,1280]{1,0:T(8,128)(2,1)}, bf16[128,1280]{1,0:T(8,128)(2,1)S(1)}, u32[]{:S(2)}, u32[]{:S(2)}) collective-permute-start(bf16[128,1280]{1,0:T(8,128)(2,1)} %collective-permute-done.15.refs_2_), channel_id=1, source_target_pairs={{0,4},{8,0},{16,8},{24,16},{28,24},{20,28},{12,20},{4,12},{1,5},{9... | collective-permute-start | bytes 983048 | tf_op jit(solution)/shard_map/ppermute | solution.py:297
  87.2 24.2 %collective-permute-start.29 = (bf16[384,1024]{1,0:T(8,128)(2,1)}, bf16[384,1024]{1,0:T(8,128)(2,1)S(1)}, u32[]{:S(2)}, u32[]{:S(2)}) collective-permute-start(bf16[384,1024]{1,0:T(8,128)(2,1)} %bitcast.136), channel_id=1, source_target_pairs={{0,2},{1,3},{2,0},{3,1},{4,6},{5,7},{6,4},{7,5},{8,10},{9,11},{10,... | collective-permute-start | bytes 2359304 | tf_op jit(solution)/shard_map/ppermute | solution.py:266
  88.8 20.2 %collective-permute-start.37 = (bf16[128,1536]{1,0:T(8,128)(2,1)S(1)}, bf16[128,1536]{1,0:T(8,128)(2,1)S(1)}, u32[]{:S(2)}, u32[]{:S(2)}) collective-permute-start(bf16[128,1536]{1,0:T(8,128)(2,1)S(1)} %slice.988.refs_0_), channel_id=1, source_target_pairs={{0,8},{8,16},{16,24},{24,28},{28,20},{20,12},{12,4},{4,0},{1,9},{9... | collective-permute-start | bytes 1179656 | tf_op jit(solution)/shard_map/ppermute | solution.py:297
  90.3 20.2 %collective-permute-start.38 = (bf16[128,1536]{1,0:T(8,128)(2,1)S(1)}, bf16[128,1536]{1,0:T(8,128)(2,1)S(1)}, u32[]{:S(2)}, u32[]{:S(2)}) collective-permute-start(bf16[128,1536]{1,0:T(8,128)(2,1)S(1)} %slice.988.refs_0_), channel_id=1, source_target_pairs={{0,4},{8,0},{16,8},{24,16},{28,24},{20,28},{12,20},{4,12},{1,5},{9... | collective-permute-start | bytes 1179656 | tf_op jit(solution)/shard_map/ppermute | solution.py:297
  108.9 16.7 %collective-permute-start.39 = (bf16[128,1536]{1,0:T(8,128)(2,1)S(1)}, bf16[128,1536]{1,0:T(8,128)(2,1)S(1)}, u32[]{:S(2)}, u32[]{:S(2)}) collective-permute-start(bf16[128,1536]{1,0:T(8,128)(2,1)S(1)} %collective-permute-done.37.refs_1_), channel_id=1, source_target_pairs={{0,8},{8,16},{16,24},{24,28},{28,20},{20,12},{12,4},{4,0},{1,9},{9... | collective-permute-start | bytes 1179656 | tf_op jit(solution)/shard_map/ppermute | solution.py:297
  110.6 16.7 %collective-permute-start.40 = (bf16[128,1536]{1,0:T(8,128)(2,1)S(1)}, bf16[128,1536]{1,0:T(8,128)(2,1)S(1)}, u32[]{:S(2)}, u32[]{:S(2)}) collective-permute-start(bf16[128,1536]{1,0:T(8,128)(2,1)S(1)} %collective-permute-done.38.refs_2_), channel_id=1, source_target_pairs={{0,4},{8,0},{16,8},{24,16},{28,24},{20,28},{12,20},{4,12},{1,5},{9... | collective-permute-start | bytes 1179656 | tf_op jit(solution)/shard_map/ppermute | solution.py:297
  147.5 47.6 %collective-permute-start.45 = (bf16[1024,1536]{1,0:T(8,128)(2,1)S(1)}, bf16[1024,1536]{1,0:T(8,128)(2,1)S(1)}, u32[]{:S(2)}, u32[]{:S(2)}) collective-permute-start(bf16[1024,1536]{1,0:T(8,128)(2,1)S(1)} %assemble.6), channel_id=1, source_target_pairs={{0,1},{1,0},{2,3},{3,2},{4,5},{5,4},{6,7},{7,6},{8,9},{9,8},{10,11... | collective-permute-start | bytes 9437192 | tf_op jit(solution)/shard_map/ppermute | solution.py:266
  147.5 20.0 %collective-permute-start.35 = (bf16[384,1024]{1,0:T(8,128)(2,1)S(1)}, bf16[384,1024]{1,0:T(8,128)(2,1)S(1)}, u32[]{:S(2)}, u32[]{:S(2)}) collective-permute-start(bf16[384,1024]{1,0:T(8,128)(2,1)S(1)} %fusion.36), channel_id=1, source_target_pairs={{0,2},{1,3},{2,0},{3,1},{4,6},{5,7},{6,4},{7,5},{8,10},{9,11},{10,... | collective-permute-start | bytes 2359304 | tf_op jit(solution)/shard_map/ppermute | solution.py:266
  148.1 21.1 %collective-permute-start.34 = (bf16[384,1024]{1,0:T(8,128)(2,1)S(1)}, bf16[384,1024]{1,0:T(8,128)(2,1)S(1)}, u32[]{:S(2)}, u32[]{:S(2)}) collective-permute-start(bf16[384,1024]{1,0:T(8,128)(2,1)S(1)} %fusion.36), channel_id=1, source_target_pairs={{0,1},{1,0},{2,3},{3,2},{4,5},{5,4},{6,7},{7,6},{8,9},{9,8},{10,11... | collective-permute-start | bytes 2359304 | tf_op jit(solution)/shard_map/ppermute | solution.py:266
  167.5 27.6 %collective-permute-start.48 = (bf16[384,1024]{1,0:T(8,128)(2,1)S(1)}, bf16[384,1024]{1,0:T(8,128)(2,1)S(1)}, u32[]{:S(2)}, u32[]{:S(2)}) collective-permute-start(bf16[384,1024]{1,0:T(8,128)(2,1)S(1)} %bitcast.141), channel_id=1, source_target_pairs={{0,2},{1,3},{2,0},{3,1},{4,6},{5,7},{6,4},{7,5},{8,10},{9,11},{10,... | collective-permute-start | bytes 2359304 | tf_op jit(solution)/shard_map/ppermute | solution.py:266
  168.2 49.9 %collective-permute-start.54 = (bf16[1024,512]{1,0:T(8,128)(2,1)S(1)}, bf16[1024,512]{1,0:T(8,128)(2,1)S(1)}, u32[]{:S(2)}, u32[]{:S(2)}) collective-permute-start(bf16[1024,512]{1,0:T(8,128)(2,1)S(1)} %slice.990), channel_id=1, source_target_pairs={{0,1},{1,0},{2,3},{3,2},{4,5},{5,4},{6,7},{7,6},{8,9},{9,8},{10,11... | collective-permute-start | bytes 3145736 | tf_op jit(solution)/shard_map/ppermute | solution.py:266
  169.2 25.8 %collective-permute-start.46 = (bf16[128,2048]{1,0:T(8,128)(2,1)S(1)}, bf16[128,2048]{1,0:T(8,128)(2,1)S(1)}, u32[]{:S(2)}, u32[]{:S(2)}) collective-permute-start(bf16[128,2048]{1,0:T(8,128)(2,1)S(1)} %fusion.79.refs_0_), channel_id=1, source_target_pairs={{0,8},{8,16},{16,24},{24,28},{28,20},{20,12},{12,4},{4,0},{1,9},{9... | collective-permute-start | bytes 1572872 | tf_op jit(solution)/shard_map/ppermute | solution.py:297
  171.7 23.3 %collective-permute-start.47 = (bf16[128,2048]{1,0:T(8,128)(2,1)S(1)}, bf16[128,2048]{1,0:T(8,128)(2,1)S(1)}, u32[]{:S(2)}, u32[]{:S(2)}) collective-permute-start(bf16[128,2048]{1,0:T(8,128)(2,1)S(1)} %fusion.79.refs_0_), channel_id=1, source_target_pairs={{0,4},{8,0},{16,8},{24,16},{28,24},{20,28},{12,20},{4,12},{1,5},{9... | collective-permute-start | bytes 1572872 | tf_op jit(solution)/shard_map/ppermute | solution.py:297
  203.0 14.1 %collective-permute-start.52 = (bf16[128,2048]{1,0:T(8,128)(2,1)S(1)}, bf16[128,2048]{1,0:T(8,128)(2,1)S(1)}, u32[]{:S(2)}, u32[]{:S(2)}) collective-permute-start(bf16[128,2048]{1,0:T(8,128)(2,1)S(1)} %collective-permute-done.46.refs_1_), channel_id=1, source_target_pairs={{0,8},{8,16},{16,24},{24,28},{28,20},{20,12},{12,4},{4,0},{1,9},{9... | collective-permute-start | bytes 1572872 | tf_op jit(solution)/shard_map/ppermute | solution.py:297
  204.4 13.7 %collective-permute-start.53 = (bf16[128,2048]{1,0:T(8,128)(2,1)S(1)}, bf16[128,2048]{1,0:T(8,128)(2,1)S(1)}, u32[]{:S(2)}, u32[]{:S(2)}) collective-permute-start(bf16[128,2048]{1,0:T(8,128)(2,1)S(1)} %collective-permute-done.47.refs_2_), channel_id=1, source_target_pairs={{0,4},{8,0},{16,8},{24,16},{28,24},{20,28},{12,20},{4,12},{1,5},{9... | collective-permute-start | bytes 1572872 | tf_op jit(solution)/shard_map/ppermute | solution.py:297
  206.3 32.1 %collective-permute-start.56 = (bf16[384,1024]{1,0:T(8,128)(2,1)}, bf16[384,1024]{1,0:T(8,128)(2,1)}, u32[]{:S(2)}, u32[]{:S(2)}) collective-permute-start(bf16[384,1024]{1,0:T(8,128)(2,1)} %fusion.24), channel_id=1, source_target_pairs={{0,2},{1,3},{2,0},{3,1},{4,6},{5,7},{6,4},{7,5},{8,10},{9,11},{10,... | collective-permute-start | bytes 2359304 | tf_op jit(solution)/shard_map/ppermute | solution.py:266
  219.6 13.0 %collective-permute-start.58 = (bf16[128,2048]{1,0:T(8,128)(2,1)S(1)}, bf16[128,2048]{1,0:T(8,128)(2,1)}, u32[]{:S(2)}, u32[]{:S(2)}) collective-permute-start(bf16[128,2048]{1,0:T(8,128)(2,1)S(1)} %collective-permute-done.52.refs_3_), channel_id=1, source_target_pairs={{0,8},{8,16},{16,24},{24,28},{28,20},{20,12},{12,4},{4,0},{1,9},{9... | collective-permute-start | bytes 1572872 | tf_op jit(solution)/shard_map/ppermute | solution.py:297
  220.7 12.8 %collective-permute-start.59 = (bf16[128,2048]{1,0:T(8,128)(2,1)S(1)}, bf16[128,2048]{1,0:T(8,128)(2,1)}, u32[]{:S(2)}, u32[]{:S(2)}) collective-permute-start(bf16[128,2048]{1,0:T(8,128)(2,1)S(1)} %collective-permute-done.53.refs_4_), channel_id=1, source_target_pairs={{0,4},{8,0},{16,8},{24,16},{28,24},{20,28},{12,20},{4,12},{1,5},{9... | collective-permute-start | bytes 1572872 | tf_op jit(solution)/shard_map/ppermute | solution.py:297
  233.5 17.7 %collective-permute-start.62 = (bf16[384,1024]{1,0:T(8,128)(2,1)}, bf16[384,1024]{1,0:T(8,128)(2,1)}, u32[]{:S(2)}, u32[]{:S(2)}) collective-permute-start(bf16[384,1024]{1,0:T(8,128)(2,1)} %fusion.34), channel_id=1, source_target_pairs={{0,2},{1,3},{2,0},{3,1},{4,6},{5,7},{6,4},{7,5},{8,10},{9,11},{10,... | collective-permute-start | bytes 2359304 | tf_op jit(solution)/shard_map/ppermute | solution.py:266
  238.4 28.2 %collective-permute-start.57 = (bf16[384,1024]{1,0:T(8,128)(2,1)}, bf16[384,1024]{1,0:T(8,128)(2,1)S(1)}, u32[]{:S(2)}, u32[]{:S(2)}) collective-permute-start(bf16[384,1024]{1,0:T(8,128)(2,1)} %collective-permute-done.56), channel_id=1, source_target_pairs={{0,1},{1,0},{2,3},{3,2},{4,5},{5,4},{6,7},{7,6},{8,9},{9,8},{10,11... | collective-permute-start | bytes 2359304 | tf_op jit(solution)/shard_map/ppermute | solution.py:266
  251.3 17.7 %collective-permute-start.63 = (bf16[384,1024]{1,0:T(8,128)(2,1)}, bf16[384,1024]{1,0:T(8,128)(2,1)S(1)}, u32[]{:S(2)}, u32[]{:S(2)}) collective-permute-start(bf16[384,1024]{1,0:T(8,128)(2,1)} %collective-permute-done.62), channel_id=1, source_target_pairs={{0,1},{1,0},{2,3},{3,2},{4,5},{5,4},{6,7},{7,6},{8,9},{9,8},{10,11... | collective-permute-start | bytes 2359304 | tf_op jit(solution)/shard_map/ppermute | solution.py:266
  253.0 144.2 %collective-permute-start.80 = (bf16[384,3072]{1,0:T(8,128)(2,1)}, bf16[384,3072]{1,0:T(8,128)(2,1)}, u32[]{:S(2)}, u32[]{:S(2)}) collective-permute-start(bf16[384,3072]{1,0:T(8,128)(2,1)} %pad_maximum_fusion.3), channel_id=1, source_target_pairs={{0,1},{1,0},{2,3},{3,2},{4,5},{5,4},{6,7},{7,6},{8,9},{9,8},{10,11... | collective-permute-start | bytes 7077896 | tf_op jit(solution)/shard_map/ppermute | solution.py:266
  262.8 14.1 %collective-permute-start.55 = (bf16[384,1024]{1,0:T(8,128)(2,1)}, bf16[384,1024]{1,0:T(8,128)(2,1)S(1)}, u32[]{:S(2)}, u32[]{:S(2)}) collective-permute-start(bf16[384,1024]{1,0:T(8,128)(2,1)} %fusion.24), channel_id=1, source_target_pairs={{0,1},{1,0},{2,3},{3,2},{4,5},{5,4},{6,7},{7,6},{8,9},{9,8},{10,11... | collective-permute-start | bytes 2359304 | tf_op jit(solution)/shard_map/ppermute | solution.py:266
  264.5 130.8 %collective-permute-start.79 = (bf16[384,3072]{1,0:T(8,128)(2,1)}, bf16[384,3072]{1,0:T(8,128)(2,1)}, u32[]{:S(2)}, u32[]{:S(2)}) collective-permute-start(bf16[384,3072]{1,0:T(8,128)(2,1)} %pad_maximum_fusion.2), channel_id=1, source_target_pairs={{0,1},{1,0},{2,3},{3,2},{4,5},{5,4},{6,7},{7,6},{8,9},{9,8},{10,11... | collective-permute-start | bytes 7077896 | tf_op jit(solution)/shard_map/ppermute | solution.py:266
  266.6 11.7 %collective-permute-start.65 = (bf16[384,1024]{1,0:T(8,128)(2,1)}, bf16[384,1024]{1,0:T(8,128)(2,1)S(1)}, u32[]{:S(2)}, u32[]{:S(2)}) collective-permute-start(bf16[384,1024]{1,0:T(8,128)(2,1)} %fusion.34), channel_id=1, source_target_pairs={{0,1},{1,0},{2,3},{3,2},{4,5},{5,4},{6,7},{7,6},{8,9},{9,8},{10,11... | collective-permute-start | bytes 2359304 | tf_op jit(solution)/shard_map/ppermute | solution.py:266
  283.1 28.8 %collective-permute-start.67 = (bf16[384,1024]{1,0:T(8,128)(2,1)}, bf16[384,1024]{1,0:T(8,128)(2,1)}, u32[]{:S(2)}, u32[]{:S(2)}) collective-permute-start(bf16[384,1024]{1,0:T(8,128)(2,1)} %fusion.33), channel_id=1, source_target_pairs={{0,2},{1,3},{2,0},{3,1},{4,6},{5,7},{6,4},{7,5},{8,10},{9,11},{10,... | collective-permute-start | bytes 2359304 | tf_op jit(solution)/shard_map/ppermute | solution.py:266
  291.5 20.4 %collective-permute-start.66 = (bf16[384,1024]{1,0:T(8,128)(2,1)}, bf16[384,1024]{1,0:T(8,128)(2,1)}, u32[]{:S(2)}, u32[]{:S(2)}) collective-permute-start(bf16[384,1024]{1,0:T(8,128)(2,1)} %slice.1485), channel_id=1, source_target_pairs={{0,1},{1,0},{2,3},{3,2},{4,5},{5,4},{6,7},{7,6},{8,9},{9,8},{10,11... | collective-permute-start | bytes 2359304 | tf_op jit(solution)/shard_map/ppermute | solution.py:266
  326.4 41.1 %collective-permute-start.71 = (bf16[384,512]{1,0:T(8,128)(2,1)S(1)}, bf16[384,512]{1,0:T(8,128)(2,1)S(1)}, u32[]{:S(2)}, u32[]{:S(2)}) collective-permute-start(bf16[384,512]{1,0:T(8,128)(2,1)S(1)} %get-tuple-element.213), channel_id=1, source_target_pairs={{0,1},{1,0},{2,3},{3,2},{4,5},{5,4},{6,7},{7,6},{8,9},{9,8},{10,11... | collective-permute-start | bytes 1179656 | tf_op jit(solution)/shard_map/ppermute | solution.py:266
  331.3 36.4 %collective-permute-start.72 = (bf16[384,512]{1,0:T(8,128)(2,1)S(1)}, bf16[384,512]{1,0:T(8,128)(2,1)S(1)}, u32[]{:S(2)}, u32[]{:S(2)}) collective-permute-start(bf16[384,512]{1,0:T(8,128)(2,1)S(1)} %get-tuple-element.214), channel_id=1, source_target_pairs={{0,2},{1,3},{2,0},{3,1},{4,6},{5,7},{6,4},{7,5},{8,10},{9,11},{10,... | collective-permute-start | bytes 1179656 | tf_op jit(solution)/shard_map/ppermute | solution.py:266
  334.3 34.9 %collective-permute-start.73 = (bf16[384,512]{1,0:T(8,128)(2,1)S(1)}, bf16[384,512]{1,0:T(8,128)(2,1)S(1)}, u32[]{:S(2)}, u32[]{:S(2)}) collective-permute-start(bf16[384,512]{1,0:T(8,128)(2,1)S(1)} %get-tuple-element.215), channel_id=1, source_target_pairs={{0,3},{1,2},{2,1},{3,0},{4,7},{5,6},{6,5},{7,4},{8,11},{9,10},{10,... | collective-permute-start | bytes 1179656 | tf_op jit(solution)/shard_map/ppermute | solution.py:266
  367.7 19.9 %collective-permute-start.77 = (bf16[384,1024]{1,0:T(8,128)(2,1)S(1)}, bf16[384,1024]{1,0:T(8,128)(2,1)S(1)}, u32[]{:S(2)}, u32[]{:S(2)}) collective-permute-start(bf16[384,1024]{1,0:T(8,128)(2,1)S(1)} %add_convert_fusion.6), channel_id=1, source_target_pairs={{0,2},{1,3},{2,0},{3,1},{4,6},{5,7},{6,4},{7,5},{8,10},{9,11},{10,... | collective-permute-start | bytes 2359304 | tf_op jit(solution)/shard_map/ppermute | solution.py:266
  372.0 18.9 %collective-permute-start.78 = (bf16[384,1024]{1,0:T(8,128)(2,1)S(1)}, bf16[384,1024]{1,0:T(8,128)(2,1)S(1)}, u32[]{:S(2)}, u32[]{:S(2)}) collective-permute-start(bf16[384,1024]{1,0:T(8,128)(2,1)S(1)} %get-tuple-element.287), channel_id=1, source_target_pairs={{0,1},{1,0},{2,3},{3,2},{4,5},{5,4},{6,7},{7,6},{8,9},{9,8},{10,11... | collective-permute-start | bytes 2359304 | tf_op jit(solution)/shard_map/ppermute | solution.py:266
  372.2 34.9 %collective-permute-start.81 = (bf16[384,1024]{1,0:T(8,128)(2,1)S(1)}, bf16[384,1024]{1,0:T(8,128)(2,1)S(1)}, u32[]{:S(2)}, u32[]{:S(2)}) collective-permute-start(bf16[384,1024]{1,0:T(8,128)(2,1)S(1)} %get-tuple-element.286), channel_id=1, source_target_pairs={{0,1},{1,0},{2,3},{3,2},{4,5},{5,4},{6,7},{7,6},{8,9},{9,8},{10,11... | collective-permute-start | bytes 2359304 | tf_op jit(solution)/shard_map/ppermute | solution.py:266
  391.2 19.3 %collective-permute-start.82 = (bf16[384,1024]{1,0:T(8,128)(2,1)S(1)}, bf16[384,1024]{1,0:T(8,128)(2,1)S(1)}, u32[]{:S(2)}, u32[]{:S(2)}) collective-permute-start(bf16[384,1024]{1,0:T(8,128)(2,1)S(1)} %fusion.30), channel_id=1, source_target_pairs={{0,2},{1,3},{2,0},{3,1},{4,6},{5,7},{6,4},{7,5},{8,10},{9,11},{10,... | collective-permute-start | bytes 2359304 | tf_op jit(solution)/shard_map/ppermute | solution.py:266
  401.3 18.1 %collective-permute-start.89 = (bf16[64,1792]{1,0:T(8,128)(2,1)S(1)}, bf16[64,1792]{1,0:T(8,128)(2,1)S(1)}, u32[]{:S(2)}, u32[]{:S(2)}) collective-permute-start(bf16[64,1792]{1,0:T(8,128)(2,1)S(1)} %get-tuple-element.232), channel_id=1, source_target_pairs={{0,8},{8,16},{16,24},{24,28},{28,20},{20,12},{12,4},{4,0},{1,9},{9... | collective-permute-start | bytes 688136 | tf_op jit(solution)/shard_map/ppermute | solution.py:297
  402.0 17.5 %collective-permute-start.90 = (bf16[64,1792]{1,0:T(8,128)(2,1)S(1)}, bf16[64,1792]{1,0:T(8,128)(2,1)S(1)}, u32[]{:S(2)}, u32[]{:S(2)}) collective-permute-start(bf16[64,1792]{1,0:T(8,128)(2,1)S(1)} %get-tuple-element.233), channel_id=1, source_target_pairs={{0,4},{8,0},{16,8},{24,16},{28,24},{20,28},{12,20},{4,12},{1,5},{9... | collective-permute-start | bytes 688136 | tf_op jit(solution)/shard_map/ppermute | solution.py:297
  412.6 12.0 %collective-permute-start.85 = (bf16[384,256]{1,0:T(8,128)(2,1)S(1)}, bf16[384,256]{1,0:T(8,128)(2,1)S(1)}, u32[]{:S(2)}, u32[]{:S(2)}) collective-permute-start(bf16[384,256]{1,0:T(8,128)(2,1)S(1)} %get-tuple-element.321), channel_id=1, source_target_pairs={{0,3},{1,2},{2,1},{3,0},{4,7},{5,6},{6,5},{7,4},{8,11},{9,10},{10,... | collective-permute-start | bytes 589832 | tf_op jit(solution)/shard_map/ppermute | solution.py:266
  414.2 13.0 %collective-permute-start.84 = (bf16[384,256]{1,0:T(8,128)(2,1)S(1)}, bf16[384,256]{1,0:T(8,128)(2,1)S(1)}, u32[]{:S(2)}, u32[]{:S(2)}) collective-permute-start(bf16[384,256]{1,0:T(8,128)(2,1)S(1)} %get-tuple-element.324), channel_id=1, source_target_pairs={{0,2},{1,3},{2,0},{3,1},{4,6},{5,7},{6,4},{7,5},{8,10},{9,11},{10,... | collective-permute-start | bytes 589832 | tf_op jit(solution)/shard_map/ppermute | solution.py:266
  419.4 23.4 %collective-permute-start.86 = (bf16[384,768]{1,0:T(8,128)(2,1)S(1)}, bf16[384,768]{1,0:T(8,128)(2,1)S(1)}, u32[]{:S(2)}, u32[]{:S(2)}) collective-permute-start(bf16[384,768]{1,0:T(8,128)(2,1)S(1)} %broadcast_select_fusion.8), channel_id=1, source_target_pairs={{0,1},{1,0},{2,3},{3,2},{4,5},{5,4},{6,7},{7,6},{8,9},{9,8},{10,11... | collective-permute-start | bytes 1769480 | tf_op jit(solution)/shard_map/ppermute | solution.py:266
  419.5 23.3 %collective-permute-start.87 = (bf16[384,768]{1,0:T(8,128)(2,1)S(1)}, bf16[384,768]{1,0:T(8,128)(2,1)S(1)}, u32[]{:S(2)}, u32[]{:S(2)}) collective-permute-start(bf16[384,768]{1,0:T(8,128)(2,1)S(1)} %broadcast_select_fusion.7), channel_id=1, source_target_pairs={{0,2},{1,3},{2,0},{3,1},{4,6},{5,7},{6,4},{7,5},{8,10},{9,11},{10,... | collective-permute-start | bytes 1769480 | tf_op jit(solution)/shard_map/ppermute | solution.py:266
  422.0 27.4 %collective-permute-start.88 = (bf16[384,768]{1,0:T(8,128)(2,1)S(1)}, bf16[384,768]{1,0:T(8,128)(2,1)S(1)}, u32[]{:S(2)}, u32[]{:S(2)}) collective-permute-start(bf16[384,768]{1,0:T(8,128)(2,1)S(1)} %broadcast_select_fusion.6), channel_id=1, source_target_pairs={{0,3},{1,2},{2,1},{3,0},{4,7},{5,6},{6,5},{7,4},{8,11},{9,10},{10,... | collective-permute-start | bytes 1769480 | tf_op jit(solution)/shard_map/ppermute | solution.py:266
  424.6 12.8 %collective-permute-start.91 = (bf16[128,1792]{1,0:T(8,128)(2,1)S(1)}, bf16[128,1792]{1,0:T(8,128)(2,1)S(1)}, u32[]{:S(2)}, u32[]{:S(2)}) collective-permute-start(bf16[128,1792]{1,0:T(8,128)(2,1)S(1)} %get-tuple-element.239), channel_id=1, source_target_pairs={{0,8},{8,16},{16,24},{24,28},{28,20},{20,12},{12,4},{4,0},{1,9},{9... | collective-permute-start | bytes 1376264 | tf_op jit(solution)/shard_map/ppermute | solution.py:297
  427.2 12.6 %collective-permute-start.92 = (bf16[128,1792]{1,0:T(8,128)(2,1)S(1)}, bf16[128,1792]{1,0:T(8,128)(2,1)S(1)}, u32[]{:S(2)}, u32[]{:S(2)}) collective-permute-start(bf16[128,1792]{1,0:T(8,128)(2,1)S(1)} %get-tuple-element.240), channel_id=1, source_target_pairs={{0,4},{8,0},{16,8},{24,16},{28,24},{20,28},{12,20},{4,12},{1,5},{9... | collective-permute-start | bytes 1376264 | tf_op jit(solution)/shard_map/ppermute | solution.py:297
  440.6 19.1 %collective-permute-start.97 = (bf16[128,1792]{1,0:T(8,128)(2,1)S(1)}, bf16[128,1792]{1,0:T(8,128)(2,1)S(1)}, u32[]{:S(2)}, u32[]{:S(2)}) collective-permute-start(bf16[128,1792]{1,0:T(8,128)(2,1)S(1)} %get-tuple-element.249), channel_id=1, source_target_pairs={{0,8},{8,16},{16,24},{24,28},{28,20},{20,12},{12,4},{4,0},{1,9},{9... | collective-permute-start | bytes 1376264 | tf_op jit(solution)/shard_map/ppermute | solution.py:297
  441.2 18.5 %collective-permute-start.98 = (bf16[128,1792]{1,0:T(8,128)(2,1)S(1)}, bf16[128,1792]{1,0:T(8,128)(2,1)S(1)}, u32[]{:S(2)}, u32[]{:S(2)}) collective-permute-start(bf16[128,1792]{1,0:T(8,128)(2,1)S(1)} %get-tuple-element.250), channel_id=1, source_target_pairs={{0,4},{8,0},{16,8},{24,16},{28,24},{20,28},{12,20},{4,12},{1,5},{9... | collective-permute-start | bytes 1376264 | tf_op jit(solution)/shard_map/ppermute | solution.py:297
  460.5 14.1 %collective-permute-start.99 = (bf16[128,1792]{1,0:T(8,128)(2,1)S(1)}, bf16[128,1792]{1,0:T(8,128)(2,1)S(1)}, u32[]{:S(2)}, u32[]{:S(2)}) collective-permute-start(bf16[128,1792]{1,0:T(8,128)(2,1)S(1)} %get-tuple-element.251), channel_id=1, source_target_pairs={{0,8},{8,16},{16,24},{24,28},{28,20},{20,12},{12,4},{4,0},{1,9},{9... | collective-permute-start | bytes 1376264 | tf_op jit(solution)/shard_map/ppermute | solution.py:297
  460.6 14.0 %collective-permute-start.100 = (bf16[128,1792]{1,0:T(8,128)(2,1)S(1)}, bf16[128,1792]{1,0:T(8,128)(2,1)S(1)}, u32[]{:S(2)}, u32[]{:S(2)}) collective-permute-start(bf16[128,1792]{1,0:T(8,128)(2,1)S(1)} %get-tuple-element.252), channel_id=1, source_target_pairs={{0,4},{8,0},{16,8},{24,16},{28,24},{20,28},{12,20},{4,12},{1,5},{9... | collective-permute-start | bytes 1376264 | tf_op jit(solution)/shard_map/ppermute | solution.py:297
  465.4 15.3 %collective-permute-start.95 = (bf16[128,1280]{1,0:T(8,128)(2,1)S(1)}, bf16[128,1280]{1,0:T(8,128)(2,1)S(1)}, u32[]{:S(2)}, u32[]{:S(2)}) collective-permute-start(bf16[128,1280]{1,0:T(8,128)(2,1)S(1)} %get-tuple-element.247), channel_id=1, source_target_pairs={{0,8},{8,16},{16,24},{24,28},{28,20},{20,12},{12,4},{4,0},{1,9},{9... | collective-permute-start | bytes 983048 | tf_op jit(solution)/shard_map/ppermute | solution.py:297
  466.3 14.6 %collective-permute-start.96 = (bf16[128,1280]{1,0:T(8,128)(2,1)S(1)}, bf16[128,1280]{1,0:T(8,128)(2,1)S(1)}, u32[]{:S(2)}, u32[]{:S(2)}) collective-permute-start(bf16[128,1280]{1,0:T(8,128)(2,1)S(1)} %get-tuple-element.248), channel_id=1, source_target_pairs={{0,4},{8,0},{16,8},{24,16},{28,24},{20,28},{12,20},{4,12},{1,5},{9... | collective-permute-start | bytes 983048 | tf_op jit(solution)/shard_map/ppermute | solution.py:297
  (163 other events, 1448.3 us)
Sparse Core Ops, SparseCore 0:
  307.8 85.5 reduce-scatter.1
